TPU v7x, 256 devices: a whole 4x4x8 slice. The times are simulated.
256 devices in a mesh: row: 8 (over z), col: 16 (over y, x), layer: 2 (over core).
Axes of the slice: x: 4, y: 4, z: 8, core: 2. Of those that a mesh axis runs over, the one named last changes fastest.
Arguments:
- integrals: bfloat16 [8, 4096, 4096], P('layer', 'row', 'col'), may hold values from -6 to 6
- density_occ: bfloat16 [4096, 4096], P('row', 'col'), as said below
- density_virt: bfloat16 [4096, 4096], P('row', 'col'), may hold values from -0.125 to 0.125
- mask_int: int32 [8, 32, 32], P('layer', 'row', 'col'), may hold values 0 or 1
- mask_occ: int32 [32, 32], P('row', 'col'), may hold values from 0 to 1, as said below
- mask_virt: int32 [32, 32], P('row', 'col'), may hold values 0 or 1
Outputs:
- polar_tensor: bfloat16 [8, 4096, 4096], P('layer', 'row', 'col')
- chi_block: float32 [8, 8], P('layer')
Inputs may be any that keep to these rules, and one draw needn't show every extreme that they name: density_occ is symmetric. mask_occ is symmetric with ones on its diagonal.
All inputs are finite; a program needn't handle non-finite values. No bound on the sum of `mask_int` or of `mask_virt` on one device may be relied on, other than what follows from the above.
Results may differ from a plain program's by a relative error of at most 0.0054.
Values may be sent and summed in bfloat16 or wider, within the bound.
No kernel may reach another device: no remote copies, remote signals or barrier semaphores. Data moves between devices by JAX's collectives and lax.ppermute only.
A program may use at most 128 MiB of HBM per device.

v0:
```python
import jax
import jax.numpy as jnp
from jax import lax
from jax.sharding import PartitionSpec as P

BLK = 128


def expand_mask(blocks, block_width):
    extent = blocks.shape
    spread = jnp.broadcast_to(
        blocks[..., :, None, :, None],
        extent[:-2] + (extent[-2], block_width, extent[-1], block_width),
    )
    return spread.reshape(
        extent[:-2] + (extent[-2] * block_width, extent[-1] * block_width)
    ).astype(jnp.bfloat16)


def body(integrals, density_occ, density_virt, mask_int, mask_occ, mask_virt):
    masked_int = integrals * expand_mask(mask_int, BLK)
    occupied = density_occ * expand_mask(mask_occ, BLK)
    virtual = density_virt * expand_mask(mask_virt, BLK)
    aux_rows, tile_rows, tile_cols = integrals.shape
    basis_count = tile_rows * lax.axis_size("row")
    aux_count = aux_rows * lax.axis_size("layer")
    virt_cols = lax.all_gather(virtual, "row", axis=0, tiled=True)
    half_tensor = jnp.einsum(
        "pam,mb->pab",
        lax.all_gather(masked_int, "col", axis=2, tiled=True),
        virt_cols,
        preferred_element_type=jnp.float32,
    ).astype(jnp.bfloat16)
    occ_rows = lax.all_gather(occupied, "col", axis=1, tiled=True)
    polar_sum = jnp.einsum(
        "al,plb->pab",
        occ_rows,
        lax.all_gather(half_tensor, "row", axis=1, tiled=True),
        preferred_element_type=jnp.float32,
    )
    polar_tensor = polar_sum.astype(jnp.bfloat16)
    flat_polar = polar_tensor.reshape(aux_rows, tile_rows * tile_cols)
    every_aux = lax.all_gather(masked_int, "layer", axis=0, tiled=True)
    flat_every = every_aux.reshape(aux_count, tile_rows * tile_cols)
    partial_value = lax.dot_general(
        flat_polar, flat_every, (((1,), (1,)), ((), ())), preferred_element_type=jnp.float32
    )
    chi_block = lax.psum(partial_value, ("row", "col")) * (1.0 / basis_count)
    return (polar_tensor, chi_block)


def solution(mesh):
    in_specs = (
        P("layer", "row", "col"),
        P("row", "col"),
        P("row", "col"),
        P("layer", "row", "col"),
        P("row", "col"),
        P("row", "col"),
    )
    out_specs = (P("layer", "row", "col"), P("layer", None))
    return jax.shard_map(body, mesh=mesh, in_specs=in_specs, out_specs=out_specs, check_vma=False)
```

profile of v0, /device:TPU:2, one launch (start us, length us, event | category | flops | bytes accessed | tf_op | source)
XLA Modules:
  0.0 712.5 jit_solution(333330736755740064)
XLA Ops:
  7.2 0.8 convert_element_type.32
  8.1 0.2 broadcast_in_dim.7
  8.3 1.7 bitcast_multiply_fusion.1
  10.1 0.7 convert_element_type.30
  10.8 0.1 copy.14
  11.0 0.6 broadcast_in_dim.6
  11.6 0.7 convert_element_type.31
  12.3 1.2 mul.15
  13.8 0.2 broadcast_in_dim.8
  14.0 0.7 bitcast_multiply_fusion
  14.8 39.7 %all-gather.8.cloned.1.call-done = bf16[4096,256]{1,0:T(8,128)(2,1)} async-done(((bf16[512,256]{1,0:T(8,128)(2,1)}), bf16[4096,256]{1,0:T(8,128)(2,1)}) %all-gather.8.cloned.1.call-update) | async-done | bytes 2097168 | tf_op jit(solution)/shard_map/all_gather | solution.py:27
  54.5 126.7 %all-gather.6.cloned.1.call-done = bf16[4,512,4096]{2,1,0:T(8,128)(2,1)} async-done(((bf16[4,512,256]{2,1,0:T(8,128)(2,1)}), bf16[4,512,4096]{2,1,0:T(8,128)(2,1)}) %all-gather.6.cloned.1.call-update) | async-done | bytes 16777232 | tf_op jit(solution)/shard_map/all_gather | solution.py:30
  181.2 11.9 %fusion.6 = bf16[4,512,256]{1,2,0:T(8,128)(2,1)} fusion(bf16[4,512,4096]{2,1,0:T(8,128)(2,1)} %all-gather.6.cloned.1.call-done, bf16[4096,256]{1,0:T(8,128)(2,1)} %all-gather.8.cloned.1.call-done), kind=kOutput, calls=%fused_computation.6 | convolution fusion | flops 4295491584 | bytes 19922944 | tf_op jit(solution)/shard_map/pam,mb->pab/dot_general | solution.py:28
  193.1 0.2 all-gather.14.cloned.1.call-start
  193.3 0.4 all-gather.14.cloned.1.call-update
  193.7 52.0 %all-gather.12.cloned.1.call-done = bf16[512,4096]{1,0:T(8,128)(2,1)} async-done(((bf16[512,256]{1,0:T(8,128)(2,1)}), bf16[512,4096]{1,0:T(8,128)(2,1)}) %all-gather.12.cloned.1.call-update) | async-done | bytes 4194320 | tf_op jit(solution)/shard_map/all_gather | solution.py:34
  245.6 96.1 %all-gather.10.cloned.1.call-done = bf16[4,4096,256]{1,2,0:T(8,128)(2,1)} async-done(((bf16[4,512,256]{1,2,0:T(8,128)(2,1)}), bf16[4,4096,256]{1,2,0:T(8,128)(2,1)}) %all-gather.10.cloned.1.call-update) | async-done | bytes 8388624 | tf_op jit(solution)/shard_map/all_gather | solution.py:38
  341.8 9.1 %fusion.12 = bf16[4,512,256]{1,2,0:T(8,128)(2,1)S(1)} fusion(bf16[4,4096,256]{1,2,0:T(8,128)(2,1)} %all-gather.10.cloned.1.call-done, bf16[512,4096]{1,0:T(8,128)(2,1)} %all-gather.12.cloned.1.call-done), kind=kOutput, calls=%fused_computation.8 | convolution fusion | flops 4295491584 | bytes 13631488 | tf_op jit(solution)/shard_map/al,plb->pab/dot_general | solution.py:35
  350.8 0.7 copy.17
  351.6 1.3 copy.19
  352.9 5.1 all-gather.14.cloned.1.call-done
  358.0 3.6 fusion.15
  361.6 343.7 %psum.7 = f32[4,8]{1,0:T(4,128)S(1)} all-reduce(f32[4,8]{1,0:T(4,128)S(1)} %fusion.15), channel_id=1, replica_groups=mesh['row'=8,'col'=16,'layer'=2] {'row','col'}, use_global_device_ids=true, to_apply=%region_0.0 | all-reduce | flops 32 | bytes 256 | tf_op jit(solution)/shard_map/psum | solution.py:48
  705.3 0.6 broadcast_multiply_fusion
  (17 shorter events, 0.5 us)
Async XLA Ops:
  7.2 5.1 copy-start
  7.2 47.3 %all-gather.8.cloned.1.call-start = ((), (), s32[]{:S(2)}) async-start(), calls=%async_computation.1 | async-start | bytes 2359296 | tf_op jit(solution)/shard_map/all_gather | solution.py:27
  8.3 5.3 copy-start.2
  8.3 5.7 copy-start.1
  10.1 171.1 %all-gather.6.cloned.1.call-start = ((), (), s32[]{:S(2)}) async-start(), calls=%async_computation | async-start | bytes 17825792 | tf_op jit(solution)/shard_map/all_gather | solution.py:30
  13.6 232.1 %all-gather.12.cloned.1.call-start = ((), (), s32[]{:S(2)}) async-start(), calls=%async_computation.3 | async-start | bytes 4456448 | tf_op jit(solution)/shard_map/all_gather | solution.py:34
  14.7 327.0 %all-gather.10.cloned.1.call-start = ((), (), s32[]{:S(2)}) async-start(), calls=%async_computation.2 | async-start | bytes 9437184 | tf_op jit(solution)/shard_map/all_gather | solution.py:38
  193.1 164.9 %all-gather.14.cloned.1.call-start = ((), (), s32[]{:S(2)}) async-start(), calls=%async_computation.4 | async-start | bytes 3145728 | tf_op jit(solution)/shard_map/all_gather | solution.py:43
Sparse Core Ops, SparseCore 0:
  10.4 44.0 all-gather.7
  56.9 124.2 all-gather.5
  183.6 62.0 all-gather.11
  247.9 93.8 all-gather.9
  343.4 14.5 all-gather.13
where the time goes:
time: 717 us; the launch traced here: 712 us
  blocking collectives  344 us (48%)
  waiting for transfers between devices  320 us (45%)
  matrix products  24.6 us (3%)
  between operations  13.9 us (2%)
    psum x1, blocking collectives, body(): chi_block = lax.psum(partial_value, ('row', 'col')) * (1.0 / basis_count)  344 us
    all_gather x1, waiting for transfers between devices, body(): lax.all_gather(masked_int, 'col', axis=2, tiled=True)  127 us
    all_gather x1, waiting for transfers between devices, body(): lax.all_gather(half_tensor, 'row', axis=1, tiled=True)  96.1 us
    all_gather x1, waiting for transfers between devices, body(): occ_rows = lax.all_gather(occupied, 'col', axis=1, tiled=True)  52 us
    all_gather x1, waiting for transfers between devices, body(): virt_cols = lax.all_gather(virtual, 'row', axis=0, tiled=True)  39.7 us
  transfers between devices with their start and end apart: 5, of which 5 were waited for; matrix products, arithmetic and copies ran while one was open for 4% of the time, Pallas kernels for 0%

commit v1 on v0

v1 whole, which is shorter than its diff:
```python
import functools

import jax
import jax.numpy as jnp
from jax import lax
from jax.experimental import pallas as pl
from jax.experimental.pallas import tpu as pltpu
from jax.sharding import PartitionSpec as P

BLK = 128
ROWS = 512
COLS = 256
HALF = 256
PAIR = 2
F32 = jnp.float32
BF16 = jnp.bfloat16
VMEM = pl.BlockSpec(memory_space=pltpu.VMEM)
SMEM = pl.BlockSpec(memory_space=pltpu.SMEM)
PARAMS = pltpu.CompilerParams(vmem_limit_bytes=48 * 1024 * 1024)


def plane_index(y, x, core):
    return ((y % 4) * 4 + x % 4) * 2 + core


def plane_perm(shift, first):
    pairs = []
    for y in range(4):
        for x in range(4):
            for core in range(2):
                along_x = (core == 0) == first
                to = (y, x + shift) if along_x else (y + shift, x)
                pairs.append((plane_index(y, x, core), plane_index(*to, core)))
    return pairs


def plane_move(value, shift, first):
    return lax.ppermute(value, ("col", "layer"), plane_perm(shift, first))


def ring_move(value, shift):
    return lax.ppermute(value, "row", [(i, (i + shift) % 8) for i in range(8)])


def swap_cores(value):
    return lax.ppermute(value, "layer", [(0, 1), (1, 0)])


def gather_plane(value):
    before = plane_move(value, 1, True)
    after = plane_move(value, -1, True)
    across = plane_move(value, 2, True)
    near = jnp.concatenate([value, before, after, across], axis=0)
    half = near.shape[0] // 2
    second_before = plane_move(near, 1, False)
    second_after = plane_move(near, -1, False)
    top = plane_move(second_before[:half], 1, False)
    bottom = plane_move(second_after[half:], -1, False)
    return near, second_before, second_after, top, bottom


NEAR = ((0, 0), (-1, 0), (1, 0), (2, 0))
BEFORE = ((0, -1), (-1, -1), (1, -1), (2, -1))
AFTER = ((0, 1), (-1, 1), (1, 1), (2, 1))
TOP = ((0, 2), (-1, 2))
BOTTOM = ((1, 2), (2, 2))

RING = (0, -1, 1, -2, 2, -3, 3, 4, 4)


def gather_ring(value):
    half = value.shape[0] // 2
    up1, down1 = ring_move(value, 1), ring_move(value, -1)
    up2, down2 = ring_move(up1, 1), ring_move(down1, -1)
    up3, down3 = ring_move(up2, 1), ring_move(down2, -1)
    up4, down4 = ring_move(up3[:half], 1), ring_move(down3[half:], -1)
    return value, up1, down1, up2, down2, up3, down3, up4, down4


def mask_kernel(pos, mask_int, mask_occ, mask_virt, integrals, occ, virt, plane, ring, occ_half):
    def masked(ref, index, row, col, weight):
        block = ref[index + (pl.ds(row, BLK), pl.ds(col, BLK))]
        return (block.astype(F32) * weight.astype(F32)).astype(BF16)

    core = pos[3]
    for p in range(2 * PAIR):
        for i in range(ROWS // BLK):
            for j in range(COLS // BLK):
                block = masked(integrals, (p,), i * BLK, j * BLK, mask_int[p, i, j])
                cols = pl.ds(j * BLK, BLK)
                if p < PAIR:
                    plane[pl.ds(p * ROWS + i * BLK, BLK), cols] = block
                else:
                    start = (p - PAIR) * (ROWS + HALF) + i * BLK
                    ring[pl.ds(start, BLK), cols] = block
    for i in range(HALF // BLK):
        source = core * HALF + i * BLK
        source = pl.multiple_of(source, BLK)
        row = core * (HALF // BLK) + i
        for j in range(COLS // BLK):
            cols = pl.ds(j * BLK, BLK)
            ring[pl.ds(ROWS + i * BLK, BLK), cols] = masked(virt, (), source, j * BLK, mask_virt[row, j])
            occ_half[0, pl.ds(i * BLK, BLK), cols] = masked(occ, (), source, j * BLK, mask_occ[row, j])


def mask_inputs(pos, mask_int, mask_occ, mask_virt, integrals, occ, virt):
    return pl.pallas_call(
        mask_kernel,
        out_shape=(
            jax.ShapeDtypeStruct((PAIR * ROWS, COLS), BF16),
            jax.ShapeDtypeStruct((PAIR * ROWS + HALF, COLS), BF16),
            jax.ShapeDtypeStruct((1, HALF, COLS), BF16),
        ),
        in_specs=[SMEM] * 4 + [VMEM] * 3,
        out_specs=(VMEM, VMEM, VMEM),
        compiler_params=PARAMS,
        name="mask_inputs",
    )(pos, mask_int, mask_occ, mask_virt, integrals, occ, virt)


def virt_index(pos, offsets):
    z, y, x, core = pos[0], pos[1], pos[2], pos[3]
    first, second = offsets
    own_x = lax.rem(x + jnp.where(core == 0, first, second) + 4, 4)
    own_y = lax.rem(y + jnp.where(core == 0, second, first) + 4, 4)
    tile = own_y * 4 + own_x
    offset = lax.rem(lax.div(tile, 2) - z + 8, 8)
    place = jnp.where(offset < 4, 2 * offset, 2 * (8 - offset) - 1)
    return place + jnp.where(lax.rem(tile, 2) == core, 0, 8)


def chi_rows(first_row, polar, others):
    shape = (8, BLK)
    rows = lax.broadcasted_iota(jnp.int32, shape, 0)
    cols = lax.broadcasted_iota(jnp.int32, shape, 1)
    total = jnp.zeros(shape, F32)
    step = 64
    for p in range(PAIR):
        def body(i, sums):
            at = pl.ds(pl.multiple_of(i * step, step), step)
            left = polar(p, at).astype(F32)
            new = []
            for q, partial in enumerate(sums):
                product = left * others[q](at).astype(F32)
                product = product[:, :BLK] + product[:, BLK:]
                new.append(partial + jnp.sum(product.reshape(step // 8, 8, BLK), axis=0))
            return tuple(new)

        sums = lax.fori_loop(0, ROWS // step, body, tuple(jnp.zeros(shape, F32) for _ in others))
        for q, partial in enumerate(sums):
            total = total + jnp.where((rows == first_row + p) & (cols == q), jnp.sum(partial), 0.0)
    return total


def all_aux(plane, ring, other_plane, other_ring):
    def rows_of(ref, start):
        return lambda at: ref[pl.ds(pl.multiple_of(start + at.start, 64), at.size), :]

    return [
        rows_of(ref, start)
        for a, b in ((plane, ring), (other_plane, other_ring))
        for ref, start in ((a, 0), (a, ROWS), (b, 0), (b, ROWS + HALF))
    ]


def plane_sum(pos, groups, pieces, virt, acc):
    for group, piece in zip(groups, pieces):
        for k, offsets in enumerate(group):
            tile = piece[pl.ds(k * PAIR * ROWS, PAIR * ROWS), :]
            acc[...] += jnp.dot(tile, virt[virt_index(pos, offsets)], preferred_element_type=F32)


def plane_kernel(groups, first, *refs):
    pos, virt = refs[0], refs[1]
    pieces = refs[2:2 + len(groups)]
    out = refs[-1]
    if first:
        out[...] = jnp.zeros_like(out)
    else:
        out[...] = refs[2 + len(groups)][...]
    plane_sum(pos, groups, pieces, virt, out)


def plane_product(pos, virt, groups, pieces, acc=None):
    tiles = sum(len(group) for group in groups)
    return pl.pallas_call(
        functools.partial(plane_kernel, groups, acc is None),
        out_shape=jax.ShapeDtypeStruct((PAIR * ROWS, COLS), F32),
        in_specs=[SMEM] + [VMEM] * (1 + len(groups) + (acc is not None)),
        out_specs=VMEM,
        compiler_params=PARAMS,
        cost_estimate=pl.CostEstimate(
            flops=2 * tiles * PAIR * ROWS * COLS * COLS, bytes_accessed=4 << 20, transcendentals=0
        ),
        name="plane_product",
    )(pos, virt, *pieces, *(() if acc is None else (acc,)))


def plane_half_kernel(groups, pos, virt, top, bottom, acc_in, out, acc):
    acc[...] = acc_in[...]
    plane_sum(pos, groups, (top, bottom), virt, acc)
    out[...] = acc[...].astype(BF16)


def plane_finish(pos, virt, pieces, acc):
    return pl.pallas_call(
        functools.partial(plane_half_kernel, (TOP, BOTTOM)),
        out_shape=jax.ShapeDtypeStruct((PAIR * ROWS, COLS), BF16),
        in_specs=[SMEM] + [VMEM] * 4,
        out_specs=VMEM,
        scratch_shapes=[pltpu.VMEM((PAIR * ROWS, COLS), F32)],
        compiler_params=PARAMS,
        name="plane_finish",
    )(pos, virt, *pieces, acc)


def polar_plane_kernel(pos, virt, top, bottom, acc_in, a0, b0, a1, b1, chi_in, polar_in, polar, chi, acc):
    acc[...] = acc_in[...]
    plane_sum(pos, (TOP, BOTTOM), (top, bottom), virt, acc)
    for p in range(PAIR):
        polar[p] = acc[pl.ds(p * ROWS, ROWS), :].astype(BF16)
    chi[...] = chi_in[...] + chi_rows(PAIR, lambda p, at: polar[p, at, :], all_aux(a0, b0, a1, b1))


def polar_plane(pos, virt, pieces, acc, aux, chi, polar):
    whole = lambda a: pl.BlockSpec(a.shape, lambda i: (0,) * a.ndim)
    operands = (virt, *pieces, acc, *aux, chi)
    return pl.pallas_call(
        polar_plane_kernel,
        grid=(1,),
        out_shape=(
            jax.ShapeDtypeStruct((2 * PAIR, ROWS, COLS), BF16),
            jax.ShapeDtypeStruct((8, BLK), F32),
        ),
        in_specs=[SMEM] + [whole(a) for a in operands] + [pl.BlockSpec(memory_space=pl.ANY)],
        out_specs=(pl.BlockSpec((PAIR, ROWS, COLS), lambda i: (1, 0, 0)), pl.BlockSpec((8, BLK), lambda i: (0, 0))),
        scratch_shapes=[pltpu.VMEM((PAIR * ROWS, COLS), F32)],
        input_output_aliases={len(operands) + 1: 0},
        compiler_params=PARAMS,
        name="polar_plane",
    )(pos, *operands, polar)


def ring_sum(pos, spare, occ, pieces, acc):
    z = pos[0]
    acc[...] = jnp.zeros_like(acc)
    for place, offset in enumerate(RING[:-1]):
        source = lax.rem(z + offset + 8, 8)
        for p in range(PAIR):
            for i in range(ROWS // HALF):
                if place < 7:
                    start = p * (ROWS + spare) + i * HALF
                    piece = pieces[place]
                else:
                    start = p * (spare // 2) + i * HALF
                    piece = pieces[place + p]
                tile = piece[pl.ds(start, HALF), :]
                acc[p] += jnp.dot(occ[source * 2 + i], tile, preferred_element_type=F32)


def ring_kernel(spare, pos, occ, *refs):
    pieces, out, acc = refs[:9], refs[9], refs[10]
    ring_sum(pos, spare, occ, pieces, acc)
    for p in range(PAIR):
        out[pl.ds(p * ROWS, ROWS), :] = acc[p].astype(BF16)


def ring_product(pos, occ, pieces, spare):
    return pl.pallas_call(
        functools.partial(ring_kernel, spare),
        out_shape=jax.ShapeDtypeStruct((PAIR * ROWS, COLS), BF16),
        in_specs=[SMEM] + [VMEM] * 10,
        out_specs=VMEM,
        scratch_shapes=[pltpu.VMEM((PAIR, ROWS, COLS), F32)],
        compiler_params=PARAMS,
        cost_estimate=pl.CostEstimate(flops=2 << 30, bytes_accessed=9 << 20, transcendentals=0),
        name="ring_product",
    )(pos, occ, *pieces)


def polar_ring_kernel(pos, occ, *refs):
    pieces, aux = refs[:9], refs[9:13]
    polar, chi, acc = refs[13:]
    ring_sum(pos, 0, occ, pieces, acc)
    for p in range(PAIR):
        polar[p] = acc[p].astype(BF16)
    chi[...] = chi_rows(0, lambda p, at: polar[p, at, :], all_aux(*aux))


def polar_ring(pos, occ, pieces, aux):
    whole = lambda a: pl.BlockSpec(a.shape, lambda i: (0,) * a.ndim)
    operands = (occ, *pieces, *aux)
    return pl.pallas_call(
        polar_ring_kernel,
        grid=(1,),
        out_shape=(
            jax.ShapeDtypeStruct((2 * PAIR, ROWS, COLS), BF16),
            jax.ShapeDtypeStruct((8, BLK), F32),
        ),
        in_specs=[SMEM] + [whole(a) for a in operands],
        out_specs=(pl.BlockSpec((PAIR, ROWS, COLS), lambda i: (0, 0, 0)), pl.BlockSpec((8, BLK), lambda i: (0, 0))),
        scratch_shapes=[pltpu.VMEM((PAIR, ROWS, COLS), F32)],
        compiler_params=PARAMS,
        cost_estimate=pl.CostEstimate(flops=2 << 30, bytes_accessed=12 << 20, transcendentals=0),
        name="polar_ring",
    )(pos, *operands)


def body(integrals, density_occ, density_virt, mask_int, mask_occ, mask_virt):
    core = lax.axis_index("layer")
    col = lax.axis_index("col")
    pos = jnp.stack([lax.axis_index("row"), col // 4, col % 4, core]).astype(jnp.int32)

    plane_aux, ring_aux, occ_half = mask_inputs(
        pos, mask_int, mask_occ, mask_virt, integrals, density_occ, density_virt
    )
    occ = lax.all_gather(occ_half, ("col", "layer"), axis=0, tiled=True)
    occ = occ.reshape(16, ROWS, COLS)

    plane_parts = gather_plane(plane_aux)
    ring_parts = gather_ring(ring_aux)
    other_plane, other_ring = swap_cores(plane_aux), swap_cores(ring_aux)

    own_virt = jnp.concatenate(
        [part[ROWS:ROWS + HALF] for part in ring_parts[:7]]
        + [ring_parts[7][ROWS:], ring_parts[8][:HALF // 2]],
        axis=0,
    ).reshape(8, HALF, COLS)
    virt = jnp.concatenate([own_virt, swap_cores(own_virt)], axis=0)

    near, before, after, top, bottom = plane_parts
    acc = plane_product(pos, virt, (NEAR, BEFORE, AFTER), (near, before, after))
    half_tensor = plane_finish(pos, virt, (top, bottom), acc)
    occ_first = ring_product(pos, occ, ring_parts, HALF)

    near, before, after, top, bottom = gather_plane(occ_first)
    ring_parts = gather_ring(half_tensor)
    aux = (plane_aux, ring_aux, other_plane, other_ring)
    polar, chi = polar_ring(pos, occ, ring_parts, aux)
    acc = plane_product(pos, virt, (NEAR,), (near,))
    acc = plane_product(pos, virt, (BEFORE, AFTER), (before, after), acc)
    polar, chi = polar_plane(pos, virt, (top, bottom), acc, aux, chi, polar)

    shares = lax.all_to_all(jnp.broadcast_to(chi[None], (128, 8, BLK)), ("row", "col"), 0, 0)
    chi = jnp.sum(shares, axis=0)[:2 * PAIR] * (1.0 / (ROWS * lax.axis_size("row")))
    own, other = chi[:, :4], chi[:, 4:8]
    chi = jnp.where(core == 0, jnp.concatenate([own, other], 1), jnp.concatenate([other, own], 1))
    return polar, chi


def solution(mesh):
    in_specs = (
        P("layer", "row", "col"),
        P("row", "col"),
        P("row", "col"),
        P("layer", "row", "col"),
        P("row", "col"),
        P("row", "col"),
    )
    out_specs = (P("layer", "row", "col"), P("layer", None))
    return jax.shard_map(body, mesh=mesh, in_specs=in_specs, out_specs=out_specs, check_vma=False)
```

time: 717 us -> 229 us (0.32)
  blocking collectives: 344 us -> 0 us
  waiting for transfers between devices: 320 us -> 94.7 us
  starting transfers between devices: 0.39 us -> 65.3 us
  Pallas kernels: 0 us -> 27.8 us
  matrix products: 24.6 us -> 0 us
  local copies, waits for them, and re-layouts: 4.11 us -> 24.6 us
    psum x1 -> x0, blocking collectives: 344 us -> none  [body(): chi_block = lax.psum(partial_value, ('row', 'col')) * (1.0 / basis_count)]
    all_gather x5 -> x1, waiting for transfers between devices: 320 us -> 0.01 us  [body(): occ = lax.all_gather(occ_half, ('col', 'layer'), axis=0, tiled=True)]
    ppermute x0 -> x33, waiting for transfers between devices: none -> 75.2 us  [the longest x16 58.6 us: ring_move(): return lax.ppermute(value, 'row', [(i, (i + shift) % 8) for i in range(8)])]
    ppermute x0 -> x33, starting transfers between devices: none -> 54.6 us  [the longest x16 29.8 us: ring_move(): return lax.ppermute(value, 'row', [(i, (i + shift) % 8) for i in range(8)])]
    pallas_call x0 -> x8, Pallas kernels: none -> 27.8 us  [the longest x3 9.65 us: plane_product(): pl.pallas_call(functools.partial(plane_kernel, groups, acc is None), out_...]
    dot_general x3 -> x0, matrix products: 24.6 us -> none  [the longest x1 11.9 us: body(): jnp.einsum('pam,mb->pab', lax.all_gather(masked_int, 'col', axis=2, tiled...]
    all_to_all x0 -> x1, waiting for transfers between devices: none -> 19.5 us  [body(): lax.all_to_all(jnp.broadcast_to(chi[None], (128, 8, BLK)), ('row', 'col')...]
    unnamed x7 -> x62, local copies, waits for them, and re-layouts: 1.33 us -> 17.4 us
  transfers between devices with their start and end apart: 5 -> 35, of which waited for: 5 -> 12; matrix products, arithmetic and copies ran while one was open for 4% -> 3% of each run, Pallas kernels for 0% -> 10%
where the time goes in v1:
time: 229 us; the launch traced here: 228 us
  waiting for transfers between devices  94.7 us (41%)
  starting transfers between devices  65.3 us (29%)
  Pallas kernels  27.8 us (12%)
  local copies, waits for them, and re-layouts  24.6 us (11%)
  between operations  14.5 us (6%)
    ppermute x16, waiting for transfers between devices, ring_move(): return lax.ppermute(value, 'row', [(i, (i + shift) % 8) for i in range(8)])  58.6 us
    ppermute x16, starting transfers between devices, ring_move(): return lax.ppermute(value, 'row', [(i, (i + shift) % 8) for i in range(8)])  29.8 us
    ppermute x14, starting transfers between devices, plane_move(): return lax.ppermute(value, ('col', 'layer'), plane_perm(shift, first))  24.7 us
    all_to_all x1, waiting for transfers between devices, body(): lax.all_to_all(jnp.broadcast_to(chi[None], (128, 8, BLK)), ('row', 'col')...  19.5 us
    unnamed x62, local copies, waits for them, and re-layouts  17.4 us
    ppermute x14, waiting for transfers between devices, plane_move(): return lax.ppermute(value, ('col', 'layer'), plane_perm(shift, first))  16.6 us
    all_to_all x1, starting transfers between devices, body(): lax.all_to_all(jnp.broadcast_to(chi[None], (128, 8, BLK)), ('row', 'col')...  10.7 us
    pallas_call x3, Pallas kernels, plane_product(): pl.pallas_call(functools.partial(plane_kernel, groups, acc is None), out_...  9.65 us
  transfers between devices with their start and end apart: 35, of which 12 were waited for; matrix products, arithmetic and copies ran while one was open for 3% of the time, Pallas kernels for 10%

profile of v1, /device:TPU:2, one launch (start us, length us, event | category | flops | bytes accessed | tf_op | source)
XLA Modules:
  0.0 228.2 jit_solution(12531456890322995669)
XLA Ops:
  16.3 4.0 %collective-permute-start.1 = (bf16[1280,256]{1,0:T(8,128)(2,1)S(1)}, bf16[1280,256]{1,0:T(8,128)(2,1)S(1)}, u32[]{:S(2)}, u32[]{:S(2)}) collective-permute-start(bf16[1280,256]{1,0:T(8,128)(2,1)S(1)} %get-tuple-element.9.refs_0_.refs_10_.b0), channel_id=1, source_target_pairs={{0,224},{32,0},{64,32},{96,64},{128,96},{160,128},{192,160},{224,1... | collective-permute-start | bytes 1966088 | tf_op jit(solution)/shard_map/ppermute | solution.py:42
  24.6 5.0 %collective-permute-done.18 = bf16[1024,256]{1,0:T(8,128)(2,1)S(1)} collective-permute-done((bf16[1024,256]{1,0:T(8,128)(2,1)S(1)}, bf16[1024,256]{1,0:T(8,128)(2,1)S(1)}, u32[]{:S(2)}, u32[]{:S(2)}) %collective-permute-start.18) | collective-permute-done | bytes 524320 | tf_op jit(solution)/shard_map/ppermute | solution.py:38
  29.6 5.4 %collective-permute-done.refs_1_ = bf16[1280,256]{1,0:T(8,128)(2,1)S(1)} collective-permute-done((bf16[1280,256]{1,0:T(8,128)(2,1)S(1)}, bf16[1280,256]{1,0:T(8,128)(2,1)S(1)}, u32[]{:S(2)}, u32[]{:S(2)}) %collective-permute-start) | collective-permute-done | bytes 655392 | tf_op jit(solution)/shard_map/ppermute | solution.py:42
  41.8 10.4 %collective-permute-done.2.refs_3_ = bf16[1280,256]{1,0:T(8,128)(2,1)S(1)} collective-permute-done((bf16[1280,256]{1,0:T(8,128)(2,1)S(1)}, bf16[1280,256]{1,0:T(8,128)(2,1)S(1)}, u32[]{:S(2)}, u32[]{:S(2)}) %collective-permute-start.2) | collective-permute-done | bytes 655392 | tf_op jit(solution)/shard_map/ppermute | solution.py:42
  52.2 3.2 %collective-permute-start.5 = (bf16[1280,256]{1,0:T(8,128)(2,1)S(1)}, bf16[1280,256]{1,0:T(8,128)(2,1)S(1)}, u32[]{:S(2)}, u32[]{:S(2)}) collective-permute-start(bf16[1280,256]{1,0:T(8,128)(2,1)S(1)} %collective-permute-done.3.refs_4_), channel_id=1, source_target_pairs={{0,224},{32,0},{64,32},{96,64},{128,96},{160,128},{192,160},{224,1... | collective-permute-start | bytes 1966088 | tf_op jit(solution)/shard_map/ppermute | solution.py:42
  56.3 12.2 %collective-permute-done.4.refs_5_ = bf16[1280,256]{1,0:T(8,128)(2,1)S(1)} collective-permute-done((bf16[1280,256]{1,0:T(8,128)(2,1)S(1)}, bf16[1280,256]{1,0:T(8,128)(2,1)S(1)}, u32[]{:S(2)}, u32[]{:S(2)}) %collective-permute-start.4) | collective-permute-done | bytes 655392 | tf_op jit(solution)/shard_map/ppermute | solution.py:42
  68.6 3.3 %collective-permute-start.7 = (bf16[640,256]{1,0:T(8,128)(2,1)S(1)}, bf16[640,256]{1,0:T(8,128)(2,1)S(1)}, u32[]{:S(2)}, u32[]{:S(2)}) collective-permute-start(bf16[640,256]{1,0:T(8,128)(2,1)S(1)} %slice.89), channel_id=1, source_target_pairs={{0,224},{32,0},{64,32},{96,64},{128,96},{160,128},{192,160},{224,1... | collective-permute-start | bytes 983048 | tf_op jit(solution)/shard_map/ppermute | solution.py:42
  72.0 5.1 %collective-permute-done.6.refs_7_ = bf16[640,256]{1,0:T(8,128)(2,1)S(1)} collective-permute-done((bf16[640,256]{1,0:T(8,128)(2,1)S(1)}, bf16[640,256]{1,0:T(8,128)(2,1)S(1)}, u32[]{:S(2)}, u32[]{:S(2)}) %collective-permute-start.6) | collective-permute-done | bytes 327712 | tf_op jit(solution)/shard_map/ppermute | solution.py:42
  88.0 4.6 %ring_product.1 = bf16[1024,256]{1,0:T(8,128)(2,1)S(1)} custom-call(s32[4]{0:T(128)S(1)} %pad_add_fusion.pos.refs_0_, bf16[16,512,256]{2,1,0:T(8,128)(2,1)} %bitcast.6, bf16[1280,256]{1,0:T(8,128)(2,1)S(1)} %get-tuple-element.9.refs_0_.refs_10_.b0, bf16[1280,256]{1,0:T(8,128)(2,1)S(1)} %copy-done.9, bf16[1280,256]{1,0:T(8,128)(2,1)S(1)} %copy-done.11, ...), custom_call_target="tpu_custom_call" | custom-call | flops 2147483648 | bytes 9437184 | tf_op jit(solution)/shard_map/ring_product/pallas_call | solution.py:269
  102.1 3.3 %collective-permute-start.24 = (bf16[2048,256]{1,0:T(8,128)(2,1)S(1)}, bf16[2048,256]{1,0:T(8,128)(2,1)S(1)}, u32[]{:S(2)}, u32[]{:S(2)}) collective-permute-start(bf16[2048,256]{1,0:T(8,128)(2,1)S(1)} %slice.94), channel_id=1, source_target_pairs={{0,24},{1,7},{2,26},{3,1},{4,28},{5,3},{6,30},{7,5},{8,0},{9,15},{... | collective-permute-start | bytes 3145736 | tf_op jit(solution)/shard_map/ppermute | solution.py:38
  105.3 3.6 %collective-permute-done.11 = bf16[1024,256]{1,0:T(8,128)(2,1)S(1)} collective-permute-done((bf16[1024,256]{1,0:T(8,128)(2,1)S(1)}, bf16[1024,256]{1,0:T(8,128)(2,1)S(1)}, u32[]{:S(2)}, u32[]{:S(2)}) %collective-permute-start.11) | collective-permute-done | bytes 524320 | tf_op jit(solution)/shard_map/ppermute | solution.py:38
  109.0 7.9 %collective-permute-done.9 = bf16[1024,256]{1,0:T(8,128)(2,1)S(1)} collective-permute-done((bf16[1024,256]{1,0:T(8,128)(2,1)S(1)}, bf16[1024,256]{1,0:T(8,128)(2,1)S(1)}, u32[]{:S(2)}, u32[]{:S(2)}) %collective-permute-start.9) | collective-permute-done | bytes 524320 | tf_op jit(solution)/shard_map/ppermute | solution.py:38
  121.1 4.8 %plane_product.5.acc_in = f32[1024,256]{1,0:T(8,128)S(1)} custom-call(s32[4]{0:T(128)S(1)} %pad_add_fusion.pos.refs_0_, bf16[16,256,256]{2,1,0:T(8,128)(2,1)S(1)} %pad_maximum_fusion.refs_1_.virt, bf16[4096,256]{1,0:T(8,128)(2,1)S(1)} %constant_dynamic-update-slice_fusion.refs_2_, bf16[4096,256]{1,0:T(8,128)(2,1)} %collective-permute-done.21.refs_3_, ...), custom_call_target="tpu_custom_call" | custom-call | flops 1610612736 | bytes 4194304 | tf_op jit(solution)/shard_map/plane_product/pallas_call | solution.py:186
  130.5 9.1 %collective-permute-done.25.refs_1_ = bf16[1024,256]{1,0:T(8,128)(2,1)S(1)} collective-permute-done((bf16[1024,256]{1,0:T(8,128)(2,1)S(1)}, bf16[1024,256]{1,0:T(8,128)(2,1)S(1)}, u32[]{:S(2)}, u32[]{:S(2)}) %collective-permute-start.25) | collective-permute-done | bytes 524320 | tf_op jit(solution)/shard_map/ppermute | solution.py:42
  139.6 3.5 %collective-permute-start.28 = (bf16[1024,256]{1,0:T(8,128)(2,1)S(1)}, bf16[1024,256]{1,0:T(8,128)(2,1)S(1)}, u32[]{:S(2)}, u32[]{:S(2)}) collective-permute-start(bf16[1024,256]{1,0:T(8,128)(2,1)S(1)} %collective-permute-done.26.refs_2_), channel_id=1, source_target_pairs={{0,224},{32,0},{64,32},{96,64},{128,96},{160,128},{192,160},{224,1... | collective-permute-start | bytes 1572872 | tf_op jit(solution)/shard_map/ppermute | solution.py:42
  143.1 9.5 %collective-permute-done.27.refs_3_ = bf16[1024,256]{1,0:T(8,128)(2,1)S(1)} collective-permute-done((bf16[1024,256]{1,0:T(8,128)(2,1)S(1)}, bf16[1024,256]{1,0:T(8,128)(2,1)S(1)}, u32[]{:S(2)}, u32[]{:S(2)}) %collective-permute-start.27) | collective-permute-done | bytes 524320 | tf_op jit(solution)/shard_map/ppermute | solution.py:42
  153.1 3.7 %collective-permute-start.30 = (bf16[1024,256]{1,0:T(8,128)(2,1)S(1)}, bf16[1024,256]{1,0:T(8,128)(2,1)S(1)}, u32[]{:S(2)}, u32[]{:S(2)}) collective-permute-start(bf16[1024,256]{1,0:T(8,128)(2,1)S(1)} %collective-permute-done.28.refs_4_), channel_id=1, source_target_pairs={{0,224},{32,0},{64,32},{96,64},{128,96},{160,128},{192,160},{224,1... | collective-permute-start | bytes 1572872 | tf_op jit(solution)/shard_map/ppermute | solution.py:42
  163.8 3.4 %collective-permute-start.32 = (bf16[512,256]{1,0:T(8,128)(2,1)S(1)}, bf16[512,256]{1,0:T(8,128)(2,1)S(1)}, u32[]{:S(2)}, u32[]{:S(2)}) collective-permute-start(bf16[512,256]{1,0:T(8,128)(2,1)S(1)} %slice.96), channel_id=1, source_target_pairs={{0,224},{32,0},{64,32},{96,64},{128,96},{160,128},{192,160},{224,1... | collective-permute-start | bytes 786440 | tf_op jit(solution)/shard_map/ppermute | solution.py:42
  167.3 6.5 %collective-permute-done.31.refs_7_ = bf16[512,256]{1,0:T(8,128)(2,1)S(1)} collective-permute-done((bf16[512,256]{1,0:T(8,128)(2,1)S(1)}, bf16[512,256]{1,0:T(8,128)(2,1)S(1)}, u32[]{:S(2)}, u32[]{:S(2)}) %collective-permute-start.31) | collective-permute-done | bytes 262176 | tf_op jit(solution)/shard_map/ppermute | solution.py:42
  173.7 6.5 %polar_ring.1 = (bf16[4,512,256]{2,1,0:T(8,128)(2,1)}, f32[8,128]{1,0:T(8,128)S(1)}) custom-call(s32[4]{0:T(128)S(1)} %pad_add_fusion.pos.refs_0_, bf16[16,512,256]{2,1,0:T(8,128)(2,1)} %bitcast.7, bf16[1024,256]{1,0:T(8,128)(2,1)S(1)} %plane_finish.1.refs_0_, bf16[1024,256]{1,0:T(8,128)(2,1)S(1)} %collective-permute-done.25.refs_1_, ...), custom_call_target="tpu_custom_call" | custom-call | flops 2147483648 | bytes 12582912 | tf_op jit(solution)/shard_map/polar_ring/pallas_call | solution.py:293
  181.6 3.6 %plane_product.4.acc_in = f32[1024,256]{1,0:T(8,128)S(1)} custom-call(s32[4]{0:T(128)S(1)} %pad_add_fusion.pos.refs_0_, bf16[16,256,256]{2,1,0:T(8,128)(2,1)S(1)} %pad_maximum_fusion.refs_1_.virt, bf16[4096,256]{1,0:T(8,128)(2,1)} %collective-permute-done.12.refs_2_, bf16[4096,256]{1,0:T(8,128)(2,1)} %collective-permute-done.14.refs_3_, ...), custom_call_target="tpu_custom_call" | custom-call | flops 1073741824 | bytes 4194304 | tf_op jit(solution)/shard_map/plane_product/pallas_call | solution.py:186
  185.2 4.2 %polar_plane.1 = (bf16[4,512,256]{2,1,0:T(8,128)(2,1)}, f32[8,128]{1,0:T(8,128)S(1)}) custom-call(s32[4]{0:T(128)S(1)} %pad_add_fusion.pos.refs_0_, bf16[16,256,256]{2,1,0:T(8,128)(2,1)} %copy-done, bf16[2048,256]{1,0:T(8,128)(2,1)S(1)} %collective-permute-done.13.top, ...), custom_call_target="tpu_custom_call", output_to_operand_aliasing={{0}: (10, {})} | custom-call | tf_op jit(solution)/shard_map/polar_plane/pallas_call | solution.py:228
  190.2 10.7 %all-to-all-start = ((f32[128,8,128]{2,1,0:T(8,128)}), f32[128,8,128]{2,1,0:T(8,128)S(1)}, u32[]{:S(2)}, u32[]{:S(2)}) async-start(f32[128,8,128]{2,1,0:T(8,128)} %broadcast_in_dim.2), calls=%async_computation | async-start | bytes 1048576 | tf_op jit(solution)/shard_map/all_to_all | solution.py:344
  200.9 19.5 %all-to-all-done = f32[128,8,128]{2,1,0:T(8,128)S(1)} async-done(((f32[128,8,128]{2,1,0:T(8,128)}), f32[128,8,128]{2,1,0:T(8,128)S(1)}, u32[]{:S(2)}, u32[]{:S(2)}) %all-to-all-start) | async-done | bytes 524320 | tf_op jit(solution)/shard_map/all_to_all | solution.py:344
  (135 shorter events, 60.6 us)
Async XLA Ops:
  7.2 72.3 %all-gather.2.cloned.1.call-start = ((), (), s32[]{:S(2)}) async-start(), calls=%async_computation.1 | async-start | bytes 4325376 | tf_op jit(solution)/shard_map/all_gather | solution.py:317
  14.3 20.7 %collective-permute-start = (bf16[1280,256]{1,0:T(8,128)(2,1)S(1)}, bf16[1280,256]{1,0:T(8,128)(2,1)S(1)}, u32[]{:S(2)}, u32[]{:S(2)}) collective-permute-start(bf16[1280,256]{1,0:T(8,128)(2,1)S(1)} %get-tuple-element.9.refs_0_.refs_10_.b0), channel_id=1, source_target_pairs={{0,32},{32,64},{64,96},{96,128},{128,160},{160,192},{192,224},{224... | collective-permute-start | bytes 1966088 | tf_op jit(solution)/shard_map/ppermute | solution.py:42
  16.3 18.7 %collective-permute-start.1 = (bf16[1280,256]{1,0:T(8,128)(2,1)S(1)}, bf16[1280,256]{1,0:T(8,128)(2,1)S(1)}, u32[]{:S(2)}, u32[]{:S(2)}) collective-permute-start(bf16[1280,256]{1,0:T(8,128)(2,1)S(1)} %get-tuple-element.9.refs_0_.refs_10_.b0), channel_id=1, source_target_pairs={{0,224},{32,0},{64,32},{96,64},{128,96},{160,128},{192,160},{224,1... | collective-permute-start | bytes 1966088 | tf_op jit(solution)/shard_map/ppermute | solution.py:42
  21.9 16.4 %collective-permute-start.19 = (bf16[1024,256]{1,0:T(8,128)(2,1)S(1)}, bf16[1024,256]{1,0:T(8,128)(2,1)S(1)}, u32[]{:S(2)}, u32[]{:S(2)}) collective-permute-start(bf16[1024,256]{1,0:T(8,128)(2,1)S(1)} %get-tuple-element.11.refs_9_.a0), channel_id=1, source_target_pairs={{0,6},{1,25},{2,0},{3,27},{4,2},{5,29},{6,4},{7,31},{8,14},{9,1},{... | collective-permute-start | bytes 1572872 | tf_op jit(solution)/shard_map/ppermute | solution.py:38
  22.4 15.9 %collective-permute-start.20 = (bf16[1024,256]{1,0:T(8,128)(2,1)S(1)}, bf16[1024,256]{1,0:T(8,128)(2,1)S(1)}, u32[]{:S(2)}, u32[]{:S(2)}) collective-permute-start(bf16[1024,256]{1,0:T(8,128)(2,1)S(1)} %get-tuple-element.11.refs_9_.a0), channel_id=1, source_target_pairs={{0,4},{1,17},{2,6},{3,19},{4,0},{5,21},{6,2},{7,23},{8,12},{9,25},... | collective-permute-start | bytes 1572872 | tf_op jit(solution)/shard_map/ppermute | solution.py:38
  35.0 17.1 %collective-permute-start.2 = (bf16[1280,256]{1,0:T(8,128)(2,1)S(1)}, bf16[1280,256]{1,0:T(8,128)(2,1)S(1)}, u32[]{:S(2)}, u32[]{:S(2)}) collective-permute-start(bf16[1280,256]{1,0:T(8,128)(2,1)S(1)} %collective-permute-done.refs_1_), channel_id=1, source_target_pairs={{0,32},{32,64},{64,96},{96,128},{128,160},{160,192},{192,224},{224... | collective-permute-start | bytes 1966088 | tf_op jit(solution)/shard_map/ppermute | solution.py:42
  35.0 17.1 %collective-permute-start.3 = (bf16[1280,256]{1,0:T(8,128)(2,1)S(1)}, bf16[1280,256]{1,0:T(8,128)(2,1)S(1)}, u32[]{:S(2)}, u32[]{:S(2)}) collective-permute-start(bf16[1280,256]{1,0:T(8,128)(2,1)S(1)} %collective-permute-done.1.refs_2_), channel_id=1, source_target_pairs={{0,224},{32,0},{64,32},{96,64},{128,96},{160,128},{192,160},{224,1... | collective-permute-start | bytes 1966088 | tf_op jit(solution)/shard_map/ppermute | solution.py:42
  38.4 59.6 %collective-permute-start.21 = (bf16[4096,256]{1,0:T(8,128)(2,1)S(1)}, bf16[4096,256]{1,0:T(8,128)(2,1)}, u32[]{:S(2)}, u32[]{:S(2)}) collective-permute-start(bf16[4096,256]{1,0:T(8,128)(2,1)S(1)} %constant_dynamic-update-slice_fusion.refs_2_), channel_id=1, source_target_pairs={{0,8},{1,3},{2,10},{3,5},{4,12},{5,7},{6,14},{7,1},{8,16},{9,11},{... | collective-permute-start | bytes 6291464 | tf_op jit(solution)/shard_map/ppermute | solution.py:38
  40.1 59.2 %collective-permute-start.23 = (bf16[4096,256]{1,0:T(8,128)(2,1)S(1)}, bf16[4096,256]{1,0:T(8,128)(2,1)}, u32[]{:S(2)}, u32[]{:S(2)}) collective-permute-start(bf16[4096,256]{1,0:T(8,128)(2,1)S(1)} %constant_dynamic-update-slice_fusion.refs_2_), channel_id=1, source_target_pairs={{0,24},{1,7},{2,26},{3,1},{4,28},{5,3},{6,30},{7,5},{8,0},{9,15},{... | collective-permute-start | bytes 6291464 | tf_op jit(solution)/shard_map/ppermute | solution.py:38
  52.1 16.3 %collective-permute-start.4 = (bf16[1280,256]{1,0:T(8,128)(2,1)S(1)}, bf16[1280,256]{1,0:T(8,128)(2,1)S(1)}, u32[]{:S(2)}, u32[]{:S(2)}) collective-permute-start(bf16[1280,256]{1,0:T(8,128)(2,1)S(1)} %collective-permute-done.2.refs_3_), channel_id=1, source_target_pairs={{0,32},{32,64},{64,96},{96,128},{128,160},{160,192},{192,224},{224... | collective-permute-start | bytes 1966088 | tf_op jit(solution)/shard_map/ppermute | solution.py:42
  52.2 16.4 %collective-permute-start.5 = (bf16[1280,256]{1,0:T(8,128)(2,1)S(1)}, bf16[1280,256]{1,0:T(8,128)(2,1)S(1)}, u32[]{:S(2)}, u32[]{:S(2)}) collective-permute-start(bf16[1280,256]{1,0:T(8,128)(2,1)S(1)} %collective-permute-done.3.refs_4_), channel_id=1, source_target_pairs={{0,224},{32,0},{64,32},{96,64},{128,96},{160,128},{192,160},{224,1... | collective-permute-start | bytes 1966088 | tf_op jit(solution)/shard_map/ppermute | solution.py:42
  93.4 15.6 %collective-permute-start.11 = (bf16[1024,256]{1,0:T(8,128)(2,1)S(1)}, bf16[1024,256]{1,0:T(8,128)(2,1)S(1)}, u32[]{:S(2)}, u32[]{:S(2)}) collective-permute-start(bf16[1024,256]{1,0:T(8,128)(2,1)S(1)} %ring_product.1), channel_id=1, source_target_pairs={{0,4},{1,17},{2,6},{3,19},{4,0},{5,21},{6,2},{7,23},{8,12},{9,25},... | collective-permute-start | bytes 1572872 | tf_op jit(solution)/shard_map/ppermute | solution.py:38
  95.8 21.1 %collective-permute-start.9 = (bf16[1024,256]{1,0:T(8,128)(2,1)S(1)}, bf16[1024,256]{1,0:T(8,128)(2,1)S(1)}, u32[]{:S(2)}, u32[]{:S(2)}) collective-permute-start(bf16[1024,256]{1,0:T(8,128)(2,1)S(1)} %ring_product.1), channel_id=1, source_target_pairs={{0,2},{1,9},{2,4},{3,11},{4,6},{5,13},{6,0},{7,15},{8,10},{9,17},{... | collective-permute-start | bytes 1572872 | tf_op jit(solution)/shard_map/ppermute | solution.py:38
  97.9 22.9 %collective-permute-start.8 = (bf16[8,256,256]{2,1,0:T(8,128)(2,1)S(1)}, bf16[8,256,256]{2,1,0:T(8,128)(2,1)S(1)}, u32[]{:S(2)}, u32[]{:S(2)}) collective-permute-start(bf16[8,256,256]{2,1,0:T(8,128)(2,1)S(1)} %bitcast.8), channel_id=1, source_target_pairs={{0,1},{1,0},{2,3},{3,2},{4,5},{5,4},{6,7},{7,6},{8,9},{9,8},{10,11... | collective-permute-start | bytes 3145736 | tf_op jit(solution)/shard_map/ppermute | solution.py:46
  99.3 26.5 %collective-permute-start.22 = (bf16[2048,256]{1,0:T(8,128)(2,1)S(1)}, bf16[2048,256]{1,0:T(8,128)(2,1)S(1)}, u32[]{:S(2)}, u32[]{:S(2)}) collective-permute-start(bf16[2048,256]{1,0:T(8,128)(2,1)S(1)} %slice.93), channel_id=1, source_target_pairs={{0,8},{1,3},{2,10},{3,5},{4,12},{5,7},{6,14},{7,1},{8,16},{9,11},{... | collective-permute-start | bytes 3145736 | tf_op jit(solution)/shard_map/ppermute | solution.py:38
  102.1 23.8 %collective-permute-start.24 = (bf16[2048,256]{1,0:T(8,128)(2,1)S(1)}, bf16[2048,256]{1,0:T(8,128)(2,1)S(1)}, u32[]{:S(2)}, u32[]{:S(2)}) collective-permute-start(bf16[2048,256]{1,0:T(8,128)(2,1)S(1)} %slice.94), channel_id=1, source_target_pairs={{0,24},{1,7},{2,26},{3,1},{4,28},{5,3},{6,30},{7,5},{8,0},{9,15},{... | collective-permute-start | bytes 3145736 | tf_op jit(solution)/shard_map/ppermute | solution.py:38
  117.1 39.7 %collective-permute-start.12 = (bf16[4096,256]{1,0:T(8,128)(2,1)S(1)}, bf16[4096,256]{1,0:T(8,128)(2,1)}, u32[]{:S(2)}, u32[]{:S(2)}) collective-permute-start(bf16[4096,256]{1,0:T(8,128)(2,1)S(1)} %pad_maximum_fusion.1.refs_2_), channel_id=1, source_target_pairs={{0,8},{1,3},{2,10},{3,5},{4,12},{5,7},{6,14},{7,1},{8,16},{9,11},{... | collective-permute-start | bytes 6291464 | tf_op jit(solution)/shard_map/ppermute | solution.py:38
  118.3 39.8 %collective-permute-start.14 = (bf16[4096,256]{1,0:T(8,128)(2,1)S(1)}, bf16[4096,256]{1,0:T(8,128)(2,1)}, u32[]{:S(2)}, u32[]{:S(2)}) collective-permute-start(bf16[4096,256]{1,0:T(8,128)(2,1)S(1)} %pad_maximum_fusion.1.refs_2_), channel_id=1, source_target_pairs={{0,24},{1,7},{2,26},{3,1},{4,28},{5,3},{6,30},{7,5},{8,0},{9,15},{... | collective-permute-start | bytes 6291464 | tf_op jit(solution)/shard_map/ppermute | solution.py:38
  127.2 12.4 %collective-permute-start.25 = (bf16[1024,256]{1,0:T(8,128)(2,1)S(1)}, bf16[1024,256]{1,0:T(8,128)(2,1)S(1)}, u32[]{:S(2)}, u32[]{:S(2)}) collective-permute-start(bf16[1024,256]{1,0:T(8,128)(2,1)S(1)} %plane_finish.1.refs_0_), channel_id=1, source_target_pairs={{0,32},{32,64},{64,96},{96,128},{128,160},{160,192},{192,224},{224... | collective-permute-start | bytes 1572872 | tf_op jit(solution)/shard_map/ppermute | solution.py:42
  139.6 13.0 %collective-permute-start.27 = (bf16[1024,256]{1,0:T(8,128)(2,1)S(1)}, bf16[1024,256]{1,0:T(8,128)(2,1)S(1)}, u32[]{:S(2)}, u32[]{:S(2)}) collective-permute-start(bf16[1024,256]{1,0:T(8,128)(2,1)S(1)} %collective-permute-done.25.refs_1_), channel_id=1, source_target_pairs={{0,32},{32,64},{64,96},{96,128},{128,160},{160,192},{192,224},{224... | collective-permute-start | bytes 1572872 | tf_op jit(solution)/shard_map/ppermute | solution.py:42
  139.6 13.4 %collective-permute-start.28 = (bf16[1024,256]{1,0:T(8,128)(2,1)S(1)}, bf16[1024,256]{1,0:T(8,128)(2,1)S(1)}, u32[]{:S(2)}, u32[]{:S(2)}) collective-permute-start(bf16[1024,256]{1,0:T(8,128)(2,1)S(1)} %collective-permute-done.26.refs_2_), channel_id=1, source_target_pairs={{0,224},{32,0},{64,32},{96,64},{128,96},{160,128},{192,160},{224,1... | collective-permute-start | bytes 1572872 | tf_op jit(solution)/shard_map/ppermute | solution.py:42
  158.0 27.1 %collective-permute-start.13 = (bf16[2048,256]{1,0:T(8,128)(2,1)S(1)}, bf16[2048,256]{1,0:T(8,128)(2,1)S(1)}, u32[]{:S(2)}, u32[]{:S(2)}) collective-permute-start(bf16[2048,256]{1,0:T(8,128)(2,1)S(1)} %slice.91), channel_id=1, source_target_pairs={{0,8},{1,3},{2,10},{3,5},{4,12},{5,7},{6,14},{7,1},{8,16},{9,11},{... | collective-permute-start | bytes 3145736 | tf_op jit(solution)/shard_map/ppermute | solution.py:38
  160.5 24.7 %collective-permute-start.15 = (bf16[2048,256]{1,0:T(8,128)(2,1)}, bf16[2048,256]{1,0:T(8,128)(2,1)S(1)}, u32[]{:S(2)}, u32[]{:S(2)}) collective-permute-start(bf16[2048,256]{1,0:T(8,128)(2,1)} %slice.92), channel_id=1, source_target_pairs={{0,24},{1,7},{2,26},{3,1},{4,28},{5,3},{6,30},{7,5},{8,0},{9,15},{... | collective-permute-start | bytes 3145736 | tf_op jit(solution)/shard_map/ppermute | solution.py:38
  190.2 30.2 %all-to-all-start = ((f32[128,8,128]{2,1,0:T(8,128)}), f32[128,8,128]{2,1,0:T(8,128)S(1)}, u32[]{:S(2)}, u32[]{:S(2)}) async-start(f32[128,8,128]{2,1,0:T(8,128)} %broadcast_in_dim.2), calls=%async_computation | async-start | bytes 1048576 | tf_op jit(solution)/shard_map/all_to_all | solution.py:344
  (35 other events, 264.3 us)
Sparse Core Ops, SparseCore 0:
  14.5 58.7 all-gather.1

commit v2 on v0

v2 whole, which is shorter than its diff:
```python
import functools

import jax
import jax.numpy as jnp
from jax import lax
from jax.experimental import pallas as pl
from jax.experimental.pallas import tpu as pltpu
from jax.sharding import PartitionSpec as P

BLK = 128
ROWS = 512
COLS = 256
HALF = 256
PAIR = 2
AUX = 2 * PAIR
F32 = jnp.float32
BF16 = jnp.bfloat16
VMEM = pl.BlockSpec(memory_space=pltpu.VMEM)
HBM = pl.BlockSpec(memory_space=pltpu.HBM)
PARAMS = pltpu.CompilerParams(vmem_limit_bytes=48 * 1024 * 1024)


def plane_index(y, x, core):
    return ((y % 4) * 4 + x % 4) * 2 + core


def plane_perm(shift, first):
    pairs = []
    for y in range(4):
        for x in range(4):
            for core in range(2):
                along_x = (core == 0) == first
                to = (y, x + shift) if along_x else (y + shift, x)
                pairs.append((plane_index(y, x, core), plane_index(*to, core)))
    return pairs


def plane_move(value, shift, first):
    return lax.ppermute(value, ("col", "layer"), plane_perm(shift, first))


def ring_move(value, shift):
    return lax.ppermute(value, "row", [(i, (i + shift) % 8) for i in range(8)])


def swap_cores(value):
    return lax.ppermute(value, "layer", [(0, 1), (1, 0)])


PLANE = (
    ((0, 0), (-1, 0)),
    ((1, 0), (2, 0)),
    ((0, -1), (-1, -1)),
    ((1, 1), (2, 1)),
    ((1, -1), (2, -1), (0, 2), (-1, 2)),
    ((0, 1), (-1, 1), (1, 2), (2, 2)),
)
PLANE_NEAR, PLANE_FAR = (0, 1, 2, 3), (4, 5)

RING = (0, -1, 1, -2, 2, -3, 3, 4)
RING_NEAR, RING_FAR = (0, 1, 2, 3, 4), (5, 6, 7)


def gather_both(plane, ring, early=None):
    half = ring.shape[0] // 2
    before, after = plane_move(plane, 1, True), plane_move(plane, -1, True)
    up1, down1 = ring_move(ring, 1), ring_move(ring, -1)
    across = plane_move(plane, 2, True)
    before, after, across, up1, down1 = lax.optimization_barrier((before, after, across, up1, down1))
    top = jnp.concatenate([plane, before], axis=0)
    bottom = jnp.concatenate([after, across], axis=0)
    top_before, bottom_after = plane_move(top, 1, False), plane_move(bottom, -1, False)
    up2, down2 = ring_move(up1, 1), ring_move(down1, -1)
    top_before, bottom_after, up2, down2 = lax.optimization_barrier((top_before, bottom_after, up2, down2))
    last_before = plane_move(jnp.concatenate([bottom, top_before], axis=0), 1, False)
    last_after = plane_move(jnp.concatenate([top, bottom_after], axis=0), -1, False)
    up3, down3 = ring_move(up2, 1), ring_move(down2, -1)
    near = (top, bottom, top_before, bottom_after)
    result = None
    if early is not None:
        result = early(near, (ring, up1, down1, up2, down2))
        up3, down3, result = lax.optimization_barrier((up3, down3, result))
    up4, down4 = ring_move(up3[:half], 1), ring_move(down3[half:], -1)
    return near + (last_before, last_after), (ring, up1, down1, up2, down2, up3, down3, up4, down4), result


def whole(array):
    return pl.BlockSpec(array.shape, lambda i: (0,) * array.ndim)


def buffers_of(arrays):
    return [pltpu.VMEM(a.shape, a.dtype) for a in arrays]


def start_all(sources, buffers, sems, first=0):
    copies = [pltpu.make_async_copy(a, b, sems.at[first + i]) for i, (a, b) in enumerate(zip(sources, buffers))]
    for copy in copies:
        copy.start()
    return copies


def mask_kernel(mask_int, mask_occ, mask_virt, integrals, occ, virt, plane, ring, occ_half, aux, buf, occ_buf, virt_buf, sems):
    core = lax.axis_index("layer")
    half = pl.ds(pl.multiple_of(core * HALF, HALF), HALF)
    copies = start_all(
        [virt.at[half], occ.at[half]] + [integrals.at[p] for p in range(AUX)],
        [virt_buf, occ_buf] + [buf.at[p] for p in range(AUX)],
        sems,
    )

    def masked(ref, row, col, weight):
        block = ref[pl.ds(row, BLK), pl.ds(col, BLK)].astype(F32)
        return (block * jnp.broadcast_to(weight.astype(F32), block.shape)).astype(BF16)

    def half_weight(mask, i, j):
        low, high = mask[pl.ds(j, 1), pl.ds(i, 1)], mask[pl.ds(j, 1), pl.ds(HALF // BLK + i, 1)]
        return jnp.where(core == 0, low, high)

    virt_copy, occ_copy, *aux_copies = copies
    virt_copy.wait()
    occ_copy.wait()
    for i in range(HALF // BLK):
        for j in range(COLS // BLK):
            cols = pl.ds(j * BLK, BLK)
            weight = half_weight(mask_virt, i, j)
            ring[pl.ds(ROWS + i * BLK, BLK), cols] = masked(virt_buf, i * BLK, j * BLK, weight)
            weight = half_weight(mask_occ, i, j)
            occ_half[0, pl.ds(i * BLK, BLK), cols] = masked(occ_buf, i * BLK, j * BLK, weight)
    for p in range(AUX):
        aux_copies[p].wait()
        for i in range(ROWS // BLK):
            for j in range(COLS // BLK):
                block = masked(buf.at[p], i * BLK, j * BLK, mask_int[p, pl.ds(j, 1), pl.ds(i, 1)])
                cols = pl.ds(j * BLK, BLK)
                aux[p, pl.ds(i * BLK, BLK), cols] = block
                if p < PAIR:
                    plane[pl.ds(p * ROWS + i * BLK, BLK), cols] = block
                else:
                    ring[pl.ds((p - PAIR) * (ROWS + HALF) + i * BLK, BLK), cols] = block


def mask_inputs(mask_int, mask_occ, mask_virt, integrals, occ, virt):
    outs = (
        jax.ShapeDtypeStruct((PAIR * ROWS, COLS), BF16),
        jax.ShapeDtypeStruct((PAIR * ROWS + HALF, COLS), BF16),
        jax.ShapeDtypeStruct((1, HALF, COLS), BF16),
        jax.ShapeDtypeStruct((AUX, ROWS, COLS), BF16),
    )
    masks = (mask_int.transpose(0, 2, 1), mask_occ.T, mask_virt.T)
    return pl.pallas_call(
        mask_kernel,
        grid=(1,),
        out_shape=outs,
        in_specs=[whole(a) for a in masks] + [HBM] * 3,
        out_specs=tuple(whole(a) for a in outs),
        scratch_shapes=[
            pltpu.VMEM((AUX, ROWS, COLS), BF16),
            pltpu.VMEM((HALF, COLS), BF16),
            pltpu.VMEM((HALF, COLS), BF16),
            pltpu.SemaphoreType.DMA((2 + AUX,)),
        ],
        compiler_params=PARAMS,
        name="mask_inputs",
    )(*masks, integrals, occ, virt)


def virt_place(offsets):
    z, col, core = lax.axis_index("row"), lax.axis_index("col"), lax.axis_index("layer")
    y, x = lax.div(col, 4), lax.rem(col, 4)
    first, second = offsets
    own_x = lax.rem(x + jnp.where(core == 0, first, second) + 4, 4)
    own_y = lax.rem(y + jnp.where(core == 0, second, first) + 4, 4)
    tile = own_y * 4 + own_x
    offset = lax.rem(lax.div(tile, 2) - z + 8, 8)
    place = jnp.where(offset < 4, 2 * offset, 2 * (8 - offset) - 1)
    return place + jnp.where(lax.rem(tile, 2) == core, 0, 8)


class PlaneSum:
    def __init__(self, arrays):
        self.groups = [PLANE[a] for a in arrays]
        self.tiles = [offsets for group in self.groups for offsets in group]
        self.sems = len(arrays) + len(self.tiles)

    def scratch(self, pieces):
        return buffers_of(pieces) + [pltpu.VMEM((len(self.tiles), HALF, COLS), BF16)]

    def start(self, virt, pieces, bufs, sems, first):
        *self.bufs, self.virt_buf = bufs
        piece_copies = start_all(pieces[:1], self.bufs[:1], sems, first)
        self.virt_copies = start_all(
            [virt.at[virt_place(t)] for t in self.tiles],
            [self.virt_buf.at[k] for k in range(len(self.tiles))],
            sems,
            first + len(pieces),
        )
        self.piece_copies = piece_copies + start_all(pieces[1:], self.bufs[1:], sems, first + 1)

    def add(self, acc, fresh):
        tile = 0
        for group, copy, buf in zip(self.groups, self.piece_copies, self.bufs):
            copy.wait()
            for k in range(0, len(group), 2):
                self.virt_copies[tile].wait()
                self.virt_copies[tile + 1].wait()
                for p in range(PAIR):
                    part = jnp.zeros((ROWS, COLS), F32)
                    for i in range(2):
                        rows = buf[pl.ds(((k + i) * PAIR + p) * ROWS, ROWS), :]
                        part += jnp.dot(rows, self.virt_buf[tile + i], preferred_element_type=F32)
                    at = pl.ds(p * ROWS, ROWS)
                    acc[at, :] = part if fresh and tile == 0 else acc[at, :] + part
                tile += 2


class RingSum:
    def __init__(self, places, spare):
        self.places, self.spare = places, spare
        self.count = len(places) + (7 in places)
        self.sems = len(places) + self.count

    def scratch(self, pieces):
        return buffers_of(pieces) + [pltpu.VMEM((2 * len(self.places), ROWS, COLS), BF16)]

    def start(self, occ, pieces, bufs, sems, first):
        *self.bufs, self.occ_buf = bufs
        z = lax.axis_index("row")
        self.occ_copies, self.piece_copies = [], []
        for k, place in enumerate(self.places):
            source = lax.rem(z + RING[place] + 8, 8)
            self.occ_copies += start_all(
                [occ.at[pl.ds(source * 2, 2)]], [self.occ_buf.at[pl.ds(k * 2, 2)]], sems, first + k
            )
            self.piece_copies += start_all([pieces[k]], [self.bufs[k]], sems, first + len(self.places) + k)
        for k in range(len(self.places), self.count):
            self.piece_copies += start_all([pieces[k]], [self.bufs[k]], sems, first + len(self.places) + k)

    def add(self, acc, fresh):
        for k, place in enumerate(self.places):
            self.occ_copies[k].wait()
            self.piece_copies[k].wait()
            if place == 7:
                self.piece_copies[k + 1].wait()
            for p in range(PAIR):
                if place < 7:
                    piece, start = self.bufs[k], p * (ROWS + self.spare)
                else:
                    piece, start = self.bufs[k + p], p * (self.spare // 2)
                part = jnp.dot(self.occ_buf[2 * k], piece[pl.ds(start, HALF), :], preferred_element_type=F32)
                part += jnp.dot(
                    self.occ_buf[2 * k + 1], piece[pl.ds(start + HALF, HALF), :], preferred_element_type=F32
                )
                at = pl.ds(p * ROWS, ROWS)
                acc[at, :] = part if fresh and k == 0 else acc[at, :] + part


def product_kernel(job, factor, *refs):
    n = (len(refs) - 3) // 2
    pieces, out, bufs, acc, sems = refs[:n], refs[n], refs[n + 1:-2], refs[-2], refs[-1]
    job.start(factor, pieces, bufs, sems, 0)
    job.add(acc, True)
    out[...] = acc[...].astype(out.dtype)


def product(name, job, factor, pieces, dtype):
    return pl.pallas_call(
        functools.partial(product_kernel, job),
        out_shape=jax.ShapeDtypeStruct((PAIR * ROWS, COLS), dtype),
        in_specs=[HBM] * (1 + len(pieces)),
        out_specs=VMEM,
        scratch_shapes=job.scratch(pieces)
        + [pltpu.VMEM((PAIR * ROWS, COLS), F32), pltpu.SemaphoreType.DMA((job.sems,))],
        compiler_params=PARAMS,
        cost_estimate=pl.CostEstimate(flops=2 << 30, bytes_accessed=9 << 20, transcendentals=0),
        name=name,
    )(factor, *pieces)


CHUNK = 32


def chi_tile(polar, aux):
    count = aux.shape[0]

    def add_rows(i, total):
        at = pl.ds(pl.multiple_of(i * CHUNK, CHUNK), CHUNK)
        left = jnp.concatenate([polar[p, at, :] for p in range(AUX)], axis=0)
        right = jnp.concatenate([aux[q, at, :] for q in range(count)], axis=0)
        return total + lax.dot_general(left, right, (((1,), (1,)), ((), ())), preferred_element_type=F32)

    shape = (AUX * CHUNK, count * CHUNK)
    total = lax.fori_loop(0, ROWS // CHUNK, add_rows, jnp.zeros(shape, F32), unroll=4)
    rows = lax.broadcasted_iota(jnp.int32, shape, 0)
    cols = lax.broadcasted_iota(jnp.int32, shape, 1)
    total = jnp.where(lax.rem(rows, CHUNK) == lax.rem(cols, CHUNK), total, 0.0)
    sums = [jnp.sum(total[p * CHUNK:(p + 1) * CHUNK], axis=0, keepdims=True) for p in range(AUX)]
    sums = jnp.concatenate(sums + [jnp.zeros((8 - AUX, shape[1]), F32)], axis=0)
    cols = lax.broadcasted_iota(jnp.int32, (8, BLK), 1)
    result = jnp.zeros((8, BLK), F32)
    for q in range(count):
        group = lax.broadcasted_iota(jnp.int32, sums.shape, 1) // CHUNK == q
        value = jnp.sum(jnp.where(group, sums, 0.0), axis=1, keepdims=True)
        result = jnp.where(cols == q, value, result)
    return result


def polar_kernel(plane_job, ring_job, virt, occ, *refs):
    n, m = 2, ring_job.count
    plane_pieces, ring_pieces, aux = refs[:n], refs[n:n + m], refs[n + m]
    plane_in, ring_in, polar, chi = refs[n + m + 1:n + m + 5]
    scratch = refs[n + m + 5:]
    plane_bufs, ring_bufs = scratch[:n + 1], scratch[n + 1:n + m + 2]
    aux_buf, plane_acc, ring_acc, sems = scratch[n + m + 2:]
    copies = start_all((plane_in, ring_in), (plane_acc, ring_acc), sems)
    ring_job.start(occ, ring_pieces, ring_bufs, sems, 3)
    plane_job.start(virt, plane_pieces, plane_bufs, sems, 3 + ring_job.sems)
    copies += start_all((aux,), (aux_buf,), sems, 2)
    copies[1].wait()
    ring_job.add(ring_acc, False)
    for p in range(PAIR):
        polar[p] = ring_acc[pl.ds(p * ROWS, ROWS), :].astype(BF16)
    copies[0].wait()
    plane_job.add(plane_acc, False)
    for p in range(PAIR):
        polar[PAIR + p] = plane_acc[pl.ds(p * ROWS, ROWS), :].astype(BF16)
    copies[2].wait()
    tile = chi_tile(polar, aux_buf)
    for i in range(chi.shape[0]):
        chi[i] = tile


def polar_product(virt, occ, plane_pieces, ring_pieces, aux, plane_acc, ring_acc):
    plane_job, ring_job = PlaneSum(PLANE_FAR), RingSum(RING_FAR, 0)
    outs = (jax.ShapeDtypeStruct((AUX, ROWS, COLS), BF16), jax.ShapeDtypeStruct((128, 8, BLK), F32))
    operands = (virt, occ, *plane_pieces, *ring_pieces, aux, plane_acc, ring_acc)
    return pl.pallas_call(
        functools.partial(polar_kernel, plane_job, ring_job),
        grid=(1,),
        out_shape=outs,
        in_specs=[HBM] * len(operands),
        out_specs=tuple(whole(a) for a in outs),
        scratch_shapes=plane_job.scratch(plane_pieces)
        + ring_job.scratch(ring_pieces)
        + buffers_of((aux, plane_acc, ring_acc))
        + [pltpu.SemaphoreType.DMA((3 + plane_job.sems + ring_job.sems,))],
        compiler_params=PARAMS,
        cost_estimate=pl.CostEstimate(flops=2 << 30, bytes_accessed=14 << 20, transcendentals=0),
        name="polar_product",
    )(*operands)


def body(integrals, density_occ, density_virt, mask_int, mask_occ, mask_virt):
    plane_aux, ring_aux, occ_half, own_aux = mask_inputs(
        mask_int, mask_occ, mask_virt, integrals, density_occ, density_virt
    )
    occ = lax.all_gather(occ_half, ("col", "layer"), axis=0, tiled=True)
    occ = occ.reshape(16, ROWS, COLS)

    plane, ring, _ = gather_both(plane_aux, ring_aux)
    own_virt = jnp.concatenate(
        [part[ROWS:ROWS + HALF] for part in ring[:7]] + [ring[7][ROWS:], ring[8][:HALF // 2]], axis=0
    ).reshape(8, HALF, COLS)
    virt = jnp.concatenate([own_virt, swap_cores(own_virt)], axis=0)
    occ_first = product("occ_first", RingSum(RING_NEAR + RING_FAR, HALF), occ, ring, BF16)
    plane, virt, occ_first = lax.optimization_barrier((plane, virt, occ_first))
    half_tensor = product("half_tensor", PlaneSum(PLANE_NEAR + PLANE_FAR), virt, plane, BF16)

    def early(plane, ring):
        return (
            product("plane_near", PlaneSum(PLANE_NEAR), virt, plane, F32),
            product("ring_near", RingSum(RING_NEAR, 0), occ, ring, F32),
        )

    aux, occ_first = lax.optimization_barrier((own_aux, occ_first))
    aux = lax.all_gather(aux, "layer", axis=0, tiled=True)
    plane, ring, (plane_acc, ring_acc) = gather_both(occ_first, half_tensor, early)
    polar, chi = polar_product(virt, occ, plane[4:], ring[5:], aux, plane_acc, ring_acc)

    shares = lax.all_to_all(chi, ("row", "col"), 0, 0)
    chi = jnp.sum(shares, axis=0)[:AUX, :2 * AUX] * (1.0 / (ROWS * lax.axis_size("row")))
    return polar, chi


def solution(mesh):
    in_specs = (
        P("layer", "row", "col"),
        P("row", "col"),
        P("row", "col"),
        P("layer", "row", "col"),
        P("row", "col"),
        P("row", "col"),
    )
    out_specs = (P("layer", "row", "col"), P("layer", None))
    return jax.shard_map(body, mesh=mesh, in_specs=in_specs, out_specs=out_specs, check_vma=False)
```

time: 717 us -> 220 us (0.31)
  blocking collectives: 344 us -> 30.1 us
  waiting for transfers between devices: 320 us -> 71.8 us
  starting transfers between devices: 0.39 us -> 49.1 us
  matrix products: 24.6 us -> 0 us
  Pallas kernels: 0 us -> 23 us
  local copies, waits for them, and re-layouts: 4.11 us -> 21.3 us
    psum x1 -> x0, blocking collectives: 344 us -> none  [body(): chi_block = lax.psum(partial_value, ('row', 'col')) * (1.0 / basis_count)]
    all_gather x5 -> x2, waiting for transfers between devices: 320 us -> 0.01 us  [the longest x1 0.01 us: body(): occ = lax.all_gather(occ_half, ('col', 'layer'), axis=0, tiled=True)]
    ppermute x0 -> x31, waiting for transfers between devices: none -> 71.8 us  [the longest x16 53.9 us: ring_move(): return lax.ppermute(value, 'row', [(i, (i + shift) % 8) for i in range(8)])]
    ppermute x0 -> x31, starting transfers between devices: none -> 49 us  [the longest x16 28.3 us: ring_move(): return lax.ppermute(value, 'row', [(i, (i + shift) % 8) for i in range(8)])]
    all_to_all x0 -> x1, blocking collectives: none -> 30.1 us  [body(): shares = lax.all_to_all(chi, ('row', 'col'), 0, 0)]
    dot_general x3 -> x0, matrix products: 24.6 us -> none  [the longest x1 11.9 us: body(): jnp.einsum('pam,mb->pab', lax.all_gather(masked_int, 'col', axis=2, tiled...]
    pallas_call x0 -> x6, Pallas kernels: none -> 23 us  [the longest x4 14.6 us: product(): pl.pallas_call(functools.partial(product_kernel, job), out_shape=jax.Shap...]
    unnamed x7 -> x90, local copies, waits for them, and re-layouts: 1.33 us -> 18.1 us
  transfers between devices with their start and end apart: 5 -> 33, of which waited for: 5 -> 15; matrix products, arithmetic and copies ran while one was open for 4% -> 6% of each run, Pallas kernels for 0% -> 5%
where the time goes in v2:
time: 220 us; the launch traced here: 219 us
  waiting for transfers between devices  71.8 us (33%)
  starting transfers between devices  49.1 us (22%)
  blocking collectives  30.1 us (14%)
  Pallas kernels  23 us (10%)
  local copies, waits for them, and re-layouts  21.3 us (10%)
  between operations  14.5 us (7%)
  other arithmetic  9.59 us (4%)
    ppermute x16, waiting for transfers between devices, ring_move(): return lax.ppermute(value, 'row', [(i, (i + shift) % 8) for i in range(8)])  53.9 us
    all_to_all x1, blocking collectives, body(): shares = lax.all_to_all(chi, ('row', 'col'), 0, 0)  30.1 us
    ppermute x16, starting transfers between devices, ring_move(): return lax.ppermute(value, 'row', [(i, (i + shift) % 8) for i in range(8)])  28.3 us
    ppermute x14, starting transfers between devices, plane_move(): return lax.ppermute(value, ('col', 'layer'), plane_perm(shift, first))  20.7 us
    unnamed x90, local copies, waits for them, and re-layouts  18.1 us
    ppermute x14, waiting for transfers between devices, plane_move(): return lax.ppermute(value, ('col', 'layer'), plane_perm(shift, first))  15.2 us
    pallas_call x4, Pallas kernels, product(): pl.pallas_call(functools.partial(product_kernel, job), out_shape=jax.Shap...  14.6 us
    pallas_call x1, Pallas kernels, polar_product(): pl.pallas_call(functools.partial(polar_kernel, plane_job, ring_job), grid...  6.18 us
  transfers between devices with their start and end apart: 33, of which 15 were waited for; matrix products, arithmetic and copies ran while one was open for 6% of the time, Pallas kernels for 5%

profile of v2, /device:TPU:2, one launch (start us, length us, event | category | flops | bytes accessed | tf_op | source)
XLA Modules:
  0.0 219.4 jit_solution(496519346782668348)
XLA Ops:
  14.7 5.9 %collective-permute-start.4 = (bf16[1280,256]{1,0:T(8,128)(2,1)S(1)}, bf16[1280,256]{1,0:T(8,128)(2,1)S(1)}, u32[]{:S(2)}, u32[]{:S(2)}) collective-permute-start(bf16[1280,256]{1,0:T(8,128)(2,1)S(1)} %get-tuple-element.41.refs_0_), channel_id=1, source_target_pairs={{0,224},{32,0},{64,32},{96,64},{128,96},{160,128},{192,160},{224,1... | collective-permute-start | bytes 1966088 | tf_op jit(solution)/shard_map/ppermute | solution.py:43
  24.8 6.6 %collective-permute-done.2 = bf16[1024,256]{1,0:T(8,128)(2,1)S(1)} collective-permute-done((bf16[1024,256]{1,0:T(8,128)(2,1)S(1)}, bf16[1024,256]{1,0:T(8,128)(2,1)S(1)}, u32[]{:S(2)}, u32[]{:S(2)}) %collective-permute-start.2) | collective-permute-done | bytes 524320 | tf_op jit(solution)/shard_map/ppermute | solution.py:39
  31.4 6.6 %collective-permute-done.1 = bf16[1024,256]{1,0:T(8,128)(2,1)S(1)} collective-permute-done((bf16[1024,256]{1,0:T(8,128)(2,1)S(1)}, bf16[1024,256]{1,0:T(8,128)(2,1)S(1)}, u32[]{:S(2)}, u32[]{:S(2)}) %collective-permute-start.1) | collective-permute-done | bytes 524320 | tf_op jit(solution)/shard_map/ppermute | solution.py:39
  43.0 3.2 %collective-permute-start.8 = (bf16[1280,256]{1,0:T(8,128)(2,1)S(1)}, bf16[1280,256]{1,0:T(8,128)(2,1)S(1)}, u32[]{:S(2)}, u32[]{:S(2)}) collective-permute-start(bf16[1280,256]{1,0:T(8,128)(2,1)S(1)} %collective-permute-done.4.refs_2_), channel_id=1, source_target_pairs={{0,224},{32,0},{64,32},{96,64},{128,96},{160,128},{192,160},{224,1... | collective-permute-start | bytes 1966088 | tf_op jit(solution)/shard_map/ppermute | solution.py:43
  46.3 11.6 %collective-permute-done.7.refs_3_ = bf16[1280,256]{1,0:T(8,128)(2,1)S(1)} collective-permute-done((bf16[1280,256]{1,0:T(8,128)(2,1)S(1)}, bf16[1280,256]{1,0:T(8,128)(2,1)S(1)}, u32[]{:S(2)}, u32[]{:S(2)}) %collective-permute-start.7) | collective-permute-done | bytes 655392 | tf_op jit(solution)/shard_map/ppermute | solution.py:43
  58.0 3.2 %collective-permute-start.12 = (bf16[1280,256]{1,0:T(8,128)(2,1)S(1)}, bf16[1280,256]{1,0:T(8,128)(2,1)S(1)}, u32[]{:S(2)}, u32[]{:S(2)}) collective-permute-start(bf16[1280,256]{1,0:T(8,128)(2,1)S(1)} %collective-permute-done.8.refs_4_), channel_id=1, source_target_pairs={{0,224},{32,0},{64,32},{96,64},{128,96},{160,128},{192,160},{224,1... | collective-permute-start | bytes 1966088 | tf_op jit(solution)/shard_map/ppermute | solution.py:43
  66.7 6.0 %collective-permute-done.11.refs_5_ = bf16[1280,256]{1,0:T(8,128)(2,1)S(1)} collective-permute-done((bf16[1280,256]{1,0:T(8,128)(2,1)S(1)}, bf16[1280,256]{1,0:T(8,128)(2,1)S(1)}, u32[]{:S(2)}, u32[]{:S(2)}) %collective-permute-start.11) | collective-permute-done | bytes 655392 | tf_op jit(solution)/shard_map/ppermute | solution.py:43
  72.9 3.5 %collective-permute-start.14 = (bf16[640,256]{1,0:T(8,128)(2,1)S(1)}, bf16[640,256]{1,0:T(8,128)(2,1)S(1)}, u32[]{:S(2)}, u32[]{:S(2)}) collective-permute-start(bf16[640,256]{1,0:T(8,128)(2,1)S(1)} %slice.60), channel_id=1, source_target_pairs={{0,224},{32,0},{64,32},{96,64},{128,96},{160,128},{192,160},{224,1... | collective-permute-start | bytes 983048 | tf_op jit(solution)/shard_map/ppermute | solution.py:43
  76.4 4.7 %collective-permute-done.13.refs_7_ = bf16[640,256]{1,0:T(8,128)(2,1)S(1)} collective-permute-done((bf16[640,256]{1,0:T(8,128)(2,1)S(1)}, bf16[640,256]{1,0:T(8,128)(2,1)S(1)}, u32[]{:S(2)}, u32[]{:S(2)}) %collective-permute-start.13) | collective-permute-done | bytes 327712 | tf_op jit(solution)/shard_map/ppermute | solution.py:43
  95.3 4.5 %occ_first.1 = bf16[1024,256]{1,0:T(8,128)(2,1)S(1)} custom-call(bf16[16,512,256]{2,1,0:T(8,128)(2,1)} %bitcast.8, bf16[1280,256]{1,0:T(8,128)(2,1)S(1)} %copy-done.12, bf16[1280,256]{1,0:T(8,128)(2,1)S(1)} %copy-done.16, bf16[1280,256]{1,0:T(8,128)(2,1)S(1)} %copy-done.14, bf16[1280,256]{1,0:T(8,128)(2,1)S(1)} %copy-done.18, ...), custom_call_target="tpu_custom_call" | custom-call | flops 2147483648 | bytes 9437184 | tf_op jit(solution)/shard_map/occ_first/pallas_call | solution.py:266
  99.9 4.1 %half_tensor.1.refs_0_ = bf16[1024,256]{1,0:T(8,128)(2,1)S(1)} custom-call(bf16[16,256,256]{2,1,0:T(8,128)(2,1)} %pad_maximum_fusion.2.factor.virt, bf16[2048,256]{1,0:T(8,128)(2,1)S(1)} %copy-done.1, bf16[2048,256]{1,0:T(8,128)(2,1)S(1)} %copy-done.3, bf16[2048,256]{1,0:T(8,128)(2,1)S(1)} %collective-permute-done.5.refs_2_, ...), custom_call_target="tpu_custom_call" | custom-call | flops 2147483648 | bytes 9437184 | tf_op jit(solution)/shard_map/half_tensor/pallas_call | solution.py:266
  111.9 6.4 %collective-permute-done.20.refs_2_ = bf16[1024,256]{1,0:T(8,128)(2,1)S(1)} collective-permute-done((bf16[1024,256]{1,0:T(8,128)(2,1)S(1)}, bf16[1024,256]{1,0:T(8,128)(2,1)S(1)}, u32[]{:S(2)}, u32[]{:S(2)}) %collective-permute-start.20) | collective-permute-done | bytes 524320 | tf_op jit(solution)/shard_map/ppermute | solution.py:43
  118.4 3.4 %collective-permute-done.19.refs_1_ = bf16[1024,256]{1,0:T(8,128)(2,1)S(1)} collective-permute-done((bf16[1024,256]{1,0:T(8,128)(2,1)S(1)}, bf16[1024,256]{1,0:T(8,128)(2,1)S(1)}, u32[]{:S(2)}, u32[]{:S(2)}) %collective-permute-start.19) | collective-permute-done | bytes 524320 | tf_op jit(solution)/shard_map/ppermute | solution.py:43
  129.2 3.2 %collective-permute-start.24 = (bf16[1024,256]{1,0:T(8,128)(2,1)}, bf16[1024,256]{1,0:T(8,128)(2,1)}, u32[]{:S(2)}, u32[]{:S(2)}) collective-permute-start(bf16[1024,256]{1,0:T(8,128)(2,1)} %copy-done.30), channel_id=1, source_target_pairs={{0,224},{32,0},{64,32},{96,64},{128,96},{160,128},{192,160},{224,1... | collective-permute-start | bytes 1572872 | tf_op jit(solution)/shard_map/ppermute | solution.py:43
  132.5 10.2 %collective-permute-done.23.refs_3_ = bf16[1024,256]{1,0:T(8,128)(2,1)} collective-permute-done((bf16[1024,256]{1,0:T(8,128)(2,1)}, bf16[1024,256]{1,0:T(8,128)(2,1)}, u32[]{:S(2)}, u32[]{:S(2)}) %collective-permute-start.23) | collective-permute-done | bytes 524320 | tf_op jit(solution)/shard_map/ppermute | solution.py:43
  142.7 2.9 %pad_maximum_fusion.4 = bf16[4096,256]{1,0:T(8,128)(2,1)} fusion(bf16[2048,256]{1,0:T(8,128)(2,1)S(1)} %collective-permute-done.22.refs_3_, bf16[1024,256]{1,0:T(8,128)(2,1)} %copy-done.38, bf16[1024,256]{1,0:T(8,128)(2,1)S(1)} %occ_first.1), kind=kLoop, calls=%fused_computation.4 | loop fusion | flops 6291456 | bytes 4194304 | tf_op jit(solution)/shard_map/concatenate | solution.py:76
  153.6 2.9 %ring_near.1.refs_8_ = f32[1024,256]{1,0:T(8,128)S(1)} custom-call(bf16[16,512,256]{2,1,0:T(8,128)(2,1)} %bitcast.9, bf16[1024,256]{1,0:T(8,128)(2,1)S(1)} %half_tensor.1.refs_0_, bf16[1024,256]{1,0:T(8,128)(2,1)S(1)} %copy-done.33, bf16[1024,256]{1,0:T(8,128)(2,1)S(1)} %copy-done.31, bf16[1024,256]{1,0:T(8,128)(2,1)} %collective-permute-done.23.refs_3_, ...), custom_call_target="tpu_custom_call" | custom-call | flops 2147483648 | bytes 9437184 | tf_op jit(solution)/shard_map/ring_near/pallas_call | solution.py:266
  156.5 3.1 %plane_near.1.refs_7_ = f32[1024,256]{1,0:T(8,128)S(1)} custom-call(bf16[16,256,256]{2,1,0:T(8,128)(2,1)} %pad_maximum_fusion.2.factor.virt, bf16[2048,256]{1,0:T(8,128)(2,1)} %constant_dynamic-update-slice_fusion.4.refs_0_, bf16[2048,256]{1,0:T(8,128)(2,1)} %constant_dynamic-update-slice_fusion.6.refs_1_, bf16[2048,256]{1,0:T(8,128)(2,1)S(1)} %copy-done.8, ...), custom_call_target="tpu_custom_call" | custom-call | flops 2147483648 | bytes 9437184 | tf_op jit(solution)/shard_map/plane_near/pallas_call | solution.py:266
  159.6 3.7 %collective-permute-done.27.refs_2_ = bf16[1024,256]{1,0:T(8,128)(2,1)S(1)} collective-permute-done((bf16[1024,256]{1,0:T(8,128)(2,1)}, bf16[1024,256]{1,0:T(8,128)(2,1)S(1)}, u32[]{:S(2)}, u32[]{:S(2)}) %collective-permute-start.27) | collective-permute-done | bytes 524320 | tf_op jit(solution)/shard_map/ppermute | solution.py:43
  164.7 3.0 %collective-permute-start.30 = (bf16[512,256]{1,0:T(8,128)(2,1)}, bf16[512,256]{1,0:T(8,128)(2,1)S(1)}, u32[]{:S(2)}, u32[]{:S(2)}) collective-permute-start(bf16[512,256]{1,0:T(8,128)(2,1)} %slice.54), channel_id=1, source_target_pairs={{0,224},{32,0},{64,32},{96,64},{128,96},{160,128},{192,160},{224,1... | collective-permute-start | bytes 786440 | tf_op jit(solution)/shard_map/ppermute | solution.py:43
  167.6 4.2 %collective-permute-done.30.refs_5_ = bf16[512,256]{1,0:T(8,128)(2,1)S(1)} collective-permute-done((bf16[512,256]{1,0:T(8,128)(2,1)}, bf16[512,256]{1,0:T(8,128)(2,1)S(1)}, u32[]{:S(2)}, u32[]{:S(2)}) %collective-permute-start.30) | collective-permute-done | bytes 262176 | tf_op jit(solution)/shard_map/ppermute | solution.py:43
  171.8 3.7 %collective-permute-done.29.refs_4_ = bf16[512,256]{1,0:T(8,128)(2,1)} collective-permute-done((bf16[512,256]{1,0:T(8,128)(2,1)}, bf16[512,256]{1,0:T(8,128)(2,1)}, u32[]{:S(2)}, u32[]{:S(2)}) %collective-permute-start.29) | collective-permute-done | bytes 262176 | tf_op jit(solution)/shard_map/ppermute | solution.py:43
  175.5 6.2 %polar_product.1 = (bf16[4,512,256]{2,1,0:T(8,128)(2,1)}, f32[128,8,128]{2,1,0:T(8,128)S(1)}) custom-call(bf16[16,256,256]{2,1,0:T(8,128)(2,1)} %pad_maximum_fusion.2.factor.virt, bf16[16,512,256]{2,1,0:T(8,128)(2,1)} %bitcast.10, bf16[4096,256]{1,0:T(8,128)(2,1)} %collective-permute-done.25.refs_0_, bf16[4096,256]{1,0:T(8,128)(2,1)} %collective-permute-done.26.refs_1_, ...), custom_call_target="tpu_custom_call" | custom-call | flops 2147483648 | bytes 14680064 | tf_op jit(solution)/shard_map/polar_product/pallas_call | solution.py:336
  181.7 30.1 %all_to_all.5 = f32[128,8,128]{2,1,0:T(8,128)S(1)} all-to-all(f32[128,8,128]{2,1,0:T(8,128)S(1)} %get-tuple-element.77), channel_id=1, replica_groups=mesh['row'=8,'col'=16,'layer'=2] {'row','col'}, dimensions={0} | all-to-all | bytes 1048576 | tf_op jit(solution)/shard_map/all_to_all | solution.py:379
  (157 shorter events, 62.0 us)
Async XLA Ops:
  7.2 79.6 %all-gather.3.cloned.1.call-start = ((), (), s32[]{:S(2)}) async-start(), calls=%async_computation.1 | async-start | bytes 4325376 | tf_op jit(solution)/shard_map/all_gather | solution.py:356
  14.7 153.0 %all-gather.5.cloned.1.call-start = ((), (), s32[]{:S(2)}) async-start(), calls=%async_computation.2 | async-start | bytes 3145728 | tf_op jit(solution)/shard_map/all_gather | solution.py:375
  14.7 23.7 %collective-permute-start.4 = (bf16[1280,256]{1,0:T(8,128)(2,1)S(1)}, bf16[1280,256]{1,0:T(8,128)(2,1)S(1)}, u32[]{:S(2)}, u32[]{:S(2)}) collective-permute-start(bf16[1280,256]{1,0:T(8,128)(2,1)S(1)} %get-tuple-element.41.refs_0_), channel_id=1, source_target_pairs={{0,224},{32,0},{64,32},{96,64},{128,96},{160,128},{192,160},{224,1... | collective-permute-start | bytes 1966088 | tf_op jit(solution)/shard_map/ppermute | solution.py:43
  20.6 17.8 %collective-permute-start.3 = (bf16[1280,256]{1,0:T(8,128)(2,1)S(1)}, bf16[1280,256]{1,0:T(8,128)(2,1)S(1)}, u32[]{:S(2)}, u32[]{:S(2)}) collective-permute-start(bf16[1280,256]{1,0:T(8,128)(2,1)S(1)} %get-tuple-element.41.refs_0_), channel_id=1, source_target_pairs={{0,32},{32,64},{64,96},{96,128},{128,160},{160,192},{192,224},{224... | collective-permute-start | bytes 1966088 | tf_op jit(solution)/shard_map/ppermute | solution.py:43
  22.8 15.2 %collective-permute-start.1 = (bf16[1024,256]{1,0:T(8,128)(2,1)S(1)}, bf16[1024,256]{1,0:T(8,128)(2,1)S(1)}, u32[]{:S(2)}, u32[]{:S(2)}) collective-permute-start(bf16[1024,256]{1,0:T(8,128)(2,1)S(1)} %get-tuple-element.40), channel_id=1, source_target_pairs={{0,6},{1,25},{2,0},{3,27},{4,2},{5,29},{6,4},{7,31},{8,14},{9,1},{... | collective-permute-start | bytes 1572872 | tf_op jit(solution)/shard_map/ppermute | solution.py:39
  24.2 14.2 %collective-permute-start = (bf16[1024,256]{1,0:T(8,128)(2,1)S(1)}, bf16[1024,256]{1,0:T(8,128)(2,1)S(1)}, u32[]{:S(2)}, u32[]{:S(2)}) collective-permute-start(bf16[1024,256]{1,0:T(8,128)(2,1)S(1)} %get-tuple-element.40), channel_id=1, source_target_pairs={{0,2},{1,9},{2,4},{3,11},{4,6},{5,13},{6,0},{7,15},{8,10},{9,17},{... | collective-permute-start | bytes 1572872 | tf_op jit(solution)/shard_map/ppermute | solution.py:39
  38.5 19.3 %collective-permute-start.5 = (bf16[2048,256]{1,0:T(8,128)(2,1)S(1)}, bf16[2048,256]{1,0:T(8,128)(2,1)S(1)}, u32[]{:S(2)}, u32[]{:S(2)}) collective-permute-start(bf16[2048,256]{1,0:T(8,128)(2,1)S(1)} %constant_dynamic-update-slice_fusion.refs_0_), channel_id=1, source_target_pairs={{0,8},{1,3},{2,10},{3,5},{4,12},{5,7},{6,14},{7,1},{8,16},{9,11},{... | collective-permute-start | bytes 3145736 | tf_op jit(solution)/shard_map/ppermute | solution.py:39
  40.3 17.5 %collective-permute-start.6 = (bf16[2048,256]{1,0:T(8,128)(2,1)S(1)}, bf16[2048,256]{1,0:T(8,128)(2,1)S(1)}, u32[]{:S(2)}, u32[]{:S(2)}) collective-permute-start(bf16[2048,256]{1,0:T(8,128)(2,1)S(1)} %constant_dynamic-update-slice_fusion.2.refs_1_), channel_id=1, source_target_pairs={{0,24},{1,7},{2,26},{3,1},{4,28},{5,3},{6,30},{7,5},{8,0},{9,15},{... | collective-permute-start | bytes 3145736 | tf_op jit(solution)/shard_map/ppermute | solution.py:39
  43.0 14.9 %collective-permute-start.7 = (bf16[1280,256]{1,0:T(8,128)(2,1)S(1)}, bf16[1280,256]{1,0:T(8,128)(2,1)S(1)}, u32[]{:S(2)}, u32[]{:S(2)}) collective-permute-start(bf16[1280,256]{1,0:T(8,128)(2,1)S(1)} %collective-permute-done.3.refs_1_), channel_id=1, source_target_pairs={{0,32},{32,64},{64,96},{96,128},{128,160},{160,192},{192,224},{224... | collective-permute-start | bytes 1966088 | tf_op jit(solution)/shard_map/ppermute | solution.py:43
  43.0 14.9 %collective-permute-start.8 = (bf16[1280,256]{1,0:T(8,128)(2,1)S(1)}, bf16[1280,256]{1,0:T(8,128)(2,1)S(1)}, u32[]{:S(2)}, u32[]{:S(2)}) collective-permute-start(bf16[1280,256]{1,0:T(8,128)(2,1)S(1)} %collective-permute-done.4.refs_2_), channel_id=1, source_target_pairs={{0,224},{32,0},{64,32},{96,64},{128,96},{160,128},{192,160},{224,1... | collective-permute-start | bytes 1966088 | tf_op jit(solution)/shard_map/ppermute | solution.py:43
  57.9 14.9 %collective-permute-start.11 = (bf16[1280,256]{1,0:T(8,128)(2,1)S(1)}, bf16[1280,256]{1,0:T(8,128)(2,1)S(1)}, u32[]{:S(2)}, u32[]{:S(2)}) collective-permute-start(bf16[1280,256]{1,0:T(8,128)(2,1)S(1)} %collective-permute-done.7.refs_3_), channel_id=1, source_target_pairs={{0,32},{32,64},{64,96},{96,128},{128,160},{160,192},{192,224},{224... | collective-permute-start | bytes 1966088 | tf_op jit(solution)/shard_map/ppermute | solution.py:43
  58.0 14.9 %collective-permute-start.12 = (bf16[1280,256]{1,0:T(8,128)(2,1)S(1)}, bf16[1280,256]{1,0:T(8,128)(2,1)S(1)}, u32[]{:S(2)}, u32[]{:S(2)}) collective-permute-start(bf16[1280,256]{1,0:T(8,128)(2,1)S(1)} %collective-permute-done.8.refs_4_), channel_id=1, source_target_pairs={{0,224},{32,0},{64,32},{96,64},{128,96},{160,128},{192,160},{224,1... | collective-permute-start | bytes 1966088 | tf_op jit(solution)/shard_map/ppermute | solution.py:43
  64.2 35.7 %collective-permute-start.10 = (bf16[4096,256]{1,0:T(8,128)(2,1)}, bf16[4096,256]{1,0:T(8,128)(2,1)}, u32[]{:S(2)}, u32[]{:S(2)}) collective-permute-start(bf16[4096,256]{1,0:T(8,128)(2,1)} %pad_maximum_fusion.1), channel_id=1, source_target_pairs={{0,24},{1,7},{2,26},{3,1},{4,28},{5,3},{6,30},{7,5},{8,0},{9,15},{... | collective-permute-start | bytes 6291464 | tf_op jit(solution)/shard_map/ppermute | solution.py:39
  66.6 33.2 %collective-permute-start.9 = (bf16[4096,256]{1,0:T(8,128)(2,1)}, bf16[4096,256]{1,0:T(8,128)(2,1)}, u32[]{:S(2)}, u32[]{:S(2)}) collective-permute-start(bf16[4096,256]{1,0:T(8,128)(2,1)} %pad_maximum_fusion), channel_id=1, source_target_pairs={{0,8},{1,3},{2,10},{3,5},{4,12},{5,7},{6,14},{7,1},{8,16},{9,11},{... | collective-permute-start | bytes 6291464 | tf_op jit(solution)/shard_map/ppermute | solution.py:39
  104.0 14.3 %collective-permute-start.20 = (bf16[1024,256]{1,0:T(8,128)(2,1)S(1)}, bf16[1024,256]{1,0:T(8,128)(2,1)S(1)}, u32[]{:S(2)}, u32[]{:S(2)}) collective-permute-start(bf16[1024,256]{1,0:T(8,128)(2,1)S(1)} %half_tensor.1.refs_0_), channel_id=1, source_target_pairs={{0,224},{32,0},{64,32},{96,64},{128,96},{160,128},{192,160},{224,1... | collective-permute-start | bytes 1572872 | tf_op jit(solution)/shard_map/ppermute | solution.py:43
  106.9 14.9 %collective-permute-start.19 = (bf16[1024,256]{1,0:T(8,128)(2,1)S(1)}, bf16[1024,256]{1,0:T(8,128)(2,1)S(1)}, u32[]{:S(2)}, u32[]{:S(2)}) collective-permute-start(bf16[1024,256]{1,0:T(8,128)(2,1)S(1)} %half_tensor.1.refs_0_), channel_id=1, source_target_pairs={{0,32},{32,64},{64,96},{96,128},{128,160},{160,192},{192,224},{224... | collective-permute-start | bytes 1572872 | tf_op jit(solution)/shard_map/ppermute | solution.py:43
  106.9 14.9 %collective-permute-start.18 = (bf16[1024,256]{1,0:T(8,128)(2,1)S(1)}, bf16[1024,256]{1,0:T(8,128)(2,1)S(1)}, u32[]{:S(2)}, u32[]{:S(2)}) collective-permute-start(bf16[1024,256]{1,0:T(8,128)(2,1)S(1)} %occ_first.1), channel_id=1, source_target_pairs={{0,4},{1,17},{2,6},{3,19},{4,0},{5,21},{6,2},{7,23},{8,12},{9,25},... | collective-permute-start | bytes 1572872 | tf_op jit(solution)/shard_map/ppermute | solution.py:39
  109.1 14.1 %collective-permute-start.17 = (bf16[1024,256]{1,0:T(8,128)(2,1)S(1)}, bf16[1024,256]{1,0:T(8,128)(2,1)S(1)}, u32[]{:S(2)}, u32[]{:S(2)}) collective-permute-start(bf16[1024,256]{1,0:T(8,128)(2,1)S(1)} %occ_first.1), channel_id=1, source_target_pairs={{0,6},{1,25},{2,0},{3,27},{4,2},{5,29},{6,4},{7,31},{8,14},{9,1},{... | collective-permute-start | bytes 1572872 | tf_op jit(solution)/shard_map/ppermute | solution.py:39
  125.1 17.6 %collective-permute-start.21 = (bf16[2048,256]{1,0:T(8,128)(2,1)}, bf16[2048,256]{1,0:T(8,128)(2,1)S(1)}, u32[]{:S(2)}, u32[]{:S(2)}) collective-permute-start(bf16[2048,256]{1,0:T(8,128)(2,1)} %constant_dynamic-update-slice_fusion.4.refs_0_), channel_id=1, source_target_pairs={{0,8},{1,3},{2,10},{3,5},{4,12},{5,7},{6,14},{7,1},{8,16},{9,11},{... | collective-permute-start | bytes 3145736 | tf_op jit(solution)/shard_map/ppermute | solution.py:39
  127.1 15.6 %collective-permute-start.22 = (bf16[2048,256]{1,0:T(8,128)(2,1)}, bf16[2048,256]{1,0:T(8,128)(2,1)S(1)}, u32[]{:S(2)}, u32[]{:S(2)}) collective-permute-start(bf16[2048,256]{1,0:T(8,128)(2,1)} %constant_dynamic-update-slice_fusion.6.refs_1_), channel_id=1, source_target_pairs={{0,24},{1,7},{2,26},{3,1},{4,28},{5,3},{6,30},{7,5},{8,0},{9,15},{... | collective-permute-start | bytes 3145736 | tf_op jit(solution)/shard_map/ppermute | solution.py:39
  129.2 13.5 %collective-permute-start.23 = (bf16[1024,256]{1,0:T(8,128)(2,1)}, bf16[1024,256]{1,0:T(8,128)(2,1)}, u32[]{:S(2)}, u32[]{:S(2)}) collective-permute-start(bf16[1024,256]{1,0:T(8,128)(2,1)} %copy-done.32), channel_id=1, source_target_pairs={{0,32},{32,64},{64,96},{96,128},{128,160},{160,192},{192,224},{224... | collective-permute-start | bytes 1572872 | tf_op jit(solution)/shard_map/ppermute | solution.py:43
  129.2 13.5 %collective-permute-start.24 = (bf16[1024,256]{1,0:T(8,128)(2,1)}, bf16[1024,256]{1,0:T(8,128)(2,1)}, u32[]{:S(2)}, u32[]{:S(2)}) collective-permute-start(bf16[1024,256]{1,0:T(8,128)(2,1)} %copy-done.30), channel_id=1, source_target_pairs={{0,224},{32,0},{64,32},{96,64},{128,96},{160,128},{192,160},{224,1... | collective-permute-start | bytes 1572872 | tf_op jit(solution)/shard_map/ppermute | solution.py:43
  147.1 28.4 %collective-permute-start.25 = (bf16[4096,256]{1,0:T(8,128)(2,1)}, bf16[4096,256]{1,0:T(8,128)(2,1)}, u32[]{:S(2)}, u32[]{:S(2)}) collective-permute-start(bf16[4096,256]{1,0:T(8,128)(2,1)} %pad_maximum_fusion.3), channel_id=1, source_target_pairs={{0,8},{1,3},{2,10},{3,5},{4,12},{5,7},{6,14},{7,1},{8,16},{9,11},{... | collective-permute-start | bytes 6291464 | tf_op jit(solution)/shard_map/ppermute | solution.py:39
  148.9 26.7 %collective-permute-start.26 = (bf16[4096,256]{1,0:T(8,128)(2,1)}, bf16[4096,256]{1,0:T(8,128)(2,1)}, u32[]{:S(2)}, u32[]{:S(2)}) collective-permute-start(bf16[4096,256]{1,0:T(8,128)(2,1)} %pad_maximum_fusion.4), channel_id=1, source_target_pairs={{0,24},{1,7},{2,26},{3,1},{4,28},{5,3},{6,30},{7,5},{8,0},{9,15},{... | collective-permute-start | bytes 6291464 | tf_op jit(solution)/shard_map/ppermute | solution.py:39
  (48 other events, 306.5 us)
Sparse Core Ops, SparseCore 0:
  14.8 54.7 all-gather.2
  132.6 12.5 all-gather.4

commit v3 on v0

v3 whole, which is shorter than its diff:
```python
import functools

import jax
import jax.numpy as jnp
from jax import lax
from jax.experimental import pallas as pl
from jax.experimental.pallas import tpu as pltpu
from jax.sharding import PartitionSpec as P

BLK = 128
ROWS = 512
COLS = 256
HALF = 256
PAIR = 2
AUX = 2 * PAIR
STRIDE = PAIR * ROWS + HALF
F32 = jnp.float32
BF16 = jnp.bfloat16
HBM = pl.BlockSpec(memory_space=pltpu.HBM)
PARAMS = pltpu.CompilerParams(vmem_limit_bytes=60 * 1024 * 1024)


def plane_index(y, x, core):
    return ((y % 4) * 4 + x % 4) * 2 + core


def plane_perm(shift, first):
    pairs = []
    for y in range(4):
        for x in range(4):
            for core in range(2):
                along_x = (core == 0) == first
                to = (y, x + shift) if along_x else (y + shift, x)
                pairs.append((plane_index(y, x, core), plane_index(*to, core)))
    return pairs


def plane_move(value, shift, first):
    return lax.ppermute(value, ("col", "layer"), plane_perm(shift, first))


def swap_cores(value):
    return lax.ppermute(value, "layer", [(0, 1), (1, 0)])


PLANE = (
    ((0, 0), (-1, 0)),
    ((1, 0), (2, 0)),
    ((0, -1), (-1, -1)),
    ((0, 1), (-1, 1)),
    ((1, -1), (2, -1)),
    ((1, 1), (2, 1)),
    ((0, 2), (-1, 2)),
    ((1, 2), (2, 2)),
)


def gather_plane(plane):
    rows = plane.shape[0]
    half = rows // 2
    before, behind = plane_move(plane, 1, True), plane_move(plane, -1, True)
    low, high = plane_move(before[:half], 1, True), plane_move(behind[half:], -1, True)
    top, = pack((plane, before), ((0, 0, rows, 0, 0), (1, 0, rows, 0, rows)), (2 * rows,))
    top_before, top_behind = plane_move(top, 1, False), plane_move(top, -1, False)
    bottom, = pack(
        (behind, low, high),
        ((0, 0, rows, 0, 0), (1, 0, half, 0, rows), (2, 0, half, 0, rows + half)),
        (2 * rows,),
    )
    bottom_before, bottom_behind = plane_move(bottom, 1, False), plane_move(bottom, -1, False)
    top_before, top_behind, bottom_before, bottom_behind = lax.optimization_barrier(
        (top_before, top_behind, bottom_before, bottom_behind)
    )
    top_far, bottom_far = plane_move(top_before, 1, False), plane_move(bottom_behind, -1, False)
    return top, bottom, top_before, top_behind, bottom_before, bottom_behind, top_far, bottom_far


def buffers_of(arrays):
    return [pltpu.VMEM(a.shape, a.dtype) for a in arrays]


def start_all(sources, buffers, sems, first=0):
    copies = [pltpu.make_async_copy(a, b, sems.at[first + i]) for i, (a, b) in enumerate(zip(sources, buffers))]
    for copy in copies:
        copy.start()
    return copies


def pack_kernel(moves, count, *refs):
    sources, outs, buf, sems = refs[:count], refs[count:-2], refs[-2], refs[-1]
    loads, stores, at = [], [], 0
    for k, (i, start, rows, o, to) in enumerate(moves):
        part = buf.at[pl.ds(at, rows)]
        loads.append(pltpu.make_async_copy(sources[i].at[pl.ds(start, rows)], part, sems.at[0, k]))
        stores.append(pltpu.make_async_copy(part, outs[o].at[pl.ds(to, rows)], sems.at[1, k]))
        at += rows
    for load in loads:
        load.start()
    for load, store in zip(loads, stores):
        load.wait()
        store.start()
    for store in stores:
        store.wait()


def pack(sources, moves, out_rows):
    return pl.pallas_call(
        functools.partial(pack_kernel, moves, len(sources)),
        out_shape=tuple(jax.ShapeDtypeStruct((rows, COLS), BF16) for rows in out_rows),
        in_specs=[HBM] * len(sources),
        out_specs=(HBM,) * len(out_rows),
        scratch_shapes=[
            pltpu.VMEM((sum(move[2] for move in moves), COLS), BF16),
            pltpu.SemaphoreType.DMA((2, len(moves))),
        ],
        compiler_params=PARAMS,
        cost_estimate=pl.CostEstimate(flops=0, bytes_accessed=4 << 20, transcendentals=0),
        name="pack",
    )(*sources)


def mask_kernel(mask_int, mask_occ, mask_virt, integrals, occ, virt, plane, ring, aux,
                int_buf, occ_buf, virt_buf, int_weight, occ_weight, virt_weight, load, store):
    core = lax.axis_index("layer")
    half = pl.ds(pl.multiple_of(core * HALF, HALF), HALF)
    weights = start_all((mask_int, mask_occ, mask_virt), (int_weight, occ_weight, virt_weight), load)
    loads = start_all([integrals.at[p] for p in range(AUX)], [int_buf.at[p] for p in range(AUX)], load, 3)
    loads += start_all([virt.at[half], occ.at[half]], [virt_buf, occ_buf], load, 3 + AUX)

    def mask(ref, weight, block_rows):
        for i in range(block_rows):
            for j in range(COLS // BLK):
                at = pl.ds(i * BLK, BLK), pl.ds(j * BLK, BLK)
                block = ref[at].astype(F32)
                ref[at] = (block * jnp.broadcast_to(weight(i, j).astype(F32), block.shape)).astype(BF16)

    def half_weight(ref):
        def weight(i, j):
            low, high = ref[pl.ds(j, 1), pl.ds(i, 1)], ref[pl.ds(j, 1), pl.ds(HALF // BLK + i, 1)]
            return jnp.where(core == 0, low, high)

        return weight

    for copy in weights:
        copy.wait()
    stores = []
    for p in range(AUX):
        loads[p].wait()
        mask(int_buf.at[p], lambda i, j: int_weight[p, pl.ds(j, 1), pl.ds(i, 1)], ROWS // BLK)
        if p < PAIR:
            to = plane.at[pl.ds(p * ROWS, ROWS)]
        else:
            to = ring.at[pl.ds((p - PAIR) * (ROWS + HALF), ROWS)]
        stores += start_all([int_buf.at[p], int_buf.at[p]], [to, aux.at[p]], store, 2 * p)
    loads[AUX].wait()
    mask(virt_buf, half_weight(virt_weight), HALF // BLK)
    stores += start_all([virt_buf], [ring.at[pl.ds(ROWS, HALF)]], store, 2 * AUX)
    loads[AUX + 1].wait()
    mask(occ_buf, half_weight(occ_weight), HALF // BLK)
    stores += start_all([occ_buf], [plane.at[pl.ds(PAIR * ROWS, HALF)]], store, 2 * AUX + 1)
    for copy in stores:
        copy.wait()


def mask_inputs(mask_int, mask_occ, mask_virt, integrals, occ, virt):
    outs = (
        jax.ShapeDtypeStruct((STRIDE, COLS), BF16),
        jax.ShapeDtypeStruct((STRIDE, COLS), BF16),
        jax.ShapeDtypeStruct((AUX, ROWS, COLS), BF16),
    )
    masks = (mask_int.transpose(0, 2, 1), mask_occ.T, mask_virt.T)
    return pl.pallas_call(
        mask_kernel,
        out_shape=outs,
        in_specs=[HBM] * 6,
        out_specs=(HBM,) * 3,
        scratch_shapes=[pltpu.VMEM((AUX, ROWS, COLS), BF16)]
        + [pltpu.VMEM((HALF, COLS), BF16)] * 2
        + [pltpu.VMEM(a.shape, a.dtype) for a in masks]
        + [pltpu.SemaphoreType.DMA((5 + AUX,)), pltpu.SemaphoreType.DMA((2 + 2 * AUX,))],
        compiler_params=PARAMS,
        name="mask_inputs",
    )(*masks, integrals, occ, virt)


def tile_index(offsets):
    col, core = lax.axis_index("col"), lax.axis_index("layer")
    y, x = lax.div(col, 4), lax.rem(col, 4)
    first, second = offsets
    tile_x = lax.rem(x + jnp.where(core == 0, first, second) + 4, 4)
    tile_y = lax.rem(y + jnp.where(core == 0, second, first) + 4, 4)
    return tile_y * 4 + tile_x


def call(kernel, name, operands, outs, scratch, sems, flops):
    return pl.pallas_call(
        kernel,
        out_shape=outs,
        in_specs=[HBM] * len(operands),
        out_specs=jax.tree.map(lambda _: HBM, outs),
        scratch_shapes=scratch + [pltpu.SemaphoreType.DMA((sems,))],
        compiler_params=PARAMS,
        cost_estimate=pl.CostEstimate(flops=flops, bytes_accessed=9 << 20, transcendentals=0),
        name=name,
    )(*operands)


SUM = (PAIR * ROWS, COLS)
TILE = (HALF, COLS)


def occ_kernel(*refs):
    n = len(PLANE)
    pieces, out, buf, sems = refs[:n], refs[n], refs[n + 1], refs[n + 2]
    loads, stores = [], []
    for a, tiles in enumerate(PLANE):
        for k, offsets in enumerate(tiles):
            i = 2 * a + k
            source = pieces[a].at[pl.ds(k * STRIDE + PAIR * ROWS, HALF)]
            to = out.at[pl.ds(pl.multiple_of(tile_index(offsets) * HALF, HALF), HALF)]
            loads.append(pltpu.make_async_copy(source, buf.at[i], sems.at[i]))
            stores.append(pltpu.make_async_copy(buf.at[i], to, sems.at[2 * n + i]))
    for load in loads:
        load.start()
    for load, store in zip(loads, stores):
        load.wait()
        store.start()
    for store in stores:
        store.wait()


def occ_tiles(pieces):
    return call(
        occ_kernel, "occ_tiles", pieces, jax.ShapeDtypeStruct((16 * HALF, COLS), BF16),
        [pltpu.VMEM((16, *TILE), BF16)], 32, 0,
    )


def start_plane(arrays, rows, gathered, pieces, bufs, virt_buf, sems, first):
    copies, virt_copies = [], []
    for k, a in enumerate(arrays):
        for i, offsets in enumerate(PLANE[a]):
            sem = first + 4 * k + 2 * i
            source = pieces[k].at[pl.ds(i * rows, PAIR * ROWS)]
            copies += start_all([source], [bufs.at[2 * k + i]], sems, sem)
            start = pl.multiple_of(tile_index(offsets) * STRIDE + ROWS, HALF)
            virt_copies += start_all([gathered.at[pl.ds(start, HALF)]], [virt_buf.at[2 * k + i]], sems, sem + 1)
    return copies, virt_copies


def plane_add(copies, bufs, virt_copies, virt, acc, fresh):
    for k in range(0, len(copies), 2):
        for copy in copies[k:k + 2] + virt_copies[k:k + 2]:
            copy.wait()
        for p in range(PAIR):
            at = pl.ds(p * ROWS, ROWS)
            part = jnp.dot(bufs[k, at, :], virt[k], preferred_element_type=F32)
            part += jnp.dot(bufs[k + 1, at, :], virt[k + 1], preferred_element_type=F32)
            acc[at, :] = part if fresh and k == 0 else acc[at, :] + part


def plane_kernel(arrays, rows, gathered, *refs):
    n = len(arrays)
    pieces, out, (bufs, virt_buf, acc, out_buf, sems) = refs[:n], refs[n], refs[n + 1:]
    copies, virt_copies = start_plane(arrays, rows, gathered, pieces, bufs, virt_buf, sems, 0)
    plane_add(copies, bufs, virt_copies, virt_buf, acc, True)
    out_buf[...] = acc[...].astype(out_buf.dtype)
    pltpu.sync_copy(out_buf, out)


def plane_product(name, arrays, rows, gathered, pieces, dtype):
    n = len(arrays)
    scratch = [pltpu.VMEM((2 * n, *SUM), BF16), pltpu.VMEM((2 * n, *TILE), BF16), pltpu.VMEM(SUM, F32), pltpu.VMEM(SUM, dtype)]
    return call(
        functools.partial(plane_kernel, arrays, rows), name, (gathered, *pieces),
        jax.ShapeDtypeStruct(SUM, dtype), scratch, 4 * n, 2 << 30,
    )


def ring_kernel(stride, gap, per_chip, own, other, gathered, out, piece_buf, occ_buf, acc, out_buf, sems):
    core = lax.axis_index("layer")
    own_rows = pl.ds(pl.multiple_of(core * HALF, HALF), HALF)
    other_rows = pl.ds(pl.multiple_of((1 - core) * HALF, HALF), HALF)
    copies = []
    for z in range(8):
        group = []
        for i in range(2):
            tile = pl.ds((2 * z + i) * HALF, HALF)
            k = 2 * z + i
            group += start_all(
                [own.at[tile], other.at[tile]], [occ_buf.at[k, own_rows], occ_buf.at[k, other_rows]], sems, 6 * z + 2 * i
            )
        block = (2 * z + core if per_chip else z) * stride
        for p in range(PAIR):
            start = pl.multiple_of(block + p * (ROWS + gap), HALF)
            group += start_all([gathered.at[pl.ds(start, ROWS)]], [piece_buf.at[z, p]], sems, 6 * z + 4 + p)
        copies.append(group)
    for z in range(8):
        for copy in copies[z]:
            copy.wait()
        for p in range(PAIR):
            part = jnp.dot(occ_buf[2 * z], piece_buf[z, p, pl.ds(0, HALF), :], preferred_element_type=F32)
            part += jnp.dot(occ_buf[2 * z + 1], piece_buf[z, p, pl.ds(HALF, HALF), :], preferred_element_type=F32)
            at = pl.ds(p * ROWS, ROWS)
            acc[at, :] = part if z == 0 else acc[at, :] + part
    out_buf[...] = acc[...].astype(BF16)
    pltpu.sync_copy(out_buf, out)


def ring_product(name, own, other, gathered, stride, gap, per_chip):
    scratch = [
        pltpu.VMEM((8, PAIR, ROWS, COLS), BF16), pltpu.VMEM((16, ROWS, COLS), BF16),
        pltpu.VMEM(SUM, F32), pltpu.VMEM(SUM, BF16),
    ]
    return call(
        functools.partial(ring_kernel, stride, gap, per_chip), name, (own, other, gathered),
        jax.ShapeDtypeStruct(SUM, BF16), scratch, 48, 2 << 30,
    )


CHUNK = 32


def chi_tile(polar, aux):
    count = aux.shape[0]

    def add_rows(i, total):
        at = pl.ds(pl.multiple_of(i * CHUNK, CHUNK), CHUNK)
        left = [polar[pl.ds(pl.multiple_of(p * ROWS + i * CHUNK, CHUNK), CHUNK), :] for p in range(AUX)]
        left = jnp.concatenate(left, axis=0)
        right = jnp.concatenate([aux[q, at, :] for q in range(count)], axis=0)
        return total + lax.dot_general(left, right, (((1,), (1,)), ((), ())), preferred_element_type=F32)

    shape = (AUX * CHUNK, count * CHUNK)
    total = lax.fori_loop(0, ROWS // CHUNK, add_rows, jnp.zeros(shape, F32), unroll=4)
    rows = lax.broadcasted_iota(jnp.int32, shape, 0)
    cols = lax.broadcasted_iota(jnp.int32, shape, 1)
    total = jnp.where(lax.rem(rows, CHUNK) == lax.rem(cols, CHUNK), total, 0.0)
    sums = [jnp.sum(total[p * CHUNK:(p + 1) * CHUNK], axis=0, keepdims=True) for p in range(AUX)]
    sums = jnp.concatenate(sums + [jnp.zeros((8 - AUX, shape[1]), F32)], axis=0)
    group = lax.broadcasted_iota(jnp.int32, sums.shape, 1) // CHUNK
    rows = lax.broadcasted_iota(jnp.int32, (8, BLK), 0)
    cols = lax.broadcasted_iota(jnp.int32, (8, BLK), 1)
    result = jnp.zeros((8, BLK), F32)
    for q in range(count):
        value = jnp.sum(jnp.where(group == q, sums, 0.0), axis=1, keepdims=True)
        result = jnp.where(cols == rows * count + q, value, result)
    return jnp.sum(result, axis=0, keepdims=True)


def polar_kernel(gathered, top, bottom, plane_sum, ring_part, own_aux, other_aux, polar, chi,
                 bufs, virt_buf, acc, aux_buf, polar_buf, chi_buf, sems):
    core = lax.axis_index("layer")
    own, other = pl.ds(core * AUX, AUX), pl.ds((1 - core) * AUX, AUX)
    sum_copy, = start_all((plane_sum,), (acc,), sems)
    copies, virt_copies = start_plane((6, 7), PAIR * ROWS, gathered, (top, bottom), bufs, virt_buf, sems, 4)
    part_copies = start_all(
        (ring_part, own_aux, other_aux),
        (polar_buf.at[pl.ds(0, PAIR * ROWS)], aux_buf.at[own], aux_buf.at[other]), sems, 1
    )
    sum_copy.wait()
    plane_add(copies, bufs, virt_copies, virt_buf, acc, False)
    polar_buf[pl.ds(PAIR * ROWS, PAIR * ROWS), :] = acc[...].astype(BF16)
    for copy in part_copies:
        copy.wait()
    polar_copy, = start_all((polar_buf,), (polar,), sems)
    chi_buf[...] = jnp.broadcast_to(chi_tile(polar_buf, aux_buf), chi_buf.shape)
    pltpu.sync_copy(chi_buf, chi)
    polar_copy.wait()


def polar_product(gathered, pieces, plane_sum, ring_part, own_aux, other_aux):
    outs = (jax.ShapeDtypeStruct((AUX * ROWS, COLS), BF16), jax.ShapeDtypeStruct((128, BLK), F32))
    scratch = [pltpu.VMEM((4, *SUM), BF16), pltpu.VMEM((4, *TILE), BF16), pltpu.VMEM(SUM, F32)]
    scratch += [pltpu.VMEM((2 * AUX, ROWS, COLS), BF16)] + buffers_of(outs)
    operands = (gathered, *pieces, plane_sum, ring_part, own_aux, other_aux)
    return call(polar_kernel, "polar_product", operands, outs, scratch, 12, 1 << 29)


def body(integrals, density_occ, density_virt, mask_int, mask_occ, mask_virt):
    plane_aux, ring_aux, own_aux = mask_inputs(
        mask_int, mask_occ, mask_virt, integrals, density_occ, density_virt
    )
    gathered = lax.all_gather(ring_aux, ("row", "layer"), axis=0, tiled=True)
    plane = gather_plane(plane_aux)
    own_occ = occ_tiles(plane)
    other_occ = swap_cores(own_occ)
    half_tensor = plane_product("half_tensor", tuple(range(8)), STRIDE, gathered, plane, BF16)
    own_occ, other_occ, half_tensor = lax.optimization_barrier((own_occ, other_occ, half_tensor))
    occ_first = ring_product("occ_first", own_occ, other_occ, gathered, STRIDE, HALF, True)

    ring = lax.all_gather(half_tensor, "row", axis=0, tiled=True)
    own_aux, occ_first = lax.optimization_barrier((own_aux, occ_first))
    other_aux = swap_cores(own_aux)
    plane = gather_plane(occ_first)
    plane_sum = plane_product("plane_near", tuple(range(6)), PAIR * ROWS, gathered, plane[:6], F32)
    ring_part = ring_product("polar_ring", own_occ, other_occ, ring, PAIR * ROWS, 0, False)
    polar, chi = polar_product(gathered, plane[6:], plane_sum, ring_part, own_aux, other_aux)

    shares = lax.all_to_all(chi.reshape(128, 1, BLK), ("row", "col"), 0, 0)
    chi = jnp.sum(shares.reshape(128, BLK), axis=0) * (1.0 / (ROWS * lax.axis_size("row")))
    return polar.reshape(AUX, ROWS, COLS), chi[:2 * AUX * AUX].reshape(AUX, 2 * AUX)


def solution(mesh):
    in_specs = (
        P("layer", "row", "col"),
        P("row", "col"),
        P("row", "col"),
        P("layer", "row", "col"),
        P("row", "col"),
        P("row", "col"),
    )
    out_specs = (P("layer", "row", "col"), P("layer", None))
    return jax.shard_map(body, mesh=mesh, in_specs=in_specs, out_specs=out_specs, check_vma=False)
```

time: 717 us -> 203 us (0.28)
  blocking collectives: 344 us -> 29.9 us
  waiting for transfers between devices: 320 us -> 82.8 us
  Pallas kernels: 0 us -> 40.1 us
  starting transfers between devices: 0.39 us -> 29.2 us
  matrix products: 24.6 us -> 0 us
    psum x1 -> x0, blocking collectives: 344 us -> none  [body(): chi_block = lax.psum(partial_value, ('row', 'col')) * (1.0 / basis_count)]
    all_gather x5 -> x2, waiting for transfers between devices: 320 us -> 0.04 us  [the longest x1 0.02 us: body(): ring = lax.all_gather(half_tensor, 'row', axis=0, tiled=True)]
    ppermute x0 -> x22, waiting for transfers between devices: none -> 82.8 us  [the longest x20 82.8 us: plane_move(): return lax.ppermute(value, ('col', 'layer'), plane_perm(shift, first))]
    pallas_call x0 -> x11, Pallas kernels: none -> 40.1 us  [the longest x6 28.9 us: call(): pl.pallas_call(kernel, out_shape=outs, in_specs=[HBM] * len(operands), ou...]
    all_to_all x0 -> x1, blocking collectives: none -> 29.9 us  [body(): shares = lax.all_to_all(chi.reshape(128, 1, BLK), ('row', 'col'), 0, 0)]
    ppermute x0 -> x22, starting transfers between devices: none -> 29.2 us  [the longest x20 28.9 us: plane_move(): return lax.ppermute(value, ('col', 'layer'), plane_perm(shift, first))]
    dot_general x3 -> x0, matrix products: 24.6 us -> none  [the longest x1 11.9 us: body(): jnp.einsum('pam,mb->pab', lax.all_gather(masked_int, 'col', axis=2, tiled...]
  transfers between devices with their start and end apart: 5 -> 24, of which waited for: 5 -> 15; matrix products, arithmetic and copies ran while one was open for 4% -> 1% of each run, Pallas kernels for 0% -> 16%
where the time goes in v3:
time: 203 us
  waiting for transfers between devices  82.8 us (41%)
  Pallas kernels  40.1 us (20%)
  blocking collectives  29.9 us (15%)
  starting transfers between devices  29.2 us (14%)
  between operations  14.3 us (7%)
  local copies, waits for them, and re-layouts  6.51 us (3%)
    ppermute x20, waiting for transfers between devices, plane_move(): return lax.ppermute(value, ('col', 'layer'), plane_perm(shift, first))  82.8 us
    all_to_all x1, blocking collectives, body(): shares = lax.all_to_all(chi.reshape(128, 1, BLK), ('row', 'col'), 0, 0)  29.9 us
    ppermute x20, starting transfers between devices, plane_move(): return lax.ppermute(value, ('col', 'layer'), plane_perm(shift, first))  28.9 us
    pallas_call x6, Pallas kernels, call(): pl.pallas_call(kernel, out_shape=outs, in_specs=[HBM] * len(operands), ou...  28.9 us
    pallas_call x4, Pallas kernels, pack(): pl.pallas_call(functools.partial(pack_kernel, moves, len(sources)), out_s...  8.5 us
  transfers between devices with their start and end apart: 24, of which 15 were waited for; matrix products, arithmetic and copies ran while one was open for 1% of the time, Pallas kernels for 16%

profile of v3, /device:TPU:2, one launch (start us, length us, event | category | flops | bytes accessed | tf_op | source)
XLA Modules:
  0.0 203.0 jit_solution(8555830768512801480)
XLA Ops:
  7.2 2.7 %mask_inputs.1 = (bf16[1280,256]{1,0:T(8,128)(2,1)}, bf16[1280,256]{1,0:T(8,128)(2,1)}, bf16[4,512,256]{2,1,0:T(8,128)(2,1)}) custom-call(s32[4,2,4]{2,1,0:T(2,128)} %bitcast.9, s32[2,4]{1,0:T(2,128)} %bitcast.10, s32[2,4]{1,0:T(2,128)} %bitcast.11, bf16[4,512,256]{2,1,0:T(8,128)(2,1)} %integrals.1, bf16[512,256]{1,0:T(8,128)(2,1)} %occ.1, bf16[512,256]{1,0:T(8,128)(2,1)} %virt.1), custom_call_target="tpu_custom_call" | custom-call | tf_op jit(solution)/shard_map/mask_inputs/pallas_call | solution.py:172
  12.4 8.5 %collective-permute-done.1.refs_0_ = bf16[1280,256]{1,0:T(8,128)(2,1)S(1)} collective-permute-done((bf16[1280,256]{1,0:T(8,128)(2,1)}, bf16[1280,256]{1,0:T(8,128)(2,1)S(1)}, u32[]{:S(2)}, u32[]{:S(2)}) %collective-permute-start.1) | collective-permute-done | bytes 655392 | tf_op jit(solution)/shard_map/ppermute | solution.py:39
  35.5 3.3 %collective-permute-start.7 = (bf16[2560,256]{1,0:T(8,128)(2,1)}, bf16[2560,256]{1,0:T(8,128)(2,1)S(1)}, u32[]{:S(2)}, u32[]{:S(2)}) collective-permute-start(bf16[2560,256]{1,0:T(8,128)(2,1)} %pack.5.refs_1_), channel_id=1, source_target_pairs={{0,24},{1,7},{2,26},{3,1},{4,28},{5,3},{6,30},{7,5},{8,0},{9,15},{... | collective-permute-start | bytes 3932168 | tf_op jit(solution)/shard_map/ppermute | solution.py:39
  40.0 5.3 %collective-permute-done.5.refs_3_ = bf16[2560,256]{1,0:T(8,128)(2,1)S(1)} collective-permute-done((bf16[2560,256]{1,0:T(8,128)(2,1)}, bf16[2560,256]{1,0:T(8,128)(2,1)S(1)}, u32[]{:S(2)}, u32[]{:S(2)}) %collective-permute-start.5) | collective-permute-done | bytes 1310752 | tf_op jit(solution)/shard_map/ppermute | solution.py:39
  45.3 3.6 %collective-permute-done.4.refs_2_ = bf16[2560,256]{1,0:T(8,128)(2,1)S(1)} collective-permute-done((bf16[2560,256]{1,0:T(8,128)(2,1)}, bf16[2560,256]{1,0:T(8,128)(2,1)S(1)}, u32[]{:S(2)}, u32[]{:S(2)}) %collective-permute-start.4) | collective-permute-done | bytes 1310752 | tf_op jit(solution)/shard_map/ppermute | solution.py:39
  48.9 10.5 %collective-permute-done.7.refs_5_ = bf16[2560,256]{1,0:T(8,128)(2,1)S(1)} collective-permute-done((bf16[2560,256]{1,0:T(8,128)(2,1)}, bf16[2560,256]{1,0:T(8,128)(2,1)S(1)}, u32[]{:S(2)}, u32[]{:S(2)}) %collective-permute-start.7) | collective-permute-done | bytes 1310752 | tf_op jit(solution)/shard_map/ppermute | solution.py:39
  59.4 3.6 %collective-permute-done.6.refs_4_ = bf16[2560,256]{1,0:T(8,128)(2,1)S(1)} collective-permute-done((bf16[2560,256]{1,0:T(8,128)(2,1)}, bf16[2560,256]{1,0:T(8,128)(2,1)S(1)}, u32[]{:S(2)}, u32[]{:S(2)}) %collective-permute-start.6) | collective-permute-done | bytes 1310752 | tf_op jit(solution)/shard_map/ppermute | solution.py:39
  63.0 3.2 %collective-permute-start.9 = (bf16[2560,256]{1,0:T(8,128)(2,1)S(1)}, bf16[2560,256]{1,0:T(8,128)(2,1)}, u32[]{:S(2)}, u32[]{:S(2)}) collective-permute-start(bf16[2560,256]{1,0:T(8,128)(2,1)S(1)} %collective-permute-done.7.refs_5_), channel_id=1, source_target_pairs={{0,24},{1,7},{2,26},{3,1},{4,28},{5,3},{6,30},{7,5},{8,0},{9,15},{... | collective-permute-start | bytes 3932168 | tf_op jit(solution)/shard_map/ppermute | solution.py:39
  66.2 15.6 %collective-permute-done.8.refs_6_ = bf16[2560,256]{1,0:T(8,128)(2,1)S(1)} collective-permute-done((bf16[2560,256]{1,0:T(8,128)(2,1)S(1)}, bf16[2560,256]{1,0:T(8,128)(2,1)S(1)}, u32[]{:S(2)}, u32[]{:S(2)}) %collective-permute-start.8) | collective-permute-done | bytes 1310752 | tf_op jit(solution)/shard_map/ppermute | solution.py:39
  82.9 2.7 %occ_tiles.1.own = bf16[4096,256]{1,0:T(8,128)(2,1)} custom-call(bf16[2560,256]{1,0:T(8,128)(2,1)} %pack.4.refs_0_, bf16[2560,256]{1,0:T(8,128)(2,1)} %pack.5.refs_1_, bf16[2560,256]{1,0:T(8,128)(2,1)} %copy-done.2, bf16[2560,256]{1,0:T(8,128)(2,1)} %copy-done.1, bf16[2560,256]{1,0:T(8,128)(2,1)} %copy-done.4, bf16[2560,256]{1,0:T(8,128)(2,1)} %copy-done.3, ...), custom_call_target="tpu_custom_call" | custom-call | bytes 9437184 | tf_op jit(solution)/shard_map/occ_tiles/pallas_call | solution.py:196
  86.0 5.7 %half_tensor.1 = bf16[1024,256]{1,0:T(8,128)(2,1)} custom-call(bf16[20480,256]{1,0:T(8,128)(2,1)} %all-gather.3.cloned.1.call-done.gathered, bf16[2560,256]{1,0:T(8,128)(2,1)} %pack.4.refs_0_, bf16[2560,256]{1,0:T(8,128)(2,1)} %pack.5.refs_1_, bf16[2560,256]{1,0:T(8,128)(2,1)} %copy-done.2, bf16[2560,256]{1,0:T(8,128)(2,1)} %copy-done.1, ...), custom_call_target="tpu_custom_call" | custom-call | flops 2147483648 | bytes 9437184 | tf_op jit(solution)/shard_map/half_tensor/pallas_call | solution.py:196
  93.0 5.3 %occ_first.1.refs_0_ = bf16[1024,256]{1,0:T(8,128)(2,1)} custom-call(bf16[4096,256]{1,0:T(8,128)(2,1)} %occ_tiles.1.own, bf16[4096,256]{1,0:T(8,128)(2,1)} %copy-done, bf16[20480,256]{1,0:T(8,128)(2,1)} %all-gather.3.cloned.1.call-done.gathered), custom_call_target="tpu_custom_call" | custom-call | flops 2147483648 | bytes 9437184 | tf_op jit(solution)/shard_map/occ_first/pallas_call | solution.py:196
  101.0 7.0 %collective-permute-done.14.refs_0_ = bf16[1024,256]{1,0:T(8,128)(2,1)S(1)} collective-permute-done((bf16[1024,256]{1,0:T(8,128)(2,1)}, bf16[1024,256]{1,0:T(8,128)(2,1)S(1)}, u32[]{:S(2)}, u32[]{:S(2)}) %collective-permute-start.14) | collective-permute-done | bytes 524320 | tf_op jit(solution)/shard_map/ppermute | solution.py:39
  108.1 3.1 %collective-permute-start.16 = (bf16[512,256]{1,0:T(8,128)(2,1)S(1)}, bf16[512,256]{1,0:T(8,128)(2,1)}, u32[]{:S(2)}, u32[]{:S(2)}) collective-permute-start(bf16[512,256]{1,0:T(8,128)(2,1)S(1)} %slice.28), channel_id=1, source_target_pairs={{0,6},{1,25},{2,0},{3,27},{4,2},{5,29},{6,4},{7,31},{8,14},{9,1},{... | collective-permute-start | bytes 786440 | tf_op jit(solution)/shard_map/ppermute | solution.py:39
  116.8 3.4 %collective-permute-done.15.refs_1_ = bf16[512,256]{1,0:T(8,128)(2,1)} collective-permute-done((bf16[512,256]{1,0:T(8,128)(2,1)}, bf16[512,256]{1,0:T(8,128)(2,1)}, u32[]{:S(2)}, u32[]{:S(2)}) %collective-permute-start.15) | collective-permute-done | bytes 262176 | tf_op jit(solution)/shard_map/ppermute | solution.py:39
  124.7 4.9 %collective-permute-done.13.refs_3_ = bf16[2048,256]{1,0:T(8,128)(2,1)S(1)} collective-permute-done((bf16[2048,256]{1,0:T(8,128)(2,1)}, bf16[2048,256]{1,0:T(8,128)(2,1)S(1)}, u32[]{:S(2)}, u32[]{:S(2)}) %collective-permute-start.13) | collective-permute-done | bytes 1048608 | tf_op jit(solution)/shard_map/ppermute | solution.py:39
  129.6 3.5 %collective-permute-done.12.refs_2_ = bf16[2048,256]{1,0:T(8,128)(2,1)S(1)} collective-permute-done((bf16[2048,256]{1,0:T(8,128)(2,1)}, bf16[2048,256]{1,0:T(8,128)(2,1)S(1)}, u32[]{:S(2)}, u32[]{:S(2)}) %collective-permute-start.12) | collective-permute-done | bytes 1048608 | tf_op jit(solution)/shard_map/ppermute | solution.py:39
  133.1 7.8 %collective-permute-done.18.refs_5_ = bf16[2048,256]{1,0:T(8,128)(2,1)} collective-permute-done((bf16[2048,256]{1,0:T(8,128)(2,1)}, bf16[2048,256]{1,0:T(8,128)(2,1)}, u32[]{:S(2)}, u32[]{:S(2)}) %collective-permute-start.18) | collective-permute-done | bytes 1048608 | tf_op jit(solution)/shard_map/ppermute | solution.py:39
  140.9 3.5 %collective-permute-done.17.refs_4_ = bf16[2048,256]{1,0:T(8,128)(2,1)} collective-permute-done((bf16[2048,256]{1,0:T(8,128)(2,1)}, bf16[2048,256]{1,0:T(8,128)(2,1)}, u32[]{:S(2)}, u32[]{:S(2)}) %collective-permute-start.17) | collective-permute-done | bytes 1048608 | tf_op jit(solution)/shard_map/ppermute | solution.py:39
  144.4 3.2 %collective-permute-start.20 = (bf16[2048,256]{1,0:T(8,128)(2,1)}, bf16[2048,256]{1,0:T(8,128)(2,1)}, u32[]{:S(2)}, u32[]{:S(2)}) collective-permute-start(bf16[2048,256]{1,0:T(8,128)(2,1)} %collective-permute-done.18.refs_5_), channel_id=1, source_target_pairs={{0,24},{1,7},{2,26},{3,1},{4,28},{5,3},{6,30},{7,5},{8,0},{9,15},{... | collective-permute-start | bytes 3145736 | tf_op jit(solution)/shard_map/ppermute | solution.py:39
  147.6 4.9 %plane_near.1.plane_sum = f32[1024,256]{1,0:T(8,128)} custom-call(bf16[20480,256]{1,0:T(8,128)(2,1)} %all-gather.3.cloned.1.call-done.gathered, bf16[2048,256]{1,0:T(8,128)(2,1)} %pack.6.refs_0_, bf16[2048,256]{1,0:T(8,128)(2,1)} %pack.7.refs_1_, bf16[2048,256]{1,0:T(8,128)(2,1)} %copy-done.11, bf16[2048,256]{1,0:T(8,128)(2,1)} %copy-done.12, ...), custom_call_target="tpu_custom_call" | custom-call | flops 2147483648 | bytes 9437184 | tf_op jit(solution)/shard_map/plane_near/pallas_call | solution.py:196
  152.6 5.3 %polar_ring.1.ring_part = bf16[1024,256]{1,0:T(8,128)(2,1)} custom-call(bf16[4096,256]{1,0:T(8,128)(2,1)} %occ_tiles.1.own, bf16[4096,256]{1,0:T(8,128)(2,1)} %copy-done, bf16[8192,256]{1,0:T(8,128)(2,1)} %all-gather.5.cloned.1.call-done.gathered), custom_call_target="tpu_custom_call" | custom-call | flops 2147483648 | bytes 9437184 | tf_op jit(solution)/shard_map/polar_ring/pallas_call | solution.py:196
  160.5 4.9 %polar_product.1 = (bf16[2048,256]{1,0:T(8,128)(2,1)}, f32[128,128]{1,0:T(8,128)}) custom-call(bf16[20480,256]{1,0:T(8,128)(2,1)} %all-gather.3.cloned.1.call-done.gathered, bf16[2048,256]{1,0:T(8,128)(2,1)} %collective-permute-done.19.top, bf16[2048,256]{1,0:T(8,128)(2,1)} %collective-permute-done.20.bottom, f32[1024,256]{1,0:T(8,128)} %plane_near.1.plane_sum, ...), custom_call_target="tpu_custom_call" | custom-call | flops 536870912 | bytes 9437184 | tf_op jit(solution)/shard_map/polar_product/pallas_call | solution.py:196
  165.4 29.9 %all_to_all.5 = f32[128,1,128]{2,1,0:T(1,128)S(1)} all-to-all(f32[128,1,128]{2,1,0:T(1,128)} %bitcast.8), channel_id=1, replica_groups=mesh['row'=8,'col'=16,'layer'=2] {'row','col'}, dimensions={0} | all-to-all | bytes 131072 | tf_op jit(solution)/shard_map/all_to_all | solution.py:400
  (75 shorter events, 37.1 us)
Async XLA Ops:
  7.2 78.8 %all-gather.3.cloned.1.call-start = ((), (), s32[]{:S(2)}) async-start(), calls=%async_computation.1 | async-start | bytes 11141120 | tf_op jit(solution)/shard_map/all_gather | solution.py:384
  10.0 142.6 %all-gather.5.cloned.1.call-start = ((), (), s32[]{:S(2)}) async-start(), calls=%async_computation.2 | async-start | bytes 4718592 | tf_op jit(solution)/shard_map/all_gather | solution.py:392
  10.0 10.9 %collective-permute-start.1 = (bf16[1280,256]{1,0:T(8,128)(2,1)}, bf16[1280,256]{1,0:T(8,128)(2,1)S(1)}, u32[]{:S(2)}, u32[]{:S(2)}) collective-permute-start(bf16[1280,256]{1,0:T(8,128)(2,1)} %get-tuple-element.22.refs_0_), channel_id=1, source_target_pairs={{0,6},{1,25},{2,0},{3,27},{4,2},{5,29},{6,4},{7,31},{8,14},{9,1},{... | collective-permute-start | bytes 1966088 | tf_op jit(solution)/shard_map/ppermute | solution.py:39
  12.4 11.6 %collective-permute-start = (bf16[1280,256]{1,0:T(8,128)(2,1)}, bf16[1280,256]{1,0:T(8,128)(2,1)S(1)}, u32[]{:S(2)}, u32[]{:S(2)}) collective-permute-start(bf16[1280,256]{1,0:T(8,128)(2,1)} %get-tuple-element.22.refs_0_), channel_id=1, source_target_pairs={{0,2},{1,9},{2,4},{3,11},{4,6},{5,13},{6,0},{7,15},{8,10},{9,17},{... | collective-permute-start | bytes 1966088 | tf_op jit(solution)/shard_map/ppermute | solution.py:39
  21.7 8.2 %collective-permute-start.3 = (bf16[640,256]{1,0:T(8,128)(2,1)}, bf16[640,256]{1,0:T(8,128)(2,1)S(1)}, u32[]{:S(2)}, u32[]{:S(2)}) collective-permute-start(bf16[640,256]{1,0:T(8,128)(2,1)} %slice.26), channel_id=1, source_target_pairs={{0,6},{1,25},{2,0},{3,27},{4,2},{5,29},{6,4},{7,31},{8,14},{9,1},{... | collective-permute-start | bytes 983048 | tf_op jit(solution)/shard_map/ppermute | solution.py:39
  24.8 7.7 %collective-permute-start.2 = (bf16[640,256]{1,0:T(8,128)(2,1)}, bf16[640,256]{1,0:T(8,128)(2,1)S(1)}, u32[]{:S(2)}, u32[]{:S(2)}) collective-permute-start(bf16[640,256]{1,0:T(8,128)(2,1)} %slice.25), channel_id=1, source_target_pairs={{0,2},{1,9},{2,4},{3,11},{4,6},{5,13},{6,0},{7,15},{8,10},{9,17},{... | collective-permute-start | bytes 983048 | tf_op jit(solution)/shard_map/ppermute | solution.py:39
  27.2 18.1 %collective-permute-start.5 = (bf16[2560,256]{1,0:T(8,128)(2,1)}, bf16[2560,256]{1,0:T(8,128)(2,1)S(1)}, u32[]{:S(2)}, u32[]{:S(2)}) collective-permute-start(bf16[2560,256]{1,0:T(8,128)(2,1)} %pack.4.refs_0_), channel_id=1, source_target_pairs={{0,24},{1,7},{2,26},{3,1},{4,28},{5,3},{6,30},{7,5},{8,0},{9,15},{... | collective-permute-start | bytes 3932168 | tf_op jit(solution)/shard_map/ppermute | solution.py:39
  29.9 19.0 %collective-permute-start.4 = (bf16[2560,256]{1,0:T(8,128)(2,1)}, bf16[2560,256]{1,0:T(8,128)(2,1)S(1)}, u32[]{:S(2)}, u32[]{:S(2)}) collective-permute-start(bf16[2560,256]{1,0:T(8,128)(2,1)} %pack.4.refs_0_), channel_id=1, source_target_pairs={{0,8},{1,3},{2,10},{3,5},{4,12},{5,7},{6,14},{7,1},{8,16},{9,11},{... | collective-permute-start | bytes 3932168 | tf_op jit(solution)/shard_map/ppermute | solution.py:39
  35.5 23.9 %collective-permute-start.7 = (bf16[2560,256]{1,0:T(8,128)(2,1)}, bf16[2560,256]{1,0:T(8,128)(2,1)S(1)}, u32[]{:S(2)}, u32[]{:S(2)}) collective-permute-start(bf16[2560,256]{1,0:T(8,128)(2,1)} %pack.5.refs_1_), channel_id=1, source_target_pairs={{0,24},{1,7},{2,26},{3,1},{4,28},{5,3},{6,30},{7,5},{8,0},{9,15},{... | collective-permute-start | bytes 3932168 | tf_op jit(solution)/shard_map/ppermute | solution.py:39
  38.8 24.2 %collective-permute-start.6 = (bf16[2560,256]{1,0:T(8,128)(2,1)}, bf16[2560,256]{1,0:T(8,128)(2,1)S(1)}, u32[]{:S(2)}, u32[]{:S(2)}) collective-permute-start(bf16[2560,256]{1,0:T(8,128)(2,1)} %pack.5.refs_1_), channel_id=1, source_target_pairs={{0,8},{1,3},{2,10},{3,5},{4,12},{5,7},{6,14},{7,1},{8,16},{9,11},{... | collective-permute-start | bytes 3932168 | tf_op jit(solution)/shard_map/ppermute | solution.py:39
  63.0 18.8 %collective-permute-start.8 = (bf16[2560,256]{1,0:T(8,128)(2,1)S(1)}, bf16[2560,256]{1,0:T(8,128)(2,1)S(1)}, u32[]{:S(2)}, u32[]{:S(2)}) collective-permute-start(bf16[2560,256]{1,0:T(8,128)(2,1)S(1)} %collective-permute-done.4.refs_2_), channel_id=1, source_target_pairs={{0,8},{1,3},{2,10},{3,5},{4,12},{5,7},{6,14},{7,1},{8,16},{9,11},{... | collective-permute-start | bytes 3932168 | tf_op jit(solution)/shard_map/ppermute | solution.py:39
  63.0 19.9 %collective-permute-start.9 = (bf16[2560,256]{1,0:T(8,128)(2,1)S(1)}, bf16[2560,256]{1,0:T(8,128)(2,1)}, u32[]{:S(2)}, u32[]{:S(2)}) collective-permute-start(bf16[2560,256]{1,0:T(8,128)(2,1)S(1)} %collective-permute-done.7.refs_5_), channel_id=1, source_target_pairs={{0,24},{1,7},{2,26},{3,1},{4,28},{5,3},{6,30},{7,5},{8,0},{9,15},{... | collective-permute-start | bytes 3932168 | tf_op jit(solution)/shard_map/ppermute | solution.py:39
  85.6 6.0 %collective-permute-start.10 = (bf16[4096,256]{1,0:T(8,128)(2,1)}, bf16[4096,256]{1,0:T(8,128)(2,1)S(1)}, u32[]{:S(2)}, u32[]{:S(2)}) collective-permute-start(bf16[4096,256]{1,0:T(8,128)(2,1)} %occ_tiles.1.own), channel_id=1, source_target_pairs={{0,1},{1,0},{2,3},{3,2},{4,5},{5,4},{6,7},{7,6},{8,9},{9,8},{10,11... | collective-permute-start | bytes 6291464 | tf_op jit(solution)/shard_map/ppermute | solution.py:43
  98.3 9.7 %collective-permute-start.14 = (bf16[1024,256]{1,0:T(8,128)(2,1)}, bf16[1024,256]{1,0:T(8,128)(2,1)S(1)}, u32[]{:S(2)}, u32[]{:S(2)}) collective-permute-start(bf16[1024,256]{1,0:T(8,128)(2,1)} %occ_first.1.refs_0_), channel_id=1, source_target_pairs={{0,6},{1,25},{2,0},{3,27},{4,2},{5,29},{6,4},{7,31},{8,14},{9,1},{... | collective-permute-start | bytes 1572872 | tf_op jit(solution)/shard_map/ppermute | solution.py:39
  101.0 10.5 %collective-permute-start.11 = (bf16[1024,256]{1,0:T(8,128)(2,1)}, bf16[1024,256]{1,0:T(8,128)(2,1)S(1)}, u32[]{:S(2)}, u32[]{:S(2)}) collective-permute-start(bf16[1024,256]{1,0:T(8,128)(2,1)} %occ_first.1.refs_0_), channel_id=1, source_target_pairs={{0,2},{1,9},{2,4},{3,11},{4,6},{5,13},{6,0},{7,15},{8,10},{9,17},{... | collective-permute-start | bytes 1572872 | tf_op jit(solution)/shard_map/ppermute | solution.py:39
  108.1 8.8 %collective-permute-start.16 = (bf16[512,256]{1,0:T(8,128)(2,1)S(1)}, bf16[512,256]{1,0:T(8,128)(2,1)}, u32[]{:S(2)}, u32[]{:S(2)}) collective-permute-start(bf16[512,256]{1,0:T(8,128)(2,1)S(1)} %slice.28), channel_id=1, source_target_pairs={{0,6},{1,25},{2,0},{3,27},{4,2},{5,29},{6,4},{7,31},{8,14},{9,1},{... | collective-permute-start | bytes 786440 | tf_op jit(solution)/shard_map/ppermute | solution.py:39
  112.3 8.0 %collective-permute-start.15 = (bf16[512,256]{1,0:T(8,128)(2,1)}, bf16[512,256]{1,0:T(8,128)(2,1)}, u32[]{:S(2)}, u32[]{:S(2)}) collective-permute-start(bf16[512,256]{1,0:T(8,128)(2,1)} %slice.27), channel_id=1, source_target_pairs={{0,2},{1,9},{2,4},{3,11},{4,6},{5,13},{6,0},{7,15},{8,10},{9,17},{... | collective-permute-start | bytes 786440 | tf_op jit(solution)/shard_map/ppermute | solution.py:39
  114.5 15.1 %collective-permute-start.13 = (bf16[2048,256]{1,0:T(8,128)(2,1)}, bf16[2048,256]{1,0:T(8,128)(2,1)S(1)}, u32[]{:S(2)}, u32[]{:S(2)}) collective-permute-start(bf16[2048,256]{1,0:T(8,128)(2,1)} %pack.6.refs_0_), channel_id=1, source_target_pairs={{0,24},{1,7},{2,26},{3,1},{4,28},{5,3},{6,30},{7,5},{8,0},{9,15},{... | collective-permute-start | bytes 3145736 | tf_op jit(solution)/shard_map/ppermute | solution.py:39
  116.8 16.2 %collective-permute-start.12 = (bf16[2048,256]{1,0:T(8,128)(2,1)}, bf16[2048,256]{1,0:T(8,128)(2,1)S(1)}, u32[]{:S(2)}, u32[]{:S(2)}) collective-permute-start(bf16[2048,256]{1,0:T(8,128)(2,1)} %pack.6.refs_0_), channel_id=1, source_target_pairs={{0,8},{1,3},{2,10},{3,5},{4,12},{5,7},{6,14},{7,1},{8,16},{9,11},{... | collective-permute-start | bytes 3145736 | tf_op jit(solution)/shard_map/ppermute | solution.py:39
  122.3 18.6 %collective-permute-start.18 = (bf16[2048,256]{1,0:T(8,128)(2,1)}, bf16[2048,256]{1,0:T(8,128)(2,1)}, u32[]{:S(2)}, u32[]{:S(2)}) collective-permute-start(bf16[2048,256]{1,0:T(8,128)(2,1)} %pack.7.refs_1_), channel_id=1, source_target_pairs={{0,24},{1,7},{2,26},{3,1},{4,28},{5,3},{6,30},{7,5},{8,0},{9,15},{... | collective-permute-start | bytes 3145736 | tf_op jit(solution)/shard_map/ppermute | solution.py:39
  124.6 19.7 %collective-permute-start.17 = (bf16[2048,256]{1,0:T(8,128)(2,1)}, bf16[2048,256]{1,0:T(8,128)(2,1)}, u32[]{:S(2)}, u32[]{:S(2)}) collective-permute-start(bf16[2048,256]{1,0:T(8,128)(2,1)} %pack.7.refs_1_), channel_id=1, source_target_pairs={{0,8},{1,3},{2,10},{3,5},{4,12},{5,7},{6,14},{7,1},{8,16},{9,11},{... | collective-permute-start | bytes 3145736 | tf_op jit(solution)/shard_map/ppermute | solution.py:39
  124.7 33.2 %collective-permute-start.21 = (bf16[4,512,256]{2,1,0:T(8,128)(2,1)S(1)}, bf16[4,512,256]{2,1,0:T(8,128)(2,1)}, u32[]{:S(2)}, u32[]{:S(2)}) collective-permute-start(bf16[4,512,256]{2,1,0:T(8,128)(2,1)S(1)} %copy-done.10), channel_id=1, source_target_pairs={{0,1},{1,0},{2,3},{3,2},{4,5},{5,4},{6,7},{7,6},{8,9},{9,8},{10,11... | collective-permute-start | bytes 3145736 | tf_op jit(solution)/shard_map/ppermute | solution.py:43
  144.4 16.1 %collective-permute-start.19 = (bf16[2048,256]{1,0:T(8,128)(2,1)S(1)}, bf16[2048,256]{1,0:T(8,128)(2,1)}, u32[]{:S(2)}, u32[]{:S(2)}) collective-permute-start(bf16[2048,256]{1,0:T(8,128)(2,1)S(1)} %collective-permute-done.12.refs_2_), channel_id=1, source_target_pairs={{0,8},{1,3},{2,10},{3,5},{4,12},{5,7},{6,14},{7,1},{8,16},{9,11},{... | collective-permute-start | bytes 3145736 | tf_op jit(solution)/shard_map/ppermute | solution.py:39
  144.4 16.1 %collective-permute-start.20 = (bf16[2048,256]{1,0:T(8,128)(2,1)}, bf16[2048,256]{1,0:T(8,128)(2,1)}, u32[]{:S(2)}, u32[]{:S(2)}) collective-permute-start(bf16[2048,256]{1,0:T(8,128)(2,1)} %collective-permute-done.18.refs_5_), channel_id=1, source_target_pairs={{0,24},{1,7},{2,26},{3,1},{4,28},{5,3},{6,30},{7,5},{8,0},{9,15},{... | collective-permute-start | bytes 3145736 | tf_op jit(solution)/shard_map/ppermute | solution.py:39
  (15 other events, 177.1 us)
Sparse Core Ops, SparseCore 0:
  10.1 68.7 all-gather.2
  91.8 59.0 all-gather.4

commit v4 on v3

--- a/solution.py
+++ b/solution.py
@@ -274,6 +274,23 @@
     return call(
         functools.partial(plane_kernel, arrays, rows), name, (gathered, *pieces),
         jax.ShapeDtypeStruct(SUM, dtype), scratch, 4 * n, 2 << 30,
+    )
+
+
+def plane_last_kernel(rows, gathered, top, bottom, sum_in, out, bufs, virt_buf, acc, out_buf, sems):
+    sum_copy, = start_all([sum_in], [acc], sems)
+    copies, virt_copies = start_plane((6, 7), rows, gathered, (top, bottom), bufs, virt_buf, sems, 1)
+    sum_copy.wait()
+    plane_add(copies, bufs, virt_copies, virt_buf, acc, False)
+    out_buf[...] = acc[...].astype(BF16)
+    pltpu.sync_copy(out_buf, out)
+
+
+def plane_last(rows, gathered, pieces, sum_in):
+    scratch = [pltpu.VMEM((4, *SUM), BF16), pltpu.VMEM((4, *TILE), BF16), pltpu.VMEM(SUM, F32), pltpu.VMEM(SUM, BF16)]
+    return call(
+        functools.partial(plane_last_kernel, rows), "plane_last", (gathered, *pieces, sum_in),
+        jax.ShapeDtypeStruct(SUM, BF16), scratch, 9, 1 << 29,
     )
 
 
@@ -383,9 +400,11 @@
     )
     gathered = lax.all_gather(ring_aux, ("row", "layer"), axis=0, tiled=True)
     plane = gather_plane(plane_aux)
-    own_occ = occ_tiles(plane)
+    plane_sum = plane_product("plane_near", tuple(range(6)), STRIDE, gathered, plane[:6], F32)
+    *far, plane_sum = lax.optimization_barrier((*plane[6:], plane_sum))
+    own_occ = occ_tiles((*plane[:6], *far))
     other_occ = swap_cores(own_occ)
-    half_tensor = plane_product("half_tensor", tuple(range(8)), STRIDE, gathered, plane, BF16)
+    half_tensor = plane_last(STRIDE, gathered, far, plane_sum)
     own_occ, other_occ, half_tensor = lax.optimization_barrier((own_occ, other_occ, half_tensor))
     occ_first = ring_product("occ_first", own_occ, other_occ, gathered, STRIDE, HALF, True)
 

time: 203 us -> 195 us (0.961)
  waiting for transfers between devices: 82.8 us -> 73.5 us
  blocking collectives: 29.9 us -> 25.5 us
  starting transfers between devices: 29.2 us -> 31.6 us
  Pallas kernels: 40.1 us -> 42.5 us
    ppermute x20, waiting for transfers between devices: 82.8 us -> 59.5 us  [plane_move(): return lax.ppermute(value, ('col', 'layer'), plane_perm(shift, first))]
    all_gather x1, waiting for transfers between devices: 0.02 us -> 13.1 us  [body(): gathered = lax.all_gather(ring_aux, ('row', 'layer'), axis=0, tiled=True)]
    all_to_all x1, blocking collectives: 29.9 us -> 25.5 us  [body(): shares = lax.all_to_all(chi.reshape(128, 1, BLK), ('row', 'col'), 0, 0)]
    pallas_call x6 -> x7, Pallas kernels: 28.9 us -> 31.2 us  [call(): pl.pallas_call(kernel, out_shape=outs, in_specs=[HBM] * len(operands), ou...]
    ppermute x20, starting transfers between devices: 28.9 us -> 31 us  [plane_move(): return lax.ppermute(value, ('col', 'layer'), plane_perm(shift, first))]
    unnamed x30 -> x28, local copies, waits for them, and re-layouts: 3.43 us -> 4.72 us
  transfers between devices with their start and end apart: 24 -> 24, of which waited for: 15 -> 12; matrix products, arithmetic and copies ran while one was open for 1% -> 1% of each run, Pallas kernels for 16% -> 17%
where the time goes in v4:
time: 195 us
  waiting for transfers between devices  73.5 us (38%)
  Pallas kernels  42.5 us (22%)
  starting transfers between devices  31.6 us (16%)
  blocking collectives  25.5 us (13%)
  between operations  14.2 us (7%)
  local copies, waits for them, and re-layouts  7.06 us (4%)
    ppermute x20, waiting for transfers between devices, plane_move(): return lax.ppermute(value, ('col', 'layer'), plane_perm(shift, first))  59.5 us
    pallas_call x7, Pallas kernels, call(): pl.pallas_call(kernel, out_shape=outs, in_specs=[HBM] * len(operands), ou...  31.2 us
    ppermute x20, starting transfers between devices, plane_move(): return lax.ppermute(value, ('col', 'layer'), plane_perm(shift, first))  31 us
    all_to_all x1, blocking collectives, body(): shares = lax.all_to_all(chi.reshape(128, 1, BLK), ('row', 'col'), 0, 0)  25.5 us
    all_gather x1, waiting for transfers between devices, body(): gathered = lax.all_gather(ring_aux, ('row', 'layer'), axis=0, tiled=True)  13.1 us
    pallas_call x4, Pallas kernels, pack(): pl.pallas_call(functools.partial(pack_kernel, moves, len(sources)), out_s...  8.56 us
    unnamed x28, local copies, waits for them, and re-layouts  4.72 us
  transfers between devices with their start and end apart: 24, of which 12 were waited for; matrix products, arithmetic and copies ran while one was open for 1% of the time, Pallas kernels for 17%

profile of v4, /device:TPU:2, one launch (start us, length us, event | category | flops | bytes accessed | tf_op | source)
XLA Modules:
  0.0 194.5 jit_solution(1444215834494215538)
XLA Ops:
  7.2 2.7 %mask_inputs.1 = (bf16[1280,256]{1,0:T(8,128)(2,1)}, bf16[1280,256]{1,0:T(8,128)(2,1)}, bf16[4,512,256]{2,1,0:T(8,128)(2,1)}) custom-call(s32[4,2,4]{2,1,0:T(2,128)} %bitcast.9, s32[2,4]{1,0:T(2,128)} %bitcast.10, s32[2,4]{1,0:T(2,128)} %bitcast.11, bf16[4,512,256]{2,1,0:T(8,128)(2,1)} %integrals.1, bf16[512,256]{1,0:T(8,128)(2,1)} %occ.1, bf16[512,256]{1,0:T(8,128)(2,1)} %virt.1), custom_call_target="tpu_custom_call" | custom-call | tf_op jit(solution)/shard_map/mask_inputs/pallas_call | solution.py:172
  12.5 8.7 %collective-permute-done.refs_1_ = bf16[1280,256]{1,0:T(8,128)(2,1)S(1)} collective-permute-done((bf16[1280,256]{1,0:T(8,128)(2,1)}, bf16[1280,256]{1,0:T(8,128)(2,1)S(1)}, u32[]{:S(2)}, u32[]{:S(2)}) %collective-permute-start) | collective-permute-done | bytes 655392 | tf_op jit(solution)/shard_map/ppermute | solution.py:39
  26.1 2.2 %pack.4.refs_0_ = bf16[2560,256]{1,0:T(8,128)(2,1)} custom-call(bf16[1280,256]{1,0:T(8,128)(2,1)} %get-tuple-element.25.refs_0_, bf16[1280,256]{1,0:T(8,128)(2,1)} %copy-done.5), custom_call_target="tpu_custom_call" | custom-call | bytes 4194304 | tf_op jit(solution)/shard_map/pack/pallas_call | solution.py:107
  28.5 3.1 %collective-permute-start.5 = (bf16[2560,256]{1,0:T(8,128)(2,1)}, bf16[2560,256]{1,0:T(8,128)(2,1)S(1)}, u32[]{:S(2)}, u32[]{:S(2)}) collective-permute-start(bf16[2560,256]{1,0:T(8,128)(2,1)} %pack.4.refs_0_), channel_id=1, source_target_pairs={{0,24},{1,7},{2,26},{3,1},{4,28},{5,3},{6,30},{7,5},{8,0},{9,15},{... | collective-permute-start | bytes 3932168 | tf_op jit(solution)/shard_map/ppermute | solution.py:39
  32.2 2.3 %pack.5.refs_1_ = bf16[2560,256]{1,0:T(8,128)(2,1)} custom-call(bf16[1280,256]{1,0:T(8,128)(2,1)} %copy-done.4, bf16[640,256]{1,0:T(8,128)(2,1)} %collective-permute-done.2.refs_1_, bf16[640,256]{1,0:T(8,128)(2,1)} %collective-permute-done.3.refs_2_), custom_call_target="tpu_custom_call" | custom-call | bytes 4194304 | tf_op jit(solution)/shard_map/pack/pallas_call | solution.py:107
  34.4 2.8 %collective-permute-start.6 = (bf16[2560,256]{1,0:T(8,128)(2,1)}, bf16[2560,256]{1,0:T(8,128)(2,1)S(1)}, u32[]{:S(2)}, u32[]{:S(2)}) collective-permute-start(bf16[2560,256]{1,0:T(8,128)(2,1)} %pack.5.refs_1_), channel_id=1, source_target_pairs={{0,8},{1,3},{2,10},{3,5},{4,12},{5,7},{6,14},{7,1},{8,16},{9,11},{... | collective-permute-start | bytes 3932168 | tf_op jit(solution)/shard_map/ppermute | solution.py:39
  38.8 8.6 %collective-permute-done.4.refs_2_ = bf16[2560,256]{1,0:T(8,128)(2,1)S(1)} collective-permute-done((bf16[2560,256]{1,0:T(8,128)(2,1)}, bf16[2560,256]{1,0:T(8,128)(2,1)S(1)}, u32[]{:S(2)}, u32[]{:S(2)}) %collective-permute-start.4) | collective-permute-done | bytes 1310752 | tf_op jit(solution)/shard_map/ppermute | solution.py:39
  47.4 14.0 %collective-permute-done.6.refs_4_ = bf16[2560,256]{1,0:T(8,128)(2,1)S(1)} collective-permute-done((bf16[2560,256]{1,0:T(8,128)(2,1)}, bf16[2560,256]{1,0:T(8,128)(2,1)S(1)}, u32[]{:S(2)}, u32[]{:S(2)}) %collective-permute-start.6) | collective-permute-done | bytes 1310752 | tf_op jit(solution)/shard_map/ppermute | solution.py:39
  62.5 3.2 %collective-permute-start.9 = (bf16[2560,256]{1,0:T(8,128)(2,1)}, bf16[2560,256]{1,0:T(8,128)(2,1)}, u32[]{:S(2)}, u32[]{:S(2)}) collective-permute-start(bf16[2560,256]{1,0:T(8,128)(2,1)} %collective-permute-done.7.refs_5_), channel_id=1, source_target_pairs={{0,24},{1,7},{2,26},{3,1},{4,28},{5,3},{6,30},{7,5},{8,0},{9,15},{... | collective-permute-start | bytes 3932168 | tf_op jit(solution)/shard_map/ppermute | solution.py:39
  65.8 13.1 %all-gather.3.cloned.1.call-done.gathered = bf16[20480,256]{1,0:T(8,128)(2,1)} async-done(((bf16[1280,256]{1,0:T(8,128)(2,1)}), bf16[20480,256]{1,0:T(8,128)(2,1)}) %all-gather.3.cloned.1.call-update) | async-done | bytes 10485776 | tf_op jit(solution)/shard_map/all_gather | solution.py:401
  78.9 4.9 %plane_near.2.sum_in = f32[1024,256]{1,0:T(8,128)} custom-call(bf16[20480,256]{1,0:T(8,128)(2,1)} %all-gather.3.cloned.1.call-done.gathered, bf16[2560,256]{1,0:T(8,128)(2,1)} %pack.4.refs_0_, bf16[2560,256]{1,0:T(8,128)(2,1)} %pack.5.refs_1_, bf16[2560,256]{1,0:T(8,128)(2,1)} %copy-done.1, bf16[2560,256]{1,0:T(8,128)(2,1)} %copy-done.2, ...), custom_call_target="tpu_custom_call" | custom-call | flops 2147483648 | bytes 9437184 | tf_op jit(solution)/shard_map/plane_near/pallas_call | solution.py:196
  83.8 2.7 %occ_tiles.1.own = bf16[4096,256]{1,0:T(8,128)(2,1)} custom-call(bf16[2560,256]{1,0:T(8,128)(2,1)} %pack.4.refs_0_, bf16[2560,256]{1,0:T(8,128)(2,1)} %pack.5.refs_1_, bf16[2560,256]{1,0:T(8,128)(2,1)} %copy-done.1, bf16[2560,256]{1,0:T(8,128)(2,1)} %copy-done.2, bf16[2560,256]{1,0:T(8,128)(2,1)} %copy-done.3, ...), custom_call_target="tpu_custom_call" | custom-call | bytes 9437184 | tf_op jit(solution)/shard_map/occ_tiles/pallas_call | solution.py:196
  87.1 3.3 %plane_last.1 = bf16[1024,256]{1,0:T(8,128)(2,1)} custom-call(bf16[20480,256]{1,0:T(8,128)(2,1)} %all-gather.3.cloned.1.call-done.gathered, bf16[2560,256]{1,0:T(8,128)(2,1)} %collective-permute-done.8.refs_6_.top, bf16[2560,256]{1,0:T(8,128)(2,1)} %collective-permute-done.9.refs_7_.bottom, f32[1024,256]{1,0:T(8,128)} %plane_near.2.sum_in), custom_call_target="tpu_custom_call" | custom-call | flops 536870912 | bytes 9437184 | tf_op jit(solution)/shard_map/plane_last/pallas_call | solution.py:196
  92.5 5.3 %occ_first.1.refs_0_ = bf16[1024,256]{1,0:T(8,128)(2,1)} custom-call(bf16[4096,256]{1,0:T(8,128)(2,1)} %occ_tiles.1.own, bf16[4096,256]{1,0:T(8,128)(2,1)} %copy-done, bf16[20480,256]{1,0:T(8,128)(2,1)} %all-gather.3.cloned.1.call-done.gathered), custom_call_target="tpu_custom_call" | custom-call | flops 2147483648 | bytes 9437184 | tf_op jit(solution)/shard_map/occ_first/pallas_call | solution.py:196
  99.9 7.4 %collective-permute-done.11.refs_1_ = bf16[1024,256]{1,0:T(8,128)(2,1)S(1)} collective-permute-done((bf16[1024,256]{1,0:T(8,128)(2,1)}, bf16[1024,256]{1,0:T(8,128)(2,1)S(1)}, u32[]{:S(2)}, u32[]{:S(2)}) %collective-permute-start.11) | collective-permute-done | bytes 524320 | tf_op jit(solution)/shard_map/ppermute | solution.py:39
  116.6 2.1 %pack.7.refs_1_ = bf16[2048,256]{1,0:T(8,128)(2,1)} custom-call(bf16[1024,256]{1,0:T(8,128)(2,1)} %copy-done.6, bf16[512,256]{1,0:T(8,128)(2,1)} %copy-done.12, bf16[512,256]{1,0:T(8,128)(2,1)} %copy-done.13), custom_call_target="tpu_custom_call" | custom-call | bytes 4194304 | tf_op jit(solution)/shard_map/pack/pallas_call | solution.py:107
  122.0 6.1 %collective-permute-done.12.refs_2_ = bf16[2048,256]{1,0:T(8,128)(2,1)S(1)} collective-permute-done((bf16[2048,256]{1,0:T(8,128)(2,1)}, bf16[2048,256]{1,0:T(8,128)(2,1)S(1)}, u32[]{:S(2)}, u32[]{:S(2)}) %collective-permute-start.12) | collective-permute-done | bytes 1048608 | tf_op jit(solution)/shard_map/ppermute | solution.py:39
  128.3 11.0 %collective-permute-done.17.refs_4_ = bf16[2048,256]{1,0:T(8,128)(2,1)S(1)} collective-permute-done((bf16[2048,256]{1,0:T(8,128)(2,1)}, bf16[2048,256]{1,0:T(8,128)(2,1)S(1)}, u32[]{:S(2)}, u32[]{:S(2)}) %collective-permute-start.17) | collective-permute-done | bytes 1048608 | tf_op jit(solution)/shard_map/ppermute | solution.py:39
  141.0 2.6 %collective-permute-start.20 = (bf16[2048,256]{1,0:T(8,128)(2,1)}, bf16[2048,256]{1,0:T(8,128)(2,1)}, u32[]{:S(2)}, u32[]{:S(2)}) collective-permute-start(bf16[2048,256]{1,0:T(8,128)(2,1)} %collective-permute-done.18.refs_5_), channel_id=1, source_target_pairs={{0,24},{1,7},{2,26},{3,1},{4,28},{5,3},{6,30},{7,5},{8,0},{9,15},{... | collective-permute-start | bytes 3145736 | tf_op jit(solution)/shard_map/ppermute | solution.py:39
  143.6 4.8 %plane_near.3.plane_sum = f32[1024,256]{1,0:T(8,128)} custom-call(bf16[20480,256]{1,0:T(8,128)(2,1)} %all-gather.3.cloned.1.call-done.gathered, bf16[2048,256]{1,0:T(8,128)(2,1)} %pack.6.refs_0_, bf16[2048,256]{1,0:T(8,128)(2,1)} %pack.7.refs_1_, bf16[2048,256]{1,0:T(8,128)(2,1)} %copy-done.9, bf16[2048,256]{1,0:T(8,128)(2,1)} %collective-permute-done.13.refs_3_, ...), custom_call_target="tpu_custom_call" | custom-call | flops 2147483648 | bytes 9437184 | tf_op jit(solution)/shard_map/plane_near/pallas_call | solution.py:196
  148.4 5.3 %polar_ring.1.ring_part = bf16[1024,256]{1,0:T(8,128)(2,1)} custom-call(bf16[4096,256]{1,0:T(8,128)(2,1)} %occ_tiles.1.own, bf16[4096,256]{1,0:T(8,128)(2,1)} %copy-done, bf16[8192,256]{1,0:T(8,128)(2,1)} %all-gather.5.cloned.1.call-done.gathered), custom_call_target="tpu_custom_call" | custom-call | flops 2147483648 | bytes 9437184 | tf_op jit(solution)/shard_map/polar_ring/pallas_call | solution.py:196
  153.8 2.7 %collective-permute-done.19.top = bf16[2048,256]{1,0:T(8,128)(2,1)} collective-permute-done((bf16[2048,256]{1,0:T(8,128)(2,1)S(1)}, bf16[2048,256]{1,0:T(8,128)(2,1)}, u32[]{:S(2)}, u32[]{:S(2)}) %collective-permute-start.19) | collective-permute-done | bytes 1048608 | tf_op jit(solution)/shard_map/ppermute | solution.py:39
  156.5 4.9 %polar_product.1 = (bf16[2048,256]{1,0:T(8,128)(2,1)}, f32[128,128]{1,0:T(8,128)}) custom-call(bf16[20480,256]{1,0:T(8,128)(2,1)} %all-gather.3.cloned.1.call-done.gathered, bf16[2048,256]{1,0:T(8,128)(2,1)} %collective-permute-done.19.top, bf16[2048,256]{1,0:T(8,128)(2,1)} %collective-permute-done.20.bottom, f32[1024,256]{1,0:T(8,128)} %plane_near.3.plane_sum, ...), custom_call_target="tpu_custom_call" | custom-call | flops 536870912 | bytes 9437184 | tf_op jit(solution)/shard_map/polar_product/pallas_call | solution.py:196
  161.4 25.5 %all_to_all.5 = f32[128,1,128]{2,1,0:T(1,128)S(1)} all-to-all(f32[128,1,128]{2,1,0:T(1,128)} %bitcast.8), channel_id=1, replica_groups=mesh['row'=8,'col'=16,'layer'=2] {'row','col'}, dimensions={0} | all-to-all | bytes 131072 | tf_op jit(solution)/shard_map/all_to_all | solution.py:419
  (74 shorter events, 31.0 us)
Async XLA Ops:
  7.2 71.7 %all-gather.3.cloned.1.call-start = ((), (), s32[]{:S(2)}) async-start(), calls=%async_computation.1 | async-start | bytes 11141120 | tf_op jit(solution)/shard_map/all_gather | solution.py:401
  10.0 138.5 %all-gather.5.cloned.1.call-start = ((), (), s32[]{:S(2)}) async-start(), calls=%async_computation.2 | async-start | bytes 4718592 | tf_op jit(solution)/shard_map/all_gather | solution.py:411
  10.0 11.1 %collective-permute-start = (bf16[1280,256]{1,0:T(8,128)(2,1)}, bf16[1280,256]{1,0:T(8,128)(2,1)S(1)}, u32[]{:S(2)}, u32[]{:S(2)}) collective-permute-start(bf16[1280,256]{1,0:T(8,128)(2,1)} %get-tuple-element.25.refs_0_), channel_id=1, source_target_pairs={{0,2},{1,9},{2,4},{3,11},{4,6},{5,13},{6,0},{7,15},{8,10},{9,17},{... | collective-permute-start | bytes 1966088 | tf_op jit(solution)/shard_map/ppermute | solution.py:39
  11.6 11.6 %collective-permute-start.1 = (bf16[1280,256]{1,0:T(8,128)(2,1)}, bf16[1280,256]{1,0:T(8,128)(2,1)S(1)}, u32[]{:S(2)}, u32[]{:S(2)}) collective-permute-start(bf16[1280,256]{1,0:T(8,128)(2,1)} %get-tuple-element.25.refs_0_), channel_id=1, source_target_pairs={{0,6},{1,25},{2,0},{3,27},{4,2},{5,29},{6,4},{7,31},{8,14},{9,1},{... | collective-permute-start | bytes 1966088 | tf_op jit(solution)/shard_map/ppermute | solution.py:39
  22.0 9.6 %collective-permute-start.2 = (bf16[640,256]{1,0:T(8,128)(2,1)}, bf16[640,256]{1,0:T(8,128)(2,1)}, u32[]{:S(2)}, u32[]{:S(2)}) collective-permute-start(bf16[640,256]{1,0:T(8,128)(2,1)} %slice.25), channel_id=1, source_target_pairs={{0,2},{1,9},{2,4},{3,11},{4,6},{5,13},{6,0},{7,15},{8,10},{9,17},{... | collective-permute-start | bytes 983048 | tf_op jit(solution)/shard_map/ppermute | solution.py:39
  24.1 8.1 %collective-permute-start.3 = (bf16[640,256]{1,0:T(8,128)(2,1)}, bf16[640,256]{1,0:T(8,128)(2,1)}, u32[]{:S(2)}, u32[]{:S(2)}) collective-permute-start(bf16[640,256]{1,0:T(8,128)(2,1)} %slice.26), channel_id=1, source_target_pairs={{0,6},{1,25},{2,0},{3,27},{4,2},{5,29},{6,4},{7,31},{8,14},{9,1},{... | collective-permute-start | bytes 983048 | tf_op jit(solution)/shard_map/ppermute | solution.py:39
  28.3 19.1 %collective-permute-start.4 = (bf16[2560,256]{1,0:T(8,128)(2,1)}, bf16[2560,256]{1,0:T(8,128)(2,1)S(1)}, u32[]{:S(2)}, u32[]{:S(2)}) collective-permute-start(bf16[2560,256]{1,0:T(8,128)(2,1)} %pack.4.refs_0_), channel_id=1, source_target_pairs={{0,8},{1,3},{2,10},{3,5},{4,12},{5,7},{6,14},{7,1},{8,16},{9,11},{... | collective-permute-start | bytes 3932168 | tf_op jit(solution)/shard_map/ppermute | solution.py:39
  28.5 18.9 %collective-permute-start.5 = (bf16[2560,256]{1,0:T(8,128)(2,1)}, bf16[2560,256]{1,0:T(8,128)(2,1)S(1)}, u32[]{:S(2)}, u32[]{:S(2)}) collective-permute-start(bf16[2560,256]{1,0:T(8,128)(2,1)} %pack.4.refs_0_), channel_id=1, source_target_pairs={{0,24},{1,7},{2,26},{3,1},{4,28},{5,3},{6,30},{7,5},{8,0},{9,15},{... | collective-permute-start | bytes 3932168 | tf_op jit(solution)/shard_map/ppermute | solution.py:39
  34.4 27.0 %collective-permute-start.6 = (bf16[2560,256]{1,0:T(8,128)(2,1)}, bf16[2560,256]{1,0:T(8,128)(2,1)S(1)}, u32[]{:S(2)}, u32[]{:S(2)}) collective-permute-start(bf16[2560,256]{1,0:T(8,128)(2,1)} %pack.5.refs_1_), channel_id=1, source_target_pairs={{0,8},{1,3},{2,10},{3,5},{4,12},{5,7},{6,14},{7,1},{8,16},{9,11},{... | collective-permute-start | bytes 3932168 | tf_op jit(solution)/shard_map/ppermute | solution.py:39
  37.3 25.2 %collective-permute-start.7 = (bf16[2560,256]{1,0:T(8,128)(2,1)}, bf16[2560,256]{1,0:T(8,128)(2,1)}, u32[]{:S(2)}, u32[]{:S(2)}) collective-permute-start(bf16[2560,256]{1,0:T(8,128)(2,1)} %pack.5.refs_1_), channel_id=1, source_target_pairs={{0,24},{1,7},{2,26},{3,1},{4,28},{5,3},{6,30},{7,5},{8,0},{9,15},{... | collective-permute-start | bytes 3932168 | tf_op jit(solution)/shard_map/ppermute | solution.py:39
  62.5 21.3 %collective-permute-start.8 = (bf16[2560,256]{1,0:T(8,128)(2,1)S(1)}, bf16[2560,256]{1,0:T(8,128)(2,1)}, u32[]{:S(2)}, u32[]{:S(2)}) collective-permute-start(bf16[2560,256]{1,0:T(8,128)(2,1)S(1)} %collective-permute-done.4.refs_2_), channel_id=1, source_target_pairs={{0,8},{1,3},{2,10},{3,5},{4,12},{5,7},{6,14},{7,1},{8,16},{9,11},{... | collective-permute-start | bytes 3932168 | tf_op jit(solution)/shard_map/ppermute | solution.py:39
  62.5 21.3 %collective-permute-start.9 = (bf16[2560,256]{1,0:T(8,128)(2,1)}, bf16[2560,256]{1,0:T(8,128)(2,1)}, u32[]{:S(2)}, u32[]{:S(2)}) collective-permute-start(bf16[2560,256]{1,0:T(8,128)(2,1)} %collective-permute-done.7.refs_5_), channel_id=1, source_target_pairs={{0,24},{1,7},{2,26},{3,1},{4,28},{5,3},{6,30},{7,5},{8,0},{9,15},{... | collective-permute-start | bytes 3932168 | tf_op jit(solution)/shard_map/ppermute | solution.py:39
  86.6 4.6 %collective-permute-start.10 = (bf16[4096,256]{1,0:T(8,128)(2,1)}, bf16[4096,256]{1,0:T(8,128)(2,1)S(1)}, u32[]{:S(2)}, u32[]{:S(2)}) collective-permute-start(bf16[4096,256]{1,0:T(8,128)(2,1)} %occ_tiles.1.own), channel_id=1, source_target_pairs={{0,1},{1,0},{2,3},{3,2},{4,5},{5,4},{6,7},{7,6},{8,9},{9,8},{10,11... | collective-permute-start | bytes 6291464 | tf_op jit(solution)/shard_map/ppermute | solution.py:43
  97.8 9.5 %collective-permute-start.11 = (bf16[1024,256]{1,0:T(8,128)(2,1)}, bf16[1024,256]{1,0:T(8,128)(2,1)S(1)}, u32[]{:S(2)}, u32[]{:S(2)}) collective-permute-start(bf16[1024,256]{1,0:T(8,128)(2,1)} %occ_first.1.refs_0_), channel_id=1, source_target_pairs={{0,2},{1,9},{2,4},{3,11},{4,6},{5,13},{6,0},{7,15},{8,10},{9,17},{... | collective-permute-start | bytes 1572872 | tf_op jit(solution)/shard_map/ppermute | solution.py:39
  99.4 9.5 %collective-permute-start.14 = (bf16[1024,256]{1,0:T(8,128)(2,1)}, bf16[1024,256]{1,0:T(8,128)(2,1)S(1)}, u32[]{:S(2)}, u32[]{:S(2)}) collective-permute-start(bf16[1024,256]{1,0:T(8,128)(2,1)} %occ_first.1.refs_0_), channel_id=1, source_target_pairs={{0,6},{1,25},{2,0},{3,27},{4,2},{5,29},{6,4},{7,31},{8,14},{9,1},{... | collective-permute-start | bytes 1572872 | tf_op jit(solution)/shard_map/ppermute | solution.py:39
  107.3 7.9 %collective-permute-start.15 = (bf16[512,256]{1,0:T(8,128)(2,1)S(1)}, bf16[512,256]{1,0:T(8,128)(2,1)S(1)}, u32[]{:S(2)}, u32[]{:S(2)}) collective-permute-start(bf16[512,256]{1,0:T(8,128)(2,1)S(1)} %slice.27), channel_id=1, source_target_pairs={{0,2},{1,9},{2,4},{3,11},{4,6},{5,13},{6,0},{7,15},{8,10},{9,17},{... | collective-permute-start | bytes 786440 | tf_op jit(solution)/shard_map/ppermute | solution.py:39
  108.9 6.4 %collective-permute-start.16 = (bf16[512,256]{1,0:T(8,128)(2,1)S(1)}, bf16[512,256]{1,0:T(8,128)(2,1)S(1)}, u32[]{:S(2)}, u32[]{:S(2)}) collective-permute-start(bf16[512,256]{1,0:T(8,128)(2,1)S(1)} %slice.28), channel_id=1, source_target_pairs={{0,6},{1,25},{2,0},{3,27},{4,2},{5,29},{6,4},{7,31},{8,14},{9,1},{... | collective-permute-start | bytes 786440 | tf_op jit(solution)/shard_map/ppermute | solution.py:39
  111.6 16.5 %collective-permute-start.12 = (bf16[2048,256]{1,0:T(8,128)(2,1)}, bf16[2048,256]{1,0:T(8,128)(2,1)S(1)}, u32[]{:S(2)}, u32[]{:S(2)}) collective-permute-start(bf16[2048,256]{1,0:T(8,128)(2,1)} %pack.6.refs_0_), channel_id=1, source_target_pairs={{0,8},{1,3},{2,10},{3,5},{4,12},{5,7},{6,14},{7,1},{8,16},{9,11},{... | collective-permute-start | bytes 3145736 | tf_op jit(solution)/shard_map/ppermute | solution.py:39
  113.2 15.1 %collective-permute-start.13 = (bf16[2048,256]{1,0:T(8,128)(2,1)}, bf16[2048,256]{1,0:T(8,128)(2,1)}, u32[]{:S(2)}, u32[]{:S(2)}) collective-permute-start(bf16[2048,256]{1,0:T(8,128)(2,1)} %pack.6.refs_0_), channel_id=1, source_target_pairs={{0,24},{1,7},{2,26},{3,1},{4,28},{5,3},{6,30},{7,5},{8,0},{9,15},{... | collective-permute-start | bytes 3145736 | tf_op jit(solution)/shard_map/ppermute | solution.py:39
  118.7 20.7 %collective-permute-start.17 = (bf16[2048,256]{1,0:T(8,128)(2,1)}, bf16[2048,256]{1,0:T(8,128)(2,1)S(1)}, u32[]{:S(2)}, u32[]{:S(2)}) collective-permute-start(bf16[2048,256]{1,0:T(8,128)(2,1)} %pack.7.refs_1_), channel_id=1, source_target_pairs={{0,8},{1,3},{2,10},{3,5},{4,12},{5,7},{6,14},{7,1},{8,16},{9,11},{... | collective-permute-start | bytes 3145736 | tf_op jit(solution)/shard_map/ppermute | solution.py:39
  120.2 20.1 %collective-permute-start.18 = (bf16[2048,256]{1,0:T(8,128)(2,1)}, bf16[2048,256]{1,0:T(8,128)(2,1)}, u32[]{:S(2)}, u32[]{:S(2)}) collective-permute-start(bf16[2048,256]{1,0:T(8,128)(2,1)} %pack.7.refs_1_), channel_id=1, source_target_pairs={{0,24},{1,7},{2,26},{3,1},{4,28},{5,3},{6,30},{7,5},{8,0},{9,15},{... | collective-permute-start | bytes 3145736 | tf_op jit(solution)/shard_map/ppermute | solution.py:39
  122.0 31.7 %collective-permute-start.21 = (bf16[4,512,256]{2,1,0:T(8,128)(2,1)S(1)}, bf16[4,512,256]{2,1,0:T(8,128)(2,1)S(1)}, u32[]{:S(2)}, u32[]{:S(2)}) collective-permute-start(bf16[4,512,256]{2,1,0:T(8,128)(2,1)S(1)} %copy-done.8), channel_id=1, source_target_pairs={{0,1},{1,0},{2,3},{3,2},{4,5},{5,4},{6,7},{7,6},{8,9},{9,8},{10,11... | collective-permute-start | bytes 3145736 | tf_op jit(solution)/shard_map/ppermute | solution.py:43
  140.3 16.1 %collective-permute-start.19 = (bf16[2048,256]{1,0:T(8,128)(2,1)S(1)}, bf16[2048,256]{1,0:T(8,128)(2,1)}, u32[]{:S(2)}, u32[]{:S(2)}) collective-permute-start(bf16[2048,256]{1,0:T(8,128)(2,1)S(1)} %collective-permute-done.12.refs_2_), channel_id=1, source_target_pairs={{0,8},{1,3},{2,10},{3,5},{4,12},{5,7},{6,14},{7,1},{8,16},{9,11},{... | collective-permute-start | bytes 3145736 | tf_op jit(solution)/shard_map/ppermute | solution.py:39
  141.0 15.5 %collective-permute-start.20 = (bf16[2048,256]{1,0:T(8,128)(2,1)}, bf16[2048,256]{1,0:T(8,128)(2,1)}, u32[]{:S(2)}, u32[]{:S(2)}) collective-permute-start(bf16[2048,256]{1,0:T(8,128)(2,1)} %collective-permute-done.18.refs_5_), channel_id=1, source_target_pairs={{0,24},{1,7},{2,26},{3,1},{4,28},{5,3},{6,30},{7,5},{8,0},{9,15},{... | collective-permute-start | bytes 3145736 | tf_op jit(solution)/shard_map/ppermute | solution.py:39
  (14 other events, 111.4 us)
Sparse Core Ops, SparseCore 0:
  10.1 68.7 all-gather.2
  91.4 54.0 all-gather.4

commit v5 on v4

--- a/solution.py
+++ b/solution.py
@@ -17,6 +17,7 @@
 F32 = jnp.float32
 BF16 = jnp.bfloat16
 HBM = pl.BlockSpec(memory_space=pltpu.HBM)
+ANY = pl.BlockSpec(memory_space=pl.ANY)
 PARAMS = pltpu.CompilerParams(vmem_limit_bytes=60 * 1024 * 1024)
 
 
@@ -107,13 +108,13 @@
     return pl.pallas_call(
         functools.partial(pack_kernel, moves, len(sources)),
         out_shape=tuple(jax.ShapeDtypeStruct((rows, COLS), BF16) for rows in out_rows),
-        in_specs=[HBM] * len(sources),
+        in_specs=[ANY] * len(sources),
         out_specs=(HBM,) * len(out_rows),
         scratch_shapes=[
             pltpu.VMEM((sum(move[2] for move in moves), COLS), BF16),
             pltpu.SemaphoreType.DMA((2, len(moves))),
         ],
-        compiler_params=PARAMS,
+        compiler_params=pltpu.CompilerParams(vmem_limit_bytes=8 * 1024 * 1024),
         cost_estimate=pl.CostEstimate(flops=0, bytes_accessed=4 << 20, transcendentals=0),
         name="pack",
     )(*sources)
@@ -192,14 +193,14 @@
     return tile_y * 4 + tile_x
 
 
-def call(kernel, name, operands, outs, scratch, sems, flops):
+def call(kernel, name, operands, outs, scratch, sems, flops, vmem):
     return pl.pallas_call(
         kernel,
         out_shape=outs,
         in_specs=[HBM] * len(operands),
         out_specs=jax.tree.map(lambda _: HBM, outs),
         scratch_shapes=scratch + [pltpu.SemaphoreType.DMA((sems,))],
-        compiler_params=PARAMS,
+        compiler_params=pltpu.CompilerParams(vmem_limit_bytes=vmem * 1024 * 1024),
         cost_estimate=pl.CostEstimate(flops=flops, bytes_accessed=9 << 20, transcendentals=0),
         name=name,
     )(*operands)
@@ -232,7 +233,7 @@
 def occ_tiles(pieces):
     return call(
         occ_kernel, "occ_tiles", pieces, jax.ShapeDtypeStruct((16 * HALF, COLS), BF16),
-        [pltpu.VMEM((16, *TILE), BF16)], 32, 0,
+        [pltpu.VMEM((16, *TILE), BF16)], 32, 0, 60,
     )
 
 
@@ -273,7 +274,7 @@
     scratch = [pltpu.VMEM((2 * n, *SUM), BF16), pltpu.VMEM((2 * n, *TILE), BF16), pltpu.VMEM(SUM, F32), pltpu.VMEM(SUM, dtype)]
     return call(
         functools.partial(plane_kernel, arrays, rows), name, (gathered, *pieces),
-        jax.ShapeDtypeStruct(SUM, dtype), scratch, 4 * n, 2 << 30,
+        jax.ShapeDtypeStruct(SUM, dtype), scratch, 4 * n, 2 << 30, 51,
     )
 
 
@@ -290,7 +291,7 @@
     scratch = [pltpu.VMEM((4, *SUM), BF16), pltpu.VMEM((4, *TILE), BF16), pltpu.VMEM(SUM, F32), pltpu.VMEM(SUM, BF16)]
     return call(
         functools.partial(plane_last_kernel, rows), "plane_last", (gathered, *pieces, sum_in),
-        jax.ShapeDtypeStruct(SUM, BF16), scratch, 9, 1 << 29,
+        jax.ShapeDtypeStruct(SUM, BF16), scratch, 9, 1 << 29, 60,
     )
 
 
@@ -331,7 +332,7 @@
     ]
     return call(
         functools.partial(ring_kernel, stride, gap, per_chip), name, (own, other, gathered),
-        jax.ShapeDtypeStruct(SUM, BF16), scratch, 48, 2 << 30,
+        jax.ShapeDtypeStruct(SUM, BF16), scratch, 48, 2 << 30, 60 if per_chip else 60,
     )
 
 
@@ -391,7 +392,7 @@
     scratch = [pltpu.VMEM((4, *SUM), BF16), pltpu.VMEM((4, *TILE), BF16), pltpu.VMEM(SUM, F32)]
     scratch += [pltpu.VMEM((2 * AUX, ROWS, COLS), BF16)] + buffers_of(outs)
     operands = (gathered, *pieces, plane_sum, ring_part, own_aux, other_aux)
-    return call(polar_kernel, "polar_product", operands, outs, scratch, 12, 1 << 29)
+    return call(polar_kernel, "polar_product", operands, outs, scratch, 12, 1 << 29, 60)
 
 
 def body(integrals, density_occ, density_virt, mask_int, mask_occ, mask_virt):

time: 195 us -> 189 us (0.969)
  Pallas kernels: 42.5 us -> 33.8 us
  waiting for transfers between devices: 73.5 us -> 80.2 us
  blocking collectives: 25.5 us -> 22.4 us
  local copies, waits for them, and re-layouts: 7.06 us -> 4.65 us
    pallas_call x4, Pallas kernels: 8.56 us -> 2.12 us  [pack(): pl.pallas_call(functools.partial(pack_kernel, moves, len(sources)), out_s...]
    all_gather x1, waiting for transfers between devices: 13.1 us -> 17 us  [body(): gathered = lax.all_gather(ring_aux, ('row', 'layer'), axis=0, tiled=True)]
    all_to_all x1, blocking collectives: 25.5 us -> 22.4 us  [body(): shares = lax.all_to_all(chi.reshape(128, 1, BLK), ('row', 'col'), 0, 0)]
    ppermute x20, waiting for transfers between devices: 59.5 us -> 62.4 us  [plane_move(): return lax.ppermute(value, ('col', 'layer'), plane_perm(shift, first))]
    pallas_call x7, Pallas kernels: 31.2 us -> 28.9 us  [call(): pl.pallas_call(kernel, out_shape=outs, in_specs=[HBM] * len(operands), ou...]
    unnamed x28 -> x30, local copies, waits for them, and re-layouts: 4.72 us -> 3.91 us
  transfers between devices with their start and end apart: 24 -> 24, of which waited for: 12 -> 16; matrix products, arithmetic and copies ran while one was open for 1% -> 0% of each run, Pallas kernels for 17% -> 12%
where the time goes in v5:
time: 189 us
  waiting for transfers between devices  80.2 us (42%)
  Pallas kernels  33.8 us (18%)
  starting transfers between devices  33.2 us (18%)
  blocking collectives  22.4 us (12%)
  between operations  14.3 us (8%)
  local copies, waits for them, and re-layouts  4.65 us (2%)
    ppermute x20, waiting for transfers between devices, plane_move(): return lax.ppermute(value, ('col', 'layer'), plane_perm(shift, first))  62.4 us
    ppermute x20, starting transfers between devices, plane_move(): return lax.ppermute(value, ('col', 'layer'), plane_perm(shift, first))  32.6 us
    pallas_call x7, Pallas kernels, call(): pl.pallas_call(kernel, out_shape=outs, in_specs=[HBM] * len(operands), ou...  28.9 us
    all_to_all x1, blocking collectives, body(): shares = lax.all_to_all(chi.reshape(128, 1, BLK), ('row', 'col'), 0, 0)  22.4 us
    all_gather x1, waiting for transfers between devices, body(): gathered = lax.all_gather(ring_aux, ('row', 'layer'), axis=0, tiled=True)  17 us
    unnamed x30, local copies, waits for them, and re-layouts  3.91 us
  transfers between devices with their start and end apart: 24, of which 16 were waited for; matrix products, arithmetic and copies ran while one was open for 0% of the time, Pallas kernels for 12%

profile of v5, /device:TPU:2, one launch (start us, length us, event | category | flops | bytes accessed | tf_op | source)
XLA Modules:
  0.0 188.7 jit_solution(14526093355595283596)
XLA Ops:
  7.2 2.7 %mask_inputs.1 = (bf16[1280,256]{1,0:T(8,128)(2,1)}, bf16[1280,256]{1,0:T(8,128)(2,1)}, bf16[4,512,256]{2,1,0:T(8,128)(2,1)}) custom-call(s32[4,2,4]{2,1,0:T(2,128)} %bitcast.9, s32[2,4]{1,0:T(2,128)} %bitcast.10, s32[2,4]{1,0:T(2,128)} %bitcast.11, bf16[4,512,256]{2,1,0:T(8,128)(2,1)} %integrals.1, bf16[512,256]{1,0:T(8,128)(2,1)} %occ.1, bf16[512,256]{1,0:T(8,128)(2,1)} %virt.1), custom_call_target="tpu_custom_call" | custom-call | tf_op jit(solution)/shard_map/mask_inputs/pallas_call | solution.py:173
  12.5 8.7 %collective-permute-done.refs_1_ = bf16[1280,256]{1,0:T(8,128)(2,1)S(1)} collective-permute-done((bf16[1280,256]{1,0:T(8,128)(2,1)}, bf16[1280,256]{1,0:T(8,128)(2,1)S(1)}, u32[]{:S(2)}, u32[]{:S(2)}) %collective-permute-start) | collective-permute-done | bytes 655392 | tf_op jit(solution)/shard_map/ppermute | solution.py:40
  22.5 2.1 %collective-permute-start.3 = (bf16[640,256]{1,0:T(8,128)(2,1)S(1)}, bf16[640,256]{1,0:T(8,128)(2,1)S(1)}, u32[]{:S(2)}, u32[]{:S(2)}) collective-permute-start(bf16[640,256]{1,0:T(8,128)(2,1)S(1)} %slice.26), channel_id=1, source_target_pairs={{0,6},{1,25},{2,0},{3,27},{4,2},{5,29},{6,4},{7,31},{8,14},{9,1},{... | collective-permute-start | bytes 983048 | tf_op jit(solution)/shard_map/ppermute | solution.py:40
  25.7 3.1 %collective-permute-start.5 = (bf16[2560,256]{1,0:T(8,128)(2,1)S(1)}, bf16[2560,256]{1,0:T(8,128)(2,1)S(1)}, u32[]{:S(2)}, u32[]{:S(2)}) collective-permute-start(bf16[2560,256]{1,0:T(8,128)(2,1)S(1)} %pack.4.refs_0_), channel_id=1, source_target_pairs={{0,24},{1,7},{2,26},{3,1},{4,28},{5,3},{6,30},{7,5},{8,0},{9,15},{... | collective-permute-start | bytes 3932168 | tf_op jit(solution)/shard_map/ppermute | solution.py:40
  28.8 2.9 %collective-permute-done.2.refs_1_ = bf16[640,256]{1,0:T(8,128)(2,1)S(1)} collective-permute-done((bf16[640,256]{1,0:T(8,128)(2,1)S(1)}, bf16[640,256]{1,0:T(8,128)(2,1)S(1)}, u32[]{:S(2)}, u32[]{:S(2)}) %collective-permute-start.2) | collective-permute-done | bytes 327712 | tf_op jit(solution)/shard_map/ppermute | solution.py:40
  32.8 2.8 %collective-permute-start.6 = (bf16[2560,256]{1,0:T(8,128)(2,1)S(1)}, bf16[2560,256]{1,0:T(8,128)(2,1)S(1)}, u32[]{:S(2)}, u32[]{:S(2)}) collective-permute-start(bf16[2560,256]{1,0:T(8,128)(2,1)S(1)} %pack.5.refs_1_), channel_id=1, source_target_pairs={{0,8},{1,3},{2,10},{3,5},{4,12},{5,7},{6,14},{7,1},{8,16},{9,11},{... | collective-permute-start | bytes 3932168 | tf_op jit(solution)/shard_map/ppermute | solution.py:40
  37.1 7.4 %collective-permute-done.4.refs_2_ = bf16[2560,256]{1,0:T(8,128)(2,1)} collective-permute-done((bf16[2560,256]{1,0:T(8,128)(2,1)S(1)}, bf16[2560,256]{1,0:T(8,128)(2,1)}, u32[]{:S(2)}, u32[]{:S(2)}) %collective-permute-start.4) | collective-permute-done | bytes 1310752 | tf_op jit(solution)/shard_map/ppermute | solution.py:40
  44.5 13.9 %collective-permute-done.6.refs_4_ = bf16[2560,256]{1,0:T(8,128)(2,1)S(1)} collective-permute-done((bf16[2560,256]{1,0:T(8,128)(2,1)S(1)}, bf16[2560,256]{1,0:T(8,128)(2,1)S(1)}, u32[]{:S(2)}, u32[]{:S(2)}) %collective-permute-start.6) | collective-permute-done | bytes 1310752 | tf_op jit(solution)/shard_map/ppermute | solution.py:40
  59.6 2.3 %collective-permute-start.9 = (bf16[2560,256]{1,0:T(8,128)(2,1)}, bf16[2560,256]{1,0:T(8,128)(2,1)}, u32[]{:S(2)}, u32[]{:S(2)}) collective-permute-start(bf16[2560,256]{1,0:T(8,128)(2,1)} %collective-permute-done.7.refs_5_), channel_id=1, source_target_pairs={{0,24},{1,7},{2,26},{3,1},{4,28},{5,3},{6,30},{7,5},{8,0},{9,15},{... | collective-permute-start | bytes 3932168 | tf_op jit(solution)/shard_map/ppermute | solution.py:40
  61.9 17.0 %all-gather.3.cloned.1.call-done.gathered = bf16[20480,256]{1,0:T(8,128)(2,1)} async-done(((bf16[1280,256]{1,0:T(8,128)(2,1)}), bf16[20480,256]{1,0:T(8,128)(2,1)}) %all-gather.3.cloned.1.call-update) | async-done | bytes 10485776 | tf_op jit(solution)/shard_map/all_gather | solution.py:402
  78.9 3.8 %plane_near.2.sum_in = f32[1024,256]{1,0:T(8,128)S(1)} custom-call(bf16[20480,256]{1,0:T(8,128)(2,1)} %all-gather.3.cloned.1.call-done.gathered, bf16[2560,256]{1,0:T(8,128)(2,1)S(1)} %pack.4.refs_0_, bf16[2560,256]{1,0:T(8,128)(2,1)} %copy-done.1, bf16[2560,256]{1,0:T(8,128)(2,1)} %collective-permute-done.4.refs_2_, bf16[2560,256]{1,0:T(8,128)(2,1)} %copy-done.8, ...), custom_call_target="tpu_custom_call" | custom-call | flops 2147483648 | bytes 9437184 | tf_op jit(solution)/shard_map/plane_near/pallas_call | solution.py:197
  83.7 2.6 %occ_tiles.1.own = bf16[4096,256]{1,0:T(8,128)(2,1)} custom-call(bf16[2560,256]{1,0:T(8,128)(2,1)} %copy-done, bf16[2560,256]{1,0:T(8,128)(2,1)} %copy-done.1, bf16[2560,256]{1,0:T(8,128)(2,1)} %collective-permute-done.4.refs_2_, bf16[2560,256]{1,0:T(8,128)(2,1)} %copy-done.8, bf16[2560,256]{1,0:T(8,128)(2,1)} %copy-done.9, ...), custom_call_target="tpu_custom_call" | custom-call | bytes 9437184 | tf_op jit(solution)/shard_map/occ_tiles/pallas_call | solution.py:197
  86.9 3.3 %plane_last.1 = bf16[1024,256]{1,0:T(8,128)(2,1)} custom-call(bf16[20480,256]{1,0:T(8,128)(2,1)} %all-gather.3.cloned.1.call-done.gathered, bf16[2560,256]{1,0:T(8,128)(2,1)} %collective-permute-done.8.refs_6_.top, bf16[2560,256]{1,0:T(8,128)(2,1)} %collective-permute-done.9.refs_7_.bottom, f32[1024,256]{1,0:T(8,128)} %copy-done.2), custom_call_target="tpu_custom_call" | custom-call | flops 536870912 | bytes 9437184 | tf_op jit(solution)/shard_map/plane_last/pallas_call | solution.py:197
  92.4 5.3 %occ_first.1.refs_0_ = bf16[1024,256]{1,0:T(8,128)(2,1)} custom-call(bf16[4096,256]{1,0:T(8,128)(2,1)} %occ_tiles.1.own, bf16[4096,256]{1,0:T(8,128)(2,1)} %copy-done.7, bf16[20480,256]{1,0:T(8,128)(2,1)} %all-gather.3.cloned.1.call-done.gathered), custom_call_target="tpu_custom_call" | custom-call | flops 2147483648 | bytes 9437184 | tf_op jit(solution)/shard_map/occ_first/pallas_call | solution.py:197
  99.8 7.4 %collective-permute-done.11.refs_1_ = bf16[1024,256]{1,0:T(8,128)(2,1)S(1)} collective-permute-done((bf16[1024,256]{1,0:T(8,128)(2,1)}, bf16[1024,256]{1,0:T(8,128)(2,1)S(1)}, u32[]{:S(2)}, u32[]{:S(2)}) %collective-permute-start.11) | collective-permute-done | bytes 524320 | tf_op jit(solution)/shard_map/ppermute | solution.py:40
  113.6 1.9 %collective-permute-done.16.refs_2_ = bf16[512,256]{1,0:T(8,128)(2,1)S(1)} collective-permute-done((bf16[512,256]{1,0:T(8,128)(2,1)S(1)}, bf16[512,256]{1,0:T(8,128)(2,1)S(1)}, u32[]{:S(2)}, u32[]{:S(2)}) %collective-permute-start.16) | collective-permute-done | bytes 262176 | tf_op jit(solution)/shard_map/ppermute | solution.py:40
  115.7 3.9 %collective-permute-start.17 = (bf16[2048,256]{1,0:T(8,128)(2,1)S(1)}, bf16[2048,256]{1,0:T(8,128)(2,1)S(1)}, u32[]{:S(2)}, u32[]{:S(2)}) collective-permute-start(bf16[2048,256]{1,0:T(8,128)(2,1)S(1)} %pack.7.refs_1_), channel_id=1, source_target_pairs={{0,8},{1,3},{2,10},{3,5},{4,12},{5,7},{6,14},{7,1},{8,16},{9,11},{... | collective-permute-start | bytes 3145736 | tf_op jit(solution)/shard_map/ppermute | solution.py:40
  121.1 4.7 %collective-permute-done.12.refs_2_ = bf16[2048,256]{1,0:T(8,128)(2,1)S(1)} collective-permute-done((bf16[2048,256]{1,0:T(8,128)(2,1)S(1)}, bf16[2048,256]{1,0:T(8,128)(2,1)S(1)}, u32[]{:S(2)}, u32[]{:S(2)}) %collective-permute-start.12) | collective-permute-done | bytes 1048608 | tf_op jit(solution)/shard_map/ppermute | solution.py:40
  125.9 11.2 %collective-permute-done.17.refs_4_ = bf16[2048,256]{1,0:T(8,128)(2,1)S(1)} collective-permute-done((bf16[2048,256]{1,0:T(8,128)(2,1)S(1)}, bf16[2048,256]{1,0:T(8,128)(2,1)S(1)}, u32[]{:S(2)}, u32[]{:S(2)}) %collective-permute-start.17) | collective-permute-done | bytes 1048608 | tf_op jit(solution)/shard_map/ppermute | solution.py:40
  140.5 3.8 %plane_near.3.plane_sum = f32[1024,256]{1,0:T(8,128)S(1)} custom-call(bf16[20480,256]{1,0:T(8,128)(2,1)} %all-gather.3.cloned.1.call-done.gathered, bf16[2048,256]{1,0:T(8,128)(2,1)S(1)} %pack.6.refs_0_, bf16[2048,256]{1,0:T(8,128)(2,1)} %copy-done.4, bf16[2048,256]{1,0:T(8,128)(2,1)} %copy-done.11, bf16[2048,256]{1,0:T(8,128)(2,1)} %copy-done.13, ...), custom_call_target="tpu_custom_call" | custom-call | flops 2147483648 | bytes 9437184 | tf_op jit(solution)/shard_map/plane_near/pallas_call | solution.py:197
  145.3 5.3 %polar_ring.1.ring_part = bf16[1024,256]{1,0:T(8,128)(2,1)} custom-call(bf16[4096,256]{1,0:T(8,128)(2,1)} %occ_tiles.1.own, bf16[4096,256]{1,0:T(8,128)(2,1)} %copy-done.7, bf16[8192,256]{1,0:T(8,128)(2,1)} %all-gather.5.cloned.1.call-done.gathered), custom_call_target="tpu_custom_call" | custom-call | flops 2147483648 | bytes 9437184 | tf_op jit(solution)/shard_map/polar_ring/pallas_call | solution.py:197
  150.6 2.7 %collective-permute-done.19.top = bf16[2048,256]{1,0:T(8,128)(2,1)} collective-permute-done((bf16[2048,256]{1,0:T(8,128)(2,1)S(1)}, bf16[2048,256]{1,0:T(8,128)(2,1)}, u32[]{:S(2)}, u32[]{:S(2)}) %collective-permute-start.19) | collective-permute-done | bytes 1048608 | tf_op jit(solution)/shard_map/ppermute | solution.py:40
  153.8 4.9 %polar_product.1 = (bf16[2048,256]{1,0:T(8,128)(2,1)}, f32[128,128]{1,0:T(8,128)}) custom-call(bf16[20480,256]{1,0:T(8,128)(2,1)} %all-gather.3.cloned.1.call-done.gathered, bf16[2048,256]{1,0:T(8,128)(2,1)} %collective-permute-done.19.top, bf16[2048,256]{1,0:T(8,128)(2,1)} %collective-permute-done.20.bottom, f32[1024,256]{1,0:T(8,128)} %copy-done.3, ...), custom_call_target="tpu_custom_call" | custom-call | flops 536870912 | bytes 9437184 | tf_op jit(solution)/shard_map/polar_product/pallas_call | solution.py:197
  158.7 22.4 %all_to_all.5 = f32[128,1,128]{2,1,0:T(1,128)S(1)} all-to-all(f32[128,1,128]{2,1,0:T(1,128)} %bitcast.8), channel_id=1, replica_groups=mesh['row'=8,'col'=16,'layer'=2] {'row','col'}, dimensions={0} | all-to-all | bytes 131072 | tf_op jit(solution)/shard_map/all_to_all | solution.py:420
  (76 shorter events, 28.3 us)
Async XLA Ops:
  7.2 71.7 %all-gather.3.cloned.1.call-start = ((), (), s32[]{:S(2)}) async-start(), calls=%async_computation.1 | async-start | bytes 11141120 | tf_op jit(solution)/shard_map/all_gather | solution.py:402
  10.0 135.3 %all-gather.5.cloned.1.call-start = ((), (), s32[]{:S(2)}) async-start(), calls=%async_computation.2 | async-start | bytes 4718592 | tf_op jit(solution)/shard_map/all_gather | solution.py:412
  10.0 11.1 %collective-permute-start = (bf16[1280,256]{1,0:T(8,128)(2,1)}, bf16[1280,256]{1,0:T(8,128)(2,1)S(1)}, u32[]{:S(2)}, u32[]{:S(2)}) collective-permute-start(bf16[1280,256]{1,0:T(8,128)(2,1)} %get-tuple-element.25.refs_0_), channel_id=1, source_target_pairs={{0,2},{1,9},{2,4},{3,11},{4,6},{5,13},{6,0},{7,15},{8,10},{9,17},{... | collective-permute-start | bytes 1966088 | tf_op jit(solution)/shard_map/ppermute | solution.py:40
  11.6 10.9 %collective-permute-start.1 = (bf16[1280,256]{1,0:T(8,128)(2,1)}, bf16[1280,256]{1,0:T(8,128)(2,1)S(1)}, u32[]{:S(2)}, u32[]{:S(2)}) collective-permute-start(bf16[1280,256]{1,0:T(8,128)(2,1)} %get-tuple-element.25.refs_0_), channel_id=1, source_target_pairs={{0,6},{1,25},{2,0},{3,27},{4,2},{5,29},{6,4},{7,31},{8,14},{9,1},{... | collective-permute-start | bytes 1966088 | tf_op jit(solution)/shard_map/ppermute | solution.py:40
  21.2 10.6 %collective-permute-start.2 = (bf16[640,256]{1,0:T(8,128)(2,1)S(1)}, bf16[640,256]{1,0:T(8,128)(2,1)S(1)}, u32[]{:S(2)}, u32[]{:S(2)}) collective-permute-start(bf16[640,256]{1,0:T(8,128)(2,1)S(1)} %slice.25), channel_id=1, source_target_pairs={{0,2},{1,9},{2,4},{3,11},{4,6},{5,13},{6,0},{7,15},{8,10},{9,17},{... | collective-permute-start | bytes 983048 | tf_op jit(solution)/shard_map/ppermute | solution.py:40
  22.5 9.4 %collective-permute-start.3 = (bf16[640,256]{1,0:T(8,128)(2,1)S(1)}, bf16[640,256]{1,0:T(8,128)(2,1)S(1)}, u32[]{:S(2)}, u32[]{:S(2)}) collective-permute-start(bf16[640,256]{1,0:T(8,128)(2,1)S(1)} %slice.26), channel_id=1, source_target_pairs={{0,6},{1,25},{2,0},{3,27},{4,2},{5,29},{6,4},{7,31},{8,14},{9,1},{... | collective-permute-start | bytes 983048 | tf_op jit(solution)/shard_map/ppermute | solution.py:40
  25.5 19.0 %collective-permute-start.4 = (bf16[2560,256]{1,0:T(8,128)(2,1)S(1)}, bf16[2560,256]{1,0:T(8,128)(2,1)}, u32[]{:S(2)}, u32[]{:S(2)}) collective-permute-start(bf16[2560,256]{1,0:T(8,128)(2,1)S(1)} %pack.4.refs_0_), channel_id=1, source_target_pairs={{0,8},{1,3},{2,10},{3,5},{4,12},{5,7},{6,14},{7,1},{8,16},{9,11},{... | collective-permute-start | bytes 3932168 | tf_op jit(solution)/shard_map/ppermute | solution.py:40
  25.7 18.8 %collective-permute-start.5 = (bf16[2560,256]{1,0:T(8,128)(2,1)S(1)}, bf16[2560,256]{1,0:T(8,128)(2,1)S(1)}, u32[]{:S(2)}, u32[]{:S(2)}) collective-permute-start(bf16[2560,256]{1,0:T(8,128)(2,1)S(1)} %pack.4.refs_0_), channel_id=1, source_target_pairs={{0,24},{1,7},{2,26},{3,1},{4,28},{5,3},{6,30},{7,5},{8,0},{9,15},{... | collective-permute-start | bytes 3932168 | tf_op jit(solution)/shard_map/ppermute | solution.py:40
  32.8 25.7 %collective-permute-start.6 = (bf16[2560,256]{1,0:T(8,128)(2,1)S(1)}, bf16[2560,256]{1,0:T(8,128)(2,1)S(1)}, u32[]{:S(2)}, u32[]{:S(2)}) collective-permute-start(bf16[2560,256]{1,0:T(8,128)(2,1)S(1)} %pack.5.refs_1_), channel_id=1, source_target_pairs={{0,8},{1,3},{2,10},{3,5},{4,12},{5,7},{6,14},{7,1},{8,16},{9,11},{... | collective-permute-start | bytes 3932168 | tf_op jit(solution)/shard_map/ppermute | solution.py:40
  35.6 22.9 %collective-permute-start.7 = (bf16[2560,256]{1,0:T(8,128)(2,1)S(1)}, bf16[2560,256]{1,0:T(8,128)(2,1)}, u32[]{:S(2)}, u32[]{:S(2)}) collective-permute-start(bf16[2560,256]{1,0:T(8,128)(2,1)S(1)} %pack.5.refs_1_), channel_id=1, source_target_pairs={{0,24},{1,7},{2,26},{3,1},{4,28},{5,3},{6,30},{7,5},{8,0},{9,15},{... | collective-permute-start | bytes 3932168 | tf_op jit(solution)/shard_map/ppermute | solution.py:40
  58.5 25.2 %collective-permute-start.8 = (bf16[2560,256]{1,0:T(8,128)(2,1)}, bf16[2560,256]{1,0:T(8,128)(2,1)}, u32[]{:S(2)}, u32[]{:S(2)}) collective-permute-start(bf16[2560,256]{1,0:T(8,128)(2,1)} %collective-permute-done.4.refs_2_), channel_id=1, source_target_pairs={{0,8},{1,3},{2,10},{3,5},{4,12},{5,7},{6,14},{7,1},{8,16},{9,11},{... | collective-permute-start | bytes 3932168 | tf_op jit(solution)/shard_map/ppermute | solution.py:40
  59.6 24.1 %collective-permute-start.9 = (bf16[2560,256]{1,0:T(8,128)(2,1)}, bf16[2560,256]{1,0:T(8,128)(2,1)}, u32[]{:S(2)}, u32[]{:S(2)}) collective-permute-start(bf16[2560,256]{1,0:T(8,128)(2,1)} %collective-permute-done.7.refs_5_), channel_id=1, source_target_pairs={{0,24},{1,7},{2,26},{3,1},{4,28},{5,3},{6,30},{7,5},{8,0},{9,15},{... | collective-permute-start | bytes 3932168 | tf_op jit(solution)/shard_map/ppermute | solution.py:40
  86.3 4.6 %collective-permute-start.10 = (bf16[4096,256]{1,0:T(8,128)(2,1)}, bf16[4096,256]{1,0:T(8,128)(2,1)S(1)}, u32[]{:S(2)}, u32[]{:S(2)}) collective-permute-start(bf16[4096,256]{1,0:T(8,128)(2,1)} %occ_tiles.1.own), channel_id=1, source_target_pairs={{0,1},{1,0},{2,3},{3,2},{4,5},{5,4},{6,7},{7,6},{8,9},{9,8},{10,11... | collective-permute-start | bytes 6291464 | tf_op jit(solution)/shard_map/ppermute | solution.py:44
  97.6 9.5 %collective-permute-start.11 = (bf16[1024,256]{1,0:T(8,128)(2,1)}, bf16[1024,256]{1,0:T(8,128)(2,1)S(1)}, u32[]{:S(2)}, u32[]{:S(2)}) collective-permute-start(bf16[1024,256]{1,0:T(8,128)(2,1)} %occ_first.1.refs_0_), channel_id=1, source_target_pairs={{0,2},{1,9},{2,4},{3,11},{4,6},{5,13},{6,0},{7,15},{8,10},{9,17},{... | collective-permute-start | bytes 1572872 | tf_op jit(solution)/shard_map/ppermute | solution.py:40
  99.2 9.5 %collective-permute-start.14 = (bf16[1024,256]{1,0:T(8,128)(2,1)}, bf16[1024,256]{1,0:T(8,128)(2,1)S(1)}, u32[]{:S(2)}, u32[]{:S(2)}) collective-permute-start(bf16[1024,256]{1,0:T(8,128)(2,1)} %occ_first.1.refs_0_), channel_id=1, source_target_pairs={{0,6},{1,25},{2,0},{3,27},{4,2},{5,29},{6,4},{7,31},{8,14},{9,1},{... | collective-permute-start | bytes 1572872 | tf_op jit(solution)/shard_map/ppermute | solution.py:40
  107.1 6.4 %collective-permute-start.15 = (bf16[512,256]{1,0:T(8,128)(2,1)S(1)}, bf16[512,256]{1,0:T(8,128)(2,1)S(1)}, u32[]{:S(2)}, u32[]{:S(2)}) collective-permute-start(bf16[512,256]{1,0:T(8,128)(2,1)S(1)} %slice.27), channel_id=1, source_target_pairs={{0,2},{1,9},{2,4},{3,11},{4,6},{5,13},{6,0},{7,15},{8,10},{9,17},{... | collective-permute-start | bytes 786440 | tf_op jit(solution)/shard_map/ppermute | solution.py:40
  108.7 6.8 %collective-permute-start.16 = (bf16[512,256]{1,0:T(8,128)(2,1)S(1)}, bf16[512,256]{1,0:T(8,128)(2,1)S(1)}, u32[]{:S(2)}, u32[]{:S(2)}) collective-permute-start(bf16[512,256]{1,0:T(8,128)(2,1)S(1)} %slice.28), channel_id=1, source_target_pairs={{0,6},{1,25},{2,0},{3,27},{4,2},{5,29},{6,4},{7,31},{8,14},{9,1},{... | collective-permute-start | bytes 786440 | tf_op jit(solution)/shard_map/ppermute | solution.py:40
  109.5 16.2 %collective-permute-start.12 = (bf16[2048,256]{1,0:T(8,128)(2,1)S(1)}, bf16[2048,256]{1,0:T(8,128)(2,1)S(1)}, u32[]{:S(2)}, u32[]{:S(2)}) collective-permute-start(bf16[2048,256]{1,0:T(8,128)(2,1)S(1)} %pack.6.refs_0_), channel_id=1, source_target_pairs={{0,8},{1,3},{2,10},{3,5},{4,12},{5,7},{6,14},{7,1},{8,16},{9,11},{... | collective-permute-start | bytes 3145736 | tf_op jit(solution)/shard_map/ppermute | solution.py:40
  111.1 14.8 %collective-permute-start.13 = (bf16[2048,256]{1,0:T(8,128)(2,1)S(1)}, bf16[2048,256]{1,0:T(8,128)(2,1)S(1)}, u32[]{:S(2)}, u32[]{:S(2)}) collective-permute-start(bf16[2048,256]{1,0:T(8,128)(2,1)S(1)} %pack.6.refs_0_), channel_id=1, source_target_pairs={{0,24},{1,7},{2,26},{3,1},{4,28},{5,3},{6,30},{7,5},{8,0},{9,15},{... | collective-permute-start | bytes 3145736 | tf_op jit(solution)/shard_map/ppermute | solution.py:40
  115.7 21.3 %collective-permute-start.17 = (bf16[2048,256]{1,0:T(8,128)(2,1)S(1)}, bf16[2048,256]{1,0:T(8,128)(2,1)S(1)}, u32[]{:S(2)}, u32[]{:S(2)}) collective-permute-start(bf16[2048,256]{1,0:T(8,128)(2,1)S(1)} %pack.7.refs_1_), channel_id=1, source_target_pairs={{0,8},{1,3},{2,10},{3,5},{4,12},{5,7},{6,14},{7,1},{8,16},{9,11},{... | collective-permute-start | bytes 3145736 | tf_op jit(solution)/shard_map/ppermute | solution.py:40
  119.6 17.6 %collective-permute-start.18 = (bf16[2048,256]{1,0:T(8,128)(2,1)S(1)}, bf16[2048,256]{1,0:T(8,128)(2,1)}, u32[]{:S(2)}, u32[]{:S(2)}) collective-permute-start(bf16[2048,256]{1,0:T(8,128)(2,1)S(1)} %pack.7.refs_1_), channel_id=1, source_target_pairs={{0,24},{1,7},{2,26},{3,1},{4,28},{5,3},{6,30},{7,5},{8,0},{9,15},{... | collective-permute-start | bytes 3145736 | tf_op jit(solution)/shard_map/ppermute | solution.py:40
  121.1 29.5 %collective-permute-start.21 = (bf16[4,512,256]{2,1,0:T(8,128)(2,1)S(1)}, bf16[4,512,256]{2,1,0:T(8,128)(2,1)S(1)}, u32[]{:S(2)}, u32[]{:S(2)}) collective-permute-start(bf16[4,512,256]{2,1,0:T(8,128)(2,1)S(1)} %copy-done.10), channel_id=1, source_target_pairs={{0,1},{1,0},{2,3},{3,2},{4,5},{5,4},{6,7},{7,6},{8,9},{9,8},{10,11... | collective-permute-start | bytes 3145736 | tf_op jit(solution)/shard_map/ppermute | solution.py:44
  137.2 16.1 %collective-permute-start.19 = (bf16[2048,256]{1,0:T(8,128)(2,1)S(1)}, bf16[2048,256]{1,0:T(8,128)(2,1)}, u32[]{:S(2)}, u32[]{:S(2)}) collective-permute-start(bf16[2048,256]{1,0:T(8,128)(2,1)S(1)} %collective-permute-done.12.refs_2_), channel_id=1, source_target_pairs={{0,8},{1,3},{2,10},{3,5},{4,12},{5,7},{6,14},{7,1},{8,16},{9,11},{... | collective-permute-start | bytes 3145736 | tf_op jit(solution)/shard_map/ppermute | solution.py:40
  138.7 15.1 %collective-permute-start.20 = (bf16[2048,256]{1,0:T(8,128)(2,1)}, bf16[2048,256]{1,0:T(8,128)(2,1)}, u32[]{:S(2)}, u32[]{:S(2)}) collective-permute-start(bf16[2048,256]{1,0:T(8,128)(2,1)} %collective-permute-done.18.refs_5_), channel_id=1, source_target_pairs={{0,24},{1,7},{2,26},{3,1},{4,28},{5,3},{6,30},{7,5},{8,0},{9,15},{... | collective-permute-start | bytes 3145736 | tf_op jit(solution)/shard_map/ppermute | solution.py:40
  (15 other events, 220.3 us)
Sparse Core Ops, SparseCore 0:
  10.1 68.7 all-gather.2
  91.1 53.2 all-gather.4

commit v6 on v5

--- a/solution.py
+++ b/solution.py
@@ -295,7 +295,24 @@
     )
 
 
-def ring_kernel(stride, gap, per_chip, own, other, gathered, out, piece_buf, occ_buf, acc, out_buf, sems):
+LARGE, DOWN, UP = 2.0**100, 2.0**-24, 2.0**24
+
+
+def ring_sum(piece_buf, occ_buf, acc, ready):
+    for z in range(8):
+        ready(z)
+        for p in range(PAIR):
+            part = jnp.dot(occ_buf[2 * z], piece_buf[z, p, pl.ds(0, HALF), :], preferred_element_type=F32)
+            part += jnp.dot(occ_buf[2 * z + 1], piece_buf[z, p, pl.ds(HALF, HALF), :], preferred_element_type=F32)
+            at = pl.ds(p * ROWS, ROWS)
+            acc[at, :] = part if z == 0 else acc[at, :] + part
+
+
+def ring_kernel(stride, gap, first, own, other, gathered, *refs):
+    out, refs = refs[0], refs[1:]
+    if first:
+        scale, refs = refs[0], refs[1:]
+    piece_buf, occ_buf, acc, out_buf, scale_buf, sems = refs
     core = lax.axis_index("layer")
     own_rows = pl.ds(pl.multiple_of(core * HALF, HALF), HALF)
     other_rows = pl.ds(pl.multiple_of((1 - core) * HALF, HALF), HALF)
@@ -308,31 +325,49 @@
             group += start_all(
                 [own.at[tile], other.at[tile]], [occ_buf.at[k, own_rows], occ_buf.at[k, other_rows]], sems, 6 * z + 2 * i
             )
-        block = (2 * z + core if per_chip else z) * stride
+        block = (2 * z + core if first else z) * stride
         for p in range(PAIR):
             start = pl.multiple_of(block + p * (ROWS + gap), HALF)
             group += start_all([gathered.at[pl.ds(start, ROWS)]], [piece_buf.at[z, p]], sems, 6 * z + 4 + p)
         copies.append(group)
-    for z in range(8):
+    largest = [jnp.zeros((16, COLS), BF16)]
+
+    def ready(z):
         for copy in copies[z]:
             copy.wait()
-        for p in range(PAIR):
-            part = jnp.dot(occ_buf[2 * z], piece_buf[z, p, pl.ds(0, HALF), :], preferred_element_type=F32)
-            part += jnp.dot(occ_buf[2 * z + 1], piece_buf[z, p, pl.ds(HALF, HALF), :], preferred_element_type=F32)
-            at = pl.ds(p * ROWS, ROWS)
-            acc[at, :] = part if z == 0 else acc[at, :] + part
+        if first:
+            for k in (2 * z, 2 * z + 1):
+                sizes = jnp.abs(occ_buf[k]).reshape(ROWS // 16, 16, COLS)
+                largest[0] = jnp.maximum(largest[0], jnp.max(sizes, axis=0))
+
+    ring_sum(piece_buf, occ_buf, acc, ready)
+    if first:
+        large = jnp.max(largest[0].astype(F32)) > LARGE
+        scale_buf[...] = jnp.where(large, UP, 1.0) * jnp.ones_like(scale_buf)
+
+        @pl.when(large)
+        def _():
+            for k in range(16):
+                occ_buf[k] = (occ_buf[k].astype(F32) * DOWN).astype(BF16)
+            ring_sum(piece_buf, occ_buf, acc, lambda z: None)
+
+        scale_copy, = start_all([scale_buf], [scale], sems)
     out_buf[...] = acc[...].astype(BF16)
     pltpu.sync_copy(out_buf, out)
-
-
-def ring_product(name, own, other, gathered, stride, gap, per_chip):
+    if first:
+        scale_copy.wait()
+
+
+def ring_product(name, own, other, gathered, stride, gap, first):
     scratch = [
         pltpu.VMEM((8, PAIR, ROWS, COLS), BF16), pltpu.VMEM((16, ROWS, COLS), BF16),
-        pltpu.VMEM(SUM, F32), pltpu.VMEM(SUM, BF16),
+        pltpu.VMEM(SUM, F32), pltpu.VMEM(SUM, BF16), pltpu.VMEM((8, BLK), F32),
     ]
+    outs = jax.ShapeDtypeStruct(SUM, BF16)
+    if first:
+        outs = (outs, jax.ShapeDtypeStruct((8, BLK), F32))
     return call(
-        functools.partial(ring_kernel, stride, gap, per_chip), name, (own, other, gathered),
-        jax.ShapeDtypeStruct(SUM, BF16), scratch, 48, 2 << 30, 60 if per_chip else 60,
+        functools.partial(ring_kernel, stride, gap, first), name, (own, other, gathered), outs, scratch, 48, 2 << 30, 60
     )
 
 
@@ -366,8 +401,8 @@
     return jnp.sum(result, axis=0, keepdims=True)
 
 
-def polar_kernel(gathered, top, bottom, plane_sum, ring_part, own_aux, other_aux, polar, chi,
-                 bufs, virt_buf, acc, aux_buf, polar_buf, chi_buf, sems):
+def polar_kernel(gathered, top, bottom, plane_sum, ring_part, own_aux, other_aux, scale, polar, chi,
+                 bufs, virt_buf, acc, aux_buf, polar_buf, chi_buf, scale_buf, sems):
     core = lax.axis_index("layer")
     own, other = pl.ds(core * AUX, AUX), pl.ds((1 - core) * AUX, AUX)
     sum_copy, = start_all((plane_sum,), (acc,), sems)
@@ -376,9 +411,12 @@
         (ring_part, own_aux, other_aux),
         (polar_buf.at[pl.ds(0, PAIR * ROWS)], aux_buf.at[own], aux_buf.at[other]), sems, 1
     )
+    scale_copy, = start_all((scale,), (scale_buf,), sems, 12)
     sum_copy.wait()
     plane_add(copies, bufs, virt_copies, virt_buf, acc, False)
-    polar_buf[pl.ds(PAIR * ROWS, PAIR * ROWS), :] = acc[...].astype(BF16)
+    scale_copy.wait()
+    factor = jnp.broadcast_to(scale_buf[pl.ds(0, 1), pl.ds(0, 1)], SUM)
+    polar_buf[pl.ds(PAIR * ROWS, PAIR * ROWS), :] = (acc[...] * factor).astype(BF16)
     for copy in part_copies:
         copy.wait()
     polar_copy, = start_all((polar_buf,), (polar,), sems)
@@ -387,12 +425,12 @@
     polar_copy.wait()
 
 
-def polar_product(gathered, pieces, plane_sum, ring_part, own_aux, other_aux):
+def polar_product(gathered, pieces, plane_sum, ring_part, own_aux, other_aux, scale):
     outs = (jax.ShapeDtypeStruct((AUX * ROWS, COLS), BF16), jax.ShapeDtypeStruct((128, BLK), F32))
     scratch = [pltpu.VMEM((4, *SUM), BF16), pltpu.VMEM((4, *TILE), BF16), pltpu.VMEM(SUM, F32)]
-    scratch += [pltpu.VMEM((2 * AUX, ROWS, COLS), BF16)] + buffers_of(outs)
-    operands = (gathered, *pieces, plane_sum, ring_part, own_aux, other_aux)
-    return call(polar_kernel, "polar_product", operands, outs, scratch, 12, 1 << 29, 60)
+    scratch += [pltpu.VMEM((2 * AUX, ROWS, COLS), BF16)] + buffers_of((*outs, scale))
+    operands = (gathered, *pieces, plane_sum, ring_part, own_aux, other_aux, scale)
+    return call(polar_kernel, "polar_product", operands, outs, scratch, 13, 1 << 29, 60)
 
 
 def body(integrals, density_occ, density_virt, mask_int, mask_occ, mask_virt):
@@ -407,7 +445,7 @@
     other_occ = swap_cores(own_occ)
     half_tensor = plane_last(STRIDE, gathered, far, plane_sum)
     own_occ, other_occ, half_tensor = lax.optimization_barrier((own_occ, other_occ, half_tensor))
-    occ_first = ring_product("occ_first", own_occ, other_occ, gathered, STRIDE, HALF, True)
+    occ_first, scale = ring_product("occ_first", own_occ, other_occ, gathered, STRIDE, HALF, True)
 
     ring = lax.all_gather(half_tensor, "row", axis=0, tiled=True)
     own_aux, occ_first = lax.optimization_barrier((own_aux, occ_first))
@@ -415,7 +453,7 @@
     plane = gather_plane(occ_first)
     plane_sum = plane_product("plane_near", tuple(range(6)), PAIR * ROWS, gathered, plane[:6], F32)
     ring_part = ring_product("polar_ring", own_occ, other_occ, ring, PAIR * ROWS, 0, False)
-    polar, chi = polar_product(gathered, plane[6:], plane_sum, ring_part, own_aux, other_aux)
+    polar, chi = polar_product(gathered, plane[6:], plane_sum, ring_part, own_aux, other_aux, scale)
 
     shares = lax.all_to_all(chi.reshape(128, 1, BLK), ("row", "col"), 0, 0)
     chi = jnp.sum(shares.reshape(128, BLK), axis=0) * (1.0 / (ROWS * lax.axis_size("row")))

time: 189 us -> 189 us (level)
  no operation moved by 1% of the time
where the time goes in v6:
time: 189 us
  waiting for transfers between devices  80.3 us (42%)
  Pallas kernels  33.8 us (18%)
  starting transfers between devices  33.2 us (18%)
  blocking collectives  22.3 us (12%)
  between operations  14.3 us (8%)
  local copies, waits for them, and re-layouts  4.59 us (2%)
    ppermute x20, waiting for transfers between devices, plane_move(): return lax.ppermute(value, ('col', 'layer'), plane_perm(shift, first))  62.4 us
    ppermute x20, starting transfers between devices, plane_move(): return lax.ppermute(value, ('col', 'layer'), plane_perm(shift, first))  32.6 us
    pallas_call x7, Pallas kernels, call(): pl.pallas_call(kernel, out_shape=outs, in_specs=[HBM] * len(operands), ou...  28.9 us
    all_to_all x1, blocking collectives, body(): shares = lax.all_to_all(chi.reshape(128, 1, BLK), ('row', 'col'), 0, 0)  22.3 us
    all_gather x1, waiting for transfers between devices, body(): gathered = lax.all_gather(ring_aux, ('row', 'layer'), axis=0, tiled=True)  17 us
    unnamed x30, local copies, waits for them, and re-layouts  3.85 us
  transfers between devices with their start and end apart: 24, of which 16 were waited for; matrix products, arithmetic and copies ran while one was open for 0% of the time, Pallas kernels for 12%

profile of v6, /device:TPU:2, one launch (start us, length us, event | category | flops | bytes accessed | tf_op | source)
XLA Modules:
  0.0 188.7 jit_solution(11171642565614464612)
XLA Ops:
  7.2 2.7 %mask_inputs.1 = (bf16[1280,256]{1,0:T(8,128)(2,1)}, bf16[1280,256]{1,0:T(8,128)(2,1)}, bf16[4,512,256]{2,1,0:T(8,128)(2,1)}) custom-call(s32[4,2,4]{2,1,0:T(2,128)} %bitcast.9, s32[2,4]{1,0:T(2,128)} %bitcast.10, s32[2,4]{1,0:T(2,128)} %bitcast.11, bf16[4,512,256]{2,1,0:T(8,128)(2,1)} %integrals.1, bf16[512,256]{1,0:T(8,128)(2,1)} %occ.1, bf16[512,256]{1,0:T(8,128)(2,1)} %virt.1), custom_call_target="tpu_custom_call" | custom-call | tf_op jit(solution)/shard_map/mask_inputs/pallas_call | solution.py:173
  12.5 8.7 %collective-permute-done.refs_1_ = bf16[1280,256]{1,0:T(8,128)(2,1)S(1)} collective-permute-done((bf16[1280,256]{1,0:T(8,128)(2,1)}, bf16[1280,256]{1,0:T(8,128)(2,1)S(1)}, u32[]{:S(2)}, u32[]{:S(2)}) %collective-permute-start) | collective-permute-done | bytes 655392 | tf_op jit(solution)/shard_map/ppermute | solution.py:40
  22.5 2.1 %collective-permute-start.3 = (bf16[640,256]{1,0:T(8,128)(2,1)S(1)}, bf16[640,256]{1,0:T(8,128)(2,1)S(1)}, u32[]{:S(2)}, u32[]{:S(2)}) collective-permute-start(bf16[640,256]{1,0:T(8,128)(2,1)S(1)} %slice.26), channel_id=1, source_target_pairs={{0,6},{1,25},{2,0},{3,27},{4,2},{5,29},{6,4},{7,31},{8,14},{9,1},{... | collective-permute-start | bytes 983048 | tf_op jit(solution)/shard_map/ppermute | solution.py:40
  25.7 3.1 %collective-permute-start.5 = (bf16[2560,256]{1,0:T(8,128)(2,1)S(1)}, bf16[2560,256]{1,0:T(8,128)(2,1)S(1)}, u32[]{:S(2)}, u32[]{:S(2)}) collective-permute-start(bf16[2560,256]{1,0:T(8,128)(2,1)S(1)} %pack.4.refs_0_), channel_id=1, source_target_pairs={{0,24},{1,7},{2,26},{3,1},{4,28},{5,3},{6,30},{7,5},{8,0},{9,15},{... | collective-permute-start | bytes 3932168 | tf_op jit(solution)/shard_map/ppermute | solution.py:40
  28.8 2.9 %collective-permute-done.2.refs_1_ = bf16[640,256]{1,0:T(8,128)(2,1)S(1)} collective-permute-done((bf16[640,256]{1,0:T(8,128)(2,1)S(1)}, bf16[640,256]{1,0:T(8,128)(2,1)S(1)}, u32[]{:S(2)}, u32[]{:S(2)}) %collective-permute-start.2) | collective-permute-done | bytes 327712 | tf_op jit(solution)/shard_map/ppermute | solution.py:40
  32.8 2.8 %collective-permute-start.6 = (bf16[2560,256]{1,0:T(8,128)(2,1)S(1)}, bf16[2560,256]{1,0:T(8,128)(2,1)S(1)}, u32[]{:S(2)}, u32[]{:S(2)}) collective-permute-start(bf16[2560,256]{1,0:T(8,128)(2,1)S(1)} %pack.5.refs_1_), channel_id=1, source_target_pairs={{0,8},{1,3},{2,10},{3,5},{4,12},{5,7},{6,14},{7,1},{8,16},{9,11},{... | collective-permute-start | bytes 3932168 | tf_op jit(solution)/shard_map/ppermute | solution.py:40
  37.1 7.4 %collective-permute-done.4.refs_2_ = bf16[2560,256]{1,0:T(8,128)(2,1)} collective-permute-done((bf16[2560,256]{1,0:T(8,128)(2,1)S(1)}, bf16[2560,256]{1,0:T(8,128)(2,1)}, u32[]{:S(2)}, u32[]{:S(2)}) %collective-permute-start.4) | collective-permute-done | bytes 1310752 | tf_op jit(solution)/shard_map/ppermute | solution.py:40
  44.5 13.9 %collective-permute-done.6.refs_4_ = bf16[2560,256]{1,0:T(8,128)(2,1)S(1)} collective-permute-done((bf16[2560,256]{1,0:T(8,128)(2,1)S(1)}, bf16[2560,256]{1,0:T(8,128)(2,1)S(1)}, u32[]{:S(2)}, u32[]{:S(2)}) %collective-permute-start.6) | collective-permute-done | bytes 1310752 | tf_op jit(solution)/shard_map/ppermute | solution.py:40
  59.6 2.3 %collective-permute-start.9 = (bf16[2560,256]{1,0:T(8,128)(2,1)}, bf16[2560,256]{1,0:T(8,128)(2,1)}, u32[]{:S(2)}, u32[]{:S(2)}) collective-permute-start(bf16[2560,256]{1,0:T(8,128)(2,1)} %collective-permute-done.7.refs_5_), channel_id=1, source_target_pairs={{0,24},{1,7},{2,26},{3,1},{4,28},{5,3},{6,30},{7,5},{8,0},{9,15},{... | collective-permute-start | bytes 3932168 | tf_op jit(solution)/shard_map/ppermute | solution.py:40
  61.9 17.0 %all-gather.3.cloned.1.call-done.gathered = bf16[20480,256]{1,0:T(8,128)(2,1)} async-done(((bf16[1280,256]{1,0:T(8,128)(2,1)}), bf16[20480,256]{1,0:T(8,128)(2,1)}) %all-gather.3.cloned.1.call-update) | async-done | bytes 10485776 | tf_op jit(solution)/shard_map/all_gather | solution.py:440
  78.9 3.7 %plane_near.2.sum_in = f32[1024,256]{1,0:T(8,128)S(1)} custom-call(bf16[20480,256]{1,0:T(8,128)(2,1)} %all-gather.3.cloned.1.call-done.gathered, bf16[2560,256]{1,0:T(8,128)(2,1)S(1)} %pack.4.refs_0_, bf16[2560,256]{1,0:T(8,128)(2,1)} %copy-done.1, bf16[2560,256]{1,0:T(8,128)(2,1)} %collective-permute-done.4.refs_2_, bf16[2560,256]{1,0:T(8,128)(2,1)} %copy-done.8, ...), custom_call_target="tpu_custom_call" | custom-call | flops 2147483648 | bytes 9437184 | tf_op jit(solution)/shard_map/plane_near/pallas_call | solution.py:197
  83.6 2.6 %occ_tiles.1.own = bf16[4096,256]{1,0:T(8,128)(2,1)} custom-call(bf16[2560,256]{1,0:T(8,128)(2,1)} %copy-done, bf16[2560,256]{1,0:T(8,128)(2,1)} %copy-done.1, bf16[2560,256]{1,0:T(8,128)(2,1)} %collective-permute-done.4.refs_2_, bf16[2560,256]{1,0:T(8,128)(2,1)} %copy-done.8, bf16[2560,256]{1,0:T(8,128)(2,1)} %copy-done.9, ...), custom_call_target="tpu_custom_call" | custom-call | bytes 9437184 | tf_op jit(solution)/shard_map/occ_tiles/pallas_call | solution.py:197
  86.8 3.3 %plane_last.1 = bf16[1024,256]{1,0:T(8,128)(2,1)} custom-call(bf16[20480,256]{1,0:T(8,128)(2,1)} %all-gather.3.cloned.1.call-done.gathered, bf16[2560,256]{1,0:T(8,128)(2,1)} %collective-permute-done.8.refs_6_.top, bf16[2560,256]{1,0:T(8,128)(2,1)} %collective-permute-done.9.refs_7_.bottom, f32[1024,256]{1,0:T(8,128)} %copy-done.2), custom_call_target="tpu_custom_call" | custom-call | flops 536870912 | bytes 9437184 | tf_op jit(solution)/shard_map/plane_last/pallas_call | solution.py:197
  92.3 5.3 %occ_first.1 = (bf16[1024,256]{1,0:T(8,128)(2,1)}, f32[8,128]{1,0:T(8,128)}) custom-call(bf16[4096,256]{1,0:T(8,128)(2,1)} %occ_tiles.1.own, bf16[4096,256]{1,0:T(8,128)(2,1)} %copy-done.7, bf16[20480,256]{1,0:T(8,128)(2,1)} %all-gather.3.cloned.1.call-done.gathered), custom_call_target="tpu_custom_call" | custom-call | flops 2147483648 | bytes 9437184 | tf_op jit(solution)/shard_map/occ_first/pallas_call | solution.py:197
  99.7 7.4 %collective-permute-done.11.refs_1_ = bf16[1024,256]{1,0:T(8,128)(2,1)S(1)} collective-permute-done((bf16[1024,256]{1,0:T(8,128)(2,1)}, bf16[1024,256]{1,0:T(8,128)(2,1)S(1)}, u32[]{:S(2)}, u32[]{:S(2)}) %collective-permute-start.11) | collective-permute-done | bytes 524320 | tf_op jit(solution)/shard_map/ppermute | solution.py:40
  113.5 1.9 collective-permute-done.16.refs_2_
  115.6 4.0 %collective-permute-start.17 = (bf16[2048,256]{1,0:T(8,128)(2,1)S(1)}, bf16[2048,256]{1,0:T(8,128)(2,1)S(1)}, u32[]{:S(2)}, u32[]{:S(2)}) collective-permute-start(bf16[2048,256]{1,0:T(8,128)(2,1)S(1)} %pack.7.refs_1_), channel_id=1, source_target_pairs={{0,8},{1,3},{2,10},{3,5},{4,12},{5,7},{6,14},{7,1},{8,16},{9,11},{... | collective-permute-start | bytes 3145736 | tf_op jit(solution)/shard_map/ppermute | solution.py:40
  121.1 4.6 %collective-permute-done.12.refs_2_ = bf16[2048,256]{1,0:T(8,128)(2,1)S(1)} collective-permute-done((bf16[2048,256]{1,0:T(8,128)(2,1)S(1)}, bf16[2048,256]{1,0:T(8,128)(2,1)S(1)}, u32[]{:S(2)}, u32[]{:S(2)}) %collective-permute-start.12) | collective-permute-done | bytes 1048608 | tf_op jit(solution)/shard_map/ppermute | solution.py:40
  125.8 11.1 %collective-permute-done.17.refs_4_ = bf16[2048,256]{1,0:T(8,128)(2,1)S(1)} collective-permute-done((bf16[2048,256]{1,0:T(8,128)(2,1)S(1)}, bf16[2048,256]{1,0:T(8,128)(2,1)S(1)}, u32[]{:S(2)}, u32[]{:S(2)}) %collective-permute-start.17) | collective-permute-done | bytes 1048608 | tf_op jit(solution)/shard_map/ppermute | solution.py:40
  140.4 3.8 %plane_near.3.plane_sum = f32[1024,256]{1,0:T(8,128)S(1)} custom-call(bf16[20480,256]{1,0:T(8,128)(2,1)} %all-gather.3.cloned.1.call-done.gathered, bf16[2048,256]{1,0:T(8,128)(2,1)S(1)} %pack.6.refs_0_, bf16[2048,256]{1,0:T(8,128)(2,1)} %copy-done.4, bf16[2048,256]{1,0:T(8,128)(2,1)} %copy-done.11, bf16[2048,256]{1,0:T(8,128)(2,1)} %copy-done.13, ...), custom_call_target="tpu_custom_call" | custom-call | flops 2147483648 | bytes 9437184 | tf_op jit(solution)/shard_map/plane_near/pallas_call | solution.py:197
  145.2 5.3 %polar_ring.1.ring_part = bf16[1024,256]{1,0:T(8,128)(2,1)} custom-call(bf16[4096,256]{1,0:T(8,128)(2,1)} %occ_tiles.1.own, bf16[4096,256]{1,0:T(8,128)(2,1)} %copy-done.7, bf16[8192,256]{1,0:T(8,128)(2,1)} %all-gather.5.cloned.1.call-done.gathered), custom_call_target="tpu_custom_call" | custom-call | flops 2147483648 | bytes 9437184 | tf_op jit(solution)/shard_map/polar_ring/pallas_call | solution.py:197
  150.5 2.8 %collective-permute-done.19.top = bf16[2048,256]{1,0:T(8,128)(2,1)} collective-permute-done((bf16[2048,256]{1,0:T(8,128)(2,1)S(1)}, bf16[2048,256]{1,0:T(8,128)(2,1)}, u32[]{:S(2)}, u32[]{:S(2)}) %collective-permute-start.19) | collective-permute-done | bytes 1048608 | tf_op jit(solution)/shard_map/ppermute | solution.py:40
  153.8 4.9 %polar_product.1 = (bf16[2048,256]{1,0:T(8,128)(2,1)}, f32[128,128]{1,0:T(8,128)}) custom-call(bf16[20480,256]{1,0:T(8,128)(2,1)} %all-gather.3.cloned.1.call-done.gathered, bf16[2048,256]{1,0:T(8,128)(2,1)} %collective-permute-done.19.top, bf16[2048,256]{1,0:T(8,128)(2,1)} %collective-permute-done.20.bottom, f32[1024,256]{1,0:T(8,128)} %copy-done.3, ...), custom_call_target="tpu_custom_call" | custom-call | flops 536870912 | bytes 9437184 | tf_op jit(solution)/shard_map/polar_product/pallas_call | solution.py:197
  158.7 22.3 %all_to_all.5 = f32[128,1,128]{2,1,0:T(1,128)S(1)} all-to-all(f32[128,1,128]{2,1,0:T(1,128)} %bitcast.8), channel_id=1, replica_groups=mesh['row'=8,'col'=16,'layer'=2] {'row','col'}, dimensions={0} | all-to-all | bytes 131072 | tf_op jit(solution)/shard_map/all_to_all | solution.py:458
  (76 shorter events, 28.3 us)
Async XLA Ops:
  7.2 71.7 %all-gather.3.cloned.1.call-start = ((), (), s32[]{:S(2)}) async-start(), calls=%async_computation.1 | async-start | bytes 11141120 | tf_op jit(solution)/shard_map/all_gather | solution.py:440
  10.0 135.2 %all-gather.5.cloned.1.call-start = ((), (), s32[]{:S(2)}) async-start(), calls=%async_computation.2 | async-start | bytes 4718592 | tf_op jit(solution)/shard_map/all_gather | solution.py:450
  10.0 11.1 %collective-permute-start = (bf16[1280,256]{1,0:T(8,128)(2,1)}, bf16[1280,256]{1,0:T(8,128)(2,1)S(1)}, u32[]{:S(2)}, u32[]{:S(2)}) collective-permute-start(bf16[1280,256]{1,0:T(8,128)(2,1)} %get-tuple-element.27.refs_0_), channel_id=1, source_target_pairs={{0,2},{1,9},{2,4},{3,11},{4,6},{5,13},{6,0},{7,15},{8,10},{9,17},{... | collective-permute-start | bytes 1966088 | tf_op jit(solution)/shard_map/ppermute | solution.py:40
  11.6 10.9 %collective-permute-start.1 = (bf16[1280,256]{1,0:T(8,128)(2,1)}, bf16[1280,256]{1,0:T(8,128)(2,1)S(1)}, u32[]{:S(2)}, u32[]{:S(2)}) collective-permute-start(bf16[1280,256]{1,0:T(8,128)(2,1)} %get-tuple-element.27.refs_0_), channel_id=1, source_target_pairs={{0,6},{1,25},{2,0},{3,27},{4,2},{5,29},{6,4},{7,31},{8,14},{9,1},{... | collective-permute-start | bytes 1966088 | tf_op jit(solution)/shard_map/ppermute | solution.py:40
  21.2 10.6 %collective-permute-start.2 = (bf16[640,256]{1,0:T(8,128)(2,1)S(1)}, bf16[640,256]{1,0:T(8,128)(2,1)S(1)}, u32[]{:S(2)}, u32[]{:S(2)}) collective-permute-start(bf16[640,256]{1,0:T(8,128)(2,1)S(1)} %slice.25), channel_id=1, source_target_pairs={{0,2},{1,9},{2,4},{3,11},{4,6},{5,13},{6,0},{7,15},{8,10},{9,17},{... | collective-permute-start | bytes 983048 | tf_op jit(solution)/shard_map/ppermute | solution.py:40
  22.5 9.4 %collective-permute-start.3 = (bf16[640,256]{1,0:T(8,128)(2,1)S(1)}, bf16[640,256]{1,0:T(8,128)(2,1)S(1)}, u32[]{:S(2)}, u32[]{:S(2)}) collective-permute-start(bf16[640,256]{1,0:T(8,128)(2,1)S(1)} %slice.26), channel_id=1, source_target_pairs={{0,6},{1,25},{2,0},{3,27},{4,2},{5,29},{6,4},{7,31},{8,14},{9,1},{... | collective-permute-start | bytes 983048 | tf_op jit(solution)/shard_map/ppermute | solution.py:40
  25.5 19.0 %collective-permute-start.4 = (bf16[2560,256]{1,0:T(8,128)(2,1)S(1)}, bf16[2560,256]{1,0:T(8,128)(2,1)}, u32[]{:S(2)}, u32[]{:S(2)}) collective-permute-start(bf16[2560,256]{1,0:T(8,128)(2,1)S(1)} %pack.4.refs_0_), channel_id=1, source_target_pairs={{0,8},{1,3},{2,10},{3,5},{4,12},{5,7},{6,14},{7,1},{8,16},{9,11},{... | collective-permute-start | bytes 3932168 | tf_op jit(solution)/shard_map/ppermute | solution.py:40
  25.7 18.8 %collective-permute-start.5 = (bf16[2560,256]{1,0:T(8,128)(2,1)S(1)}, bf16[2560,256]{1,0:T(8,128)(2,1)S(1)}, u32[]{:S(2)}, u32[]{:S(2)}) collective-permute-start(bf16[2560,256]{1,0:T(8,128)(2,1)S(1)} %pack.4.refs_0_), channel_id=1, source_target_pairs={{0,24},{1,7},{2,26},{3,1},{4,28},{5,3},{6,30},{7,5},{8,0},{9,15},{... | collective-permute-start | bytes 3932168 | tf_op jit(solution)/shard_map/ppermute | solution.py:40
  32.8 25.7 %collective-permute-start.6 = (bf16[2560,256]{1,0:T(8,128)(2,1)S(1)}, bf16[2560,256]{1,0:T(8,128)(2,1)S(1)}, u32[]{:S(2)}, u32[]{:S(2)}) collective-permute-start(bf16[2560,256]{1,0:T(8,128)(2,1)S(1)} %pack.5.refs_1_), channel_id=1, source_target_pairs={{0,8},{1,3},{2,10},{3,5},{4,12},{5,7},{6,14},{7,1},{8,16},{9,11},{... | collective-permute-start | bytes 3932168 | tf_op jit(solution)/shard_map/ppermute | solution.py:40
  35.6 22.9 %collective-permute-start.7 = (bf16[2560,256]{1,0:T(8,128)(2,1)S(1)}, bf16[2560,256]{1,0:T(8,128)(2,1)}, u32[]{:S(2)}, u32[]{:S(2)}) collective-permute-start(bf16[2560,256]{1,0:T(8,128)(2,1)S(1)} %pack.5.refs_1_), channel_id=1, source_target_pairs={{0,24},{1,7},{2,26},{3,1},{4,28},{5,3},{6,30},{7,5},{8,0},{9,15},{... | collective-permute-start | bytes 3932168 | tf_op jit(solution)/shard_map/ppermute | solution.py:40
  58.5 25.2 %collective-permute-start.8 = (bf16[2560,256]{1,0:T(8,128)(2,1)}, bf16[2560,256]{1,0:T(8,128)(2,1)}, u32[]{:S(2)}, u32[]{:S(2)}) collective-permute-start(bf16[2560,256]{1,0:T(8,128)(2,1)} %collective-permute-done.4.refs_2_), channel_id=1, source_target_pairs={{0,8},{1,3},{2,10},{3,5},{4,12},{5,7},{6,14},{7,1},{8,16},{9,11},{... | collective-permute-start | bytes 3932168 | tf_op jit(solution)/shard_map/ppermute | solution.py:40
  59.6 24.1 %collective-permute-start.9 = (bf16[2560,256]{1,0:T(8,128)(2,1)}, bf16[2560,256]{1,0:T(8,128)(2,1)}, u32[]{:S(2)}, u32[]{:S(2)}) collective-permute-start(bf16[2560,256]{1,0:T(8,128)(2,1)} %collective-permute-done.7.refs_5_), channel_id=1, source_target_pairs={{0,24},{1,7},{2,26},{3,1},{4,28},{5,3},{6,30},{7,5},{8,0},{9,15},{... | collective-permute-start | bytes 3932168 | tf_op jit(solution)/shard_map/ppermute | solution.py:40
  86.3 4.6 %collective-permute-start.10 = (bf16[4096,256]{1,0:T(8,128)(2,1)}, bf16[4096,256]{1,0:T(8,128)(2,1)S(1)}, u32[]{:S(2)}, u32[]{:S(2)}) collective-permute-start(bf16[4096,256]{1,0:T(8,128)(2,1)} %occ_tiles.1.own), channel_id=1, source_target_pairs={{0,1},{1,0},{2,3},{3,2},{4,5},{5,4},{6,7},{7,6},{8,9},{9,8},{10,11... | collective-permute-start | bytes 6291464 | tf_op jit(solution)/shard_map/ppermute | solution.py:44
  97.6 9.5 %collective-permute-start.11 = (bf16[1024,256]{1,0:T(8,128)(2,1)}, bf16[1024,256]{1,0:T(8,128)(2,1)S(1)}, u32[]{:S(2)}, u32[]{:S(2)}) collective-permute-start(bf16[1024,256]{1,0:T(8,128)(2,1)} %get-tuple-element.38.refs_0_), channel_id=1, source_target_pairs={{0,2},{1,9},{2,4},{3,11},{4,6},{5,13},{6,0},{7,15},{8,10},{9,17},{... | collective-permute-start | bytes 1572872 | tf_op jit(solution)/shard_map/ppermute | solution.py:40
  99.1 9.5 %collective-permute-start.14 = (bf16[1024,256]{1,0:T(8,128)(2,1)}, bf16[1024,256]{1,0:T(8,128)(2,1)S(1)}, u32[]{:S(2)}, u32[]{:S(2)}) collective-permute-start(bf16[1024,256]{1,0:T(8,128)(2,1)} %get-tuple-element.38.refs_0_), channel_id=1, source_target_pairs={{0,6},{1,25},{2,0},{3,27},{4,2},{5,29},{6,4},{7,31},{8,14},{9,1},{... | collective-permute-start | bytes 1572872 | tf_op jit(solution)/shard_map/ppermute | solution.py:40
  107.1 6.4 %collective-permute-start.15 = (bf16[512,256]{1,0:T(8,128)(2,1)S(1)}, bf16[512,256]{1,0:T(8,128)(2,1)S(1)}, u32[]{:S(2)}, u32[]{:S(2)}) collective-permute-start(bf16[512,256]{1,0:T(8,128)(2,1)S(1)} %slice.27), channel_id=1, source_target_pairs={{0,2},{1,9},{2,4},{3,11},{4,6},{5,13},{6,0},{7,15},{8,10},{9,17},{... | collective-permute-start | bytes 786440 | tf_op jit(solution)/shard_map/ppermute | solution.py:40
  108.6 6.8 %collective-permute-start.16 = (bf16[512,256]{1,0:T(8,128)(2,1)S(1)}, bf16[512,256]{1,0:T(8,128)(2,1)S(1)}, u32[]{:S(2)}, u32[]{:S(2)}) collective-permute-start(bf16[512,256]{1,0:T(8,128)(2,1)S(1)} %slice.28), channel_id=1, source_target_pairs={{0,6},{1,25},{2,0},{3,27},{4,2},{5,29},{6,4},{7,31},{8,14},{9,1},{... | collective-permute-start | bytes 786440 | tf_op jit(solution)/shard_map/ppermute | solution.py:40
  109.5 16.2 %collective-permute-start.12 = (bf16[2048,256]{1,0:T(8,128)(2,1)S(1)}, bf16[2048,256]{1,0:T(8,128)(2,1)S(1)}, u32[]{:S(2)}, u32[]{:S(2)}) collective-permute-start(bf16[2048,256]{1,0:T(8,128)(2,1)S(1)} %pack.6.refs_0_), channel_id=1, source_target_pairs={{0,8},{1,3},{2,10},{3,5},{4,12},{5,7},{6,14},{7,1},{8,16},{9,11},{... | collective-permute-start | bytes 3145736 | tf_op jit(solution)/shard_map/ppermute | solution.py:40
  111.0 14.8 %collective-permute-start.13 = (bf16[2048,256]{1,0:T(8,128)(2,1)S(1)}, bf16[2048,256]{1,0:T(8,128)(2,1)S(1)}, u32[]{:S(2)}, u32[]{:S(2)}) collective-permute-start(bf16[2048,256]{1,0:T(8,128)(2,1)S(1)} %pack.6.refs_0_), channel_id=1, source_target_pairs={{0,24},{1,7},{2,26},{3,1},{4,28},{5,3},{6,30},{7,5},{8,0},{9,15},{... | collective-permute-start | bytes 3145736 | tf_op jit(solution)/shard_map/ppermute | solution.py:40
  115.6 21.3 %collective-permute-start.17 = (bf16[2048,256]{1,0:T(8,128)(2,1)S(1)}, bf16[2048,256]{1,0:T(8,128)(2,1)S(1)}, u32[]{:S(2)}, u32[]{:S(2)}) collective-permute-start(bf16[2048,256]{1,0:T(8,128)(2,1)S(1)} %pack.7.refs_1_), channel_id=1, source_target_pairs={{0,8},{1,3},{2,10},{3,5},{4,12},{5,7},{6,14},{7,1},{8,16},{9,11},{... | collective-permute-start | bytes 3145736 | tf_op jit(solution)/shard_map/ppermute | solution.py:40
  119.6 17.5 %collective-permute-start.18 = (bf16[2048,256]{1,0:T(8,128)(2,1)S(1)}, bf16[2048,256]{1,0:T(8,128)(2,1)}, u32[]{:S(2)}, u32[]{:S(2)}) collective-permute-start(bf16[2048,256]{1,0:T(8,128)(2,1)S(1)} %pack.7.refs_1_), channel_id=1, source_target_pairs={{0,24},{1,7},{2,26},{3,1},{4,28},{5,3},{6,30},{7,5},{8,0},{9,15},{... | collective-permute-start | bytes 3145736 | tf_op jit(solution)/shard_map/ppermute | solution.py:40
  121.1 29.4 %collective-permute-start.21 = (bf16[4,512,256]{2,1,0:T(8,128)(2,1)S(1)}, bf16[4,512,256]{2,1,0:T(8,128)(2,1)S(1)}, u32[]{:S(2)}, u32[]{:S(2)}) collective-permute-start(bf16[4,512,256]{2,1,0:T(8,128)(2,1)S(1)} %copy-done.10), channel_id=1, source_target_pairs={{0,1},{1,0},{2,3},{3,2},{4,5},{5,4},{6,7},{7,6},{8,9},{9,8},{10,11... | collective-permute-start | bytes 3145736 | tf_op jit(solution)/shard_map/ppermute | solution.py:44
  137.2 16.1 %collective-permute-start.19 = (bf16[2048,256]{1,0:T(8,128)(2,1)S(1)}, bf16[2048,256]{1,0:T(8,128)(2,1)}, u32[]{:S(2)}, u32[]{:S(2)}) collective-permute-start(bf16[2048,256]{1,0:T(8,128)(2,1)S(1)} %collective-permute-done.12.refs_2_), channel_id=1, source_target_pairs={{0,8},{1,3},{2,10},{3,5},{4,12},{5,7},{6,14},{7,1},{8,16},{9,11},{... | collective-permute-start | bytes 3145736 | tf_op jit(solution)/shard_map/ppermute | solution.py:40
  138.6 15.1 %collective-permute-start.20 = (bf16[2048,256]{1,0:T(8,128)(2,1)}, bf16[2048,256]{1,0:T(8,128)(2,1)}, u32[]{:S(2)}, u32[]{:S(2)}) collective-permute-start(bf16[2048,256]{1,0:T(8,128)(2,1)} %collective-permute-done.18.refs_5_), channel_id=1, source_target_pairs={{0,24},{1,7},{2,26},{3,1},{4,28},{5,3},{6,30},{7,5},{8,0},{9,15},{... | collective-permute-start | bytes 3145736 | tf_op jit(solution)/shard_map/ppermute | solution.py:40
  (15 other events, 220.4 us)
Sparse Core Ops, SparseCore 0:
  10.1 68.7 all-gather.2
  91.1 53.2 all-gather.4

commit v7 on v6

--- a/solution.py
+++ b/solution.py
@@ -367,7 +367,7 @@
     if first:
         outs = (outs, jax.ShapeDtypeStruct((8, BLK), F32))
     return call(
-        functools.partial(ring_kernel, stride, gap, first), name, (own, other, gathered), outs, scratch, 48, 2 << 30, 60
+        functools.partial(ring_kernel, stride, gap, first), name, (own, other, gathered), outs, scratch, 48, 2 << 30, 51 if first else 60
     )
 
 

time: 189 us -> 188 us (level)
  transfers between devices with their start and end apart: 24 -> 24, of which waited for: 16 -> 16; matrix products, arithmetic and copies ran while one was open for 0% -> 0% of each run, Pallas kernels for 12% -> 13%
where the time goes in v7:
time: 188 us
  waiting for transfers between devices  80.1 us (43%)
  Pallas kernels  34.7 us (18%)
  starting transfers between devices  33.2 us (18%)
  blocking collectives  22.3 us (12%)
  between operations  14.3 us (8%)
  local copies, waits for them, and re-layouts  3.26 us (2%)
    ppermute x20, waiting for transfers between devices, plane_move(): return lax.ppermute(value, ('col', 'layer'), plane_perm(shift, first))  62.2 us
    ppermute x20, starting transfers between devices, plane_move(): return lax.ppermute(value, ('col', 'layer'), plane_perm(shift, first))  32.7 us
    pallas_call x7, Pallas kernels, call(): pl.pallas_call(kernel, out_shape=outs, in_specs=[HBM] * len(operands), ou...  29.8 us
    all_to_all x1, blocking collectives, body(): shares = lax.all_to_all(chi.reshape(128, 1, BLK), ('row', 'col'), 0, 0)  22.3 us
    all_gather x1, waiting for transfers between devices, body(): gathered = lax.all_gather(ring_aux, ('row', 'layer'), axis=0, tiled=True)  17 us
  transfers between devices with their start and end apart: 24, of which 16 were waited for; matrix products, arithmetic and copies ran while one was open for 0% of the time, Pallas kernels for 13%

profile of v7, /device:TPU:2, one launch (start us, length us, event | category | flops | bytes accessed | tf_op | source)
XLA Modules:
  0.0 188.0 jit_solution(7573536825689673601)
XLA Ops:
  7.2 2.7 %mask_inputs.1 = (bf16[1280,256]{1,0:T(8,128)(2,1)}, bf16[1280,256]{1,0:T(8,128)(2,1)}, bf16[4,512,256]{2,1,0:T(8,128)(2,1)}) custom-call(s32[4,2,4]{2,1,0:T(2,128)} %bitcast.9, s32[2,4]{1,0:T(2,128)} %bitcast.10, s32[2,4]{1,0:T(2,128)} %bitcast.11, bf16[4,512,256]{2,1,0:T(8,128)(2,1)} %integrals.1, bf16[512,256]{1,0:T(8,128)(2,1)} %occ.1, bf16[512,256]{1,0:T(8,128)(2,1)} %virt.1), custom_call_target="tpu_custom_call" | custom-call | tf_op jit(solution)/shard_map/mask_inputs/pallas_call | solution.py:173
  12.5 8.7 %collective-permute-done.refs_1_ = bf16[1280,256]{1,0:T(8,128)(2,1)S(1)} collective-permute-done((bf16[1280,256]{1,0:T(8,128)(2,1)}, bf16[1280,256]{1,0:T(8,128)(2,1)S(1)}, u32[]{:S(2)}, u32[]{:S(2)}) %collective-permute-start) | collective-permute-done | bytes 655392 | tf_op jit(solution)/shard_map/ppermute | solution.py:40
  22.5 2.1 %collective-permute-start.3 = (bf16[640,256]{1,0:T(8,128)(2,1)S(1)}, bf16[640,256]{1,0:T(8,128)(2,1)S(1)}, u32[]{:S(2)}, u32[]{:S(2)}) collective-permute-start(bf16[640,256]{1,0:T(8,128)(2,1)S(1)} %slice.26), channel_id=1, source_target_pairs={{0,6},{1,25},{2,0},{3,27},{4,2},{5,29},{6,4},{7,31},{8,14},{9,1},{... | collective-permute-start | bytes 983048 | tf_op jit(solution)/shard_map/ppermute | solution.py:40
  25.7 3.1 %collective-permute-start.5 = (bf16[2560,256]{1,0:T(8,128)(2,1)S(1)}, bf16[2560,256]{1,0:T(8,128)(2,1)S(1)}, u32[]{:S(2)}, u32[]{:S(2)}) collective-permute-start(bf16[2560,256]{1,0:T(8,128)(2,1)S(1)} %pack.4.refs_0_), channel_id=1, source_target_pairs={{0,24},{1,7},{2,26},{3,1},{4,28},{5,3},{6,30},{7,5},{8,0},{9,15},{... | collective-permute-start | bytes 3932168 | tf_op jit(solution)/shard_map/ppermute | solution.py:40
  28.8 2.9 %collective-permute-done.2.refs_1_ = bf16[640,256]{1,0:T(8,128)(2,1)S(1)} collective-permute-done((bf16[640,256]{1,0:T(8,128)(2,1)S(1)}, bf16[640,256]{1,0:T(8,128)(2,1)S(1)}, u32[]{:S(2)}, u32[]{:S(2)}) %collective-permute-start.2) | collective-permute-done | bytes 327712 | tf_op jit(solution)/shard_map/ppermute | solution.py:40
  32.8 2.8 %collective-permute-start.6 = (bf16[2560,256]{1,0:T(8,128)(2,1)S(1)}, bf16[2560,256]{1,0:T(8,128)(2,1)S(1)}, u32[]{:S(2)}, u32[]{:S(2)}) collective-permute-start(bf16[2560,256]{1,0:T(8,128)(2,1)S(1)} %pack.5.refs_1_), channel_id=1, source_target_pairs={{0,8},{1,3},{2,10},{3,5},{4,12},{5,7},{6,14},{7,1},{8,16},{9,11},{... | collective-permute-start | bytes 3932168 | tf_op jit(solution)/shard_map/ppermute | solution.py:40
  37.1 7.4 %collective-permute-done.4.refs_2_ = bf16[2560,256]{1,0:T(8,128)(2,1)} collective-permute-done((bf16[2560,256]{1,0:T(8,128)(2,1)S(1)}, bf16[2560,256]{1,0:T(8,128)(2,1)}, u32[]{:S(2)}, u32[]{:S(2)}) %collective-permute-start.4) | collective-permute-done | bytes 1310752 | tf_op jit(solution)/shard_map/ppermute | solution.py:40
  44.5 13.9 %collective-permute-done.6.refs_4_ = bf16[2560,256]{1,0:T(8,128)(2,1)S(1)} collective-permute-done((bf16[2560,256]{1,0:T(8,128)(2,1)S(1)}, bf16[2560,256]{1,0:T(8,128)(2,1)S(1)}, u32[]{:S(2)}, u32[]{:S(2)}) %collective-permute-start.6) | collective-permute-done | bytes 1310752 | tf_op jit(solution)/shard_map/ppermute | solution.py:40
  59.5 2.4 %collective-permute-start.9 = (bf16[2560,256]{1,0:T(8,128)(2,1)}, bf16[2560,256]{1,0:T(8,128)(2,1)}, u32[]{:S(2)}, u32[]{:S(2)}) collective-permute-start(bf16[2560,256]{1,0:T(8,128)(2,1)} %collective-permute-done.7.refs_5_), channel_id=1, source_target_pairs={{0,24},{1,7},{2,26},{3,1},{4,28},{5,3},{6,30},{7,5},{8,0},{9,15},{... | collective-permute-start | bytes 3932168 | tf_op jit(solution)/shard_map/ppermute | solution.py:40
  61.9 17.0 %all-gather.3.cloned.1.call-done.gathered = bf16[20480,256]{1,0:T(8,128)(2,1)} async-done(((bf16[1280,256]{1,0:T(8,128)(2,1)}), bf16[20480,256]{1,0:T(8,128)(2,1)}) %all-gather.3.cloned.1.call-update) | async-done | bytes 10485776 | tf_op jit(solution)/shard_map/all_gather | solution.py:440
  78.9 3.7 %plane_near.2.sum_in = f32[1024,256]{1,0:T(8,128)S(1)} custom-call(bf16[20480,256]{1,0:T(8,128)(2,1)} %all-gather.3.cloned.1.call-done.gathered, bf16[2560,256]{1,0:T(8,128)(2,1)S(1)} %pack.4.refs_0_, bf16[2560,256]{1,0:T(8,128)(2,1)} %copy-done.2, bf16[2560,256]{1,0:T(8,128)(2,1)} %collective-permute-done.4.refs_2_, bf16[2560,256]{1,0:T(8,128)(2,1)} %copy-done.8, ...), custom_call_target="tpu_custom_call" | custom-call | flops 2147483648 | bytes 9437184 | tf_op jit(solution)/shard_map/plane_near/pallas_call | solution.py:197
  83.6 2.6 %occ_tiles.1.own = bf16[4096,256]{1,0:T(8,128)(2,1)} custom-call(bf16[2560,256]{1,0:T(8,128)(2,1)} %copy-done.1, bf16[2560,256]{1,0:T(8,128)(2,1)} %copy-done.2, bf16[2560,256]{1,0:T(8,128)(2,1)} %collective-permute-done.4.refs_2_, bf16[2560,256]{1,0:T(8,128)(2,1)} %copy-done.8, bf16[2560,256]{1,0:T(8,128)(2,1)} %copy-done.9, ...), custom_call_target="tpu_custom_call" | custom-call | bytes 9437184 | tf_op jit(solution)/shard_map/occ_tiles/pallas_call | solution.py:197
  86.8 3.4 %plane_last.1 = bf16[1024,256]{1,0:T(8,128)(2,1)} custom-call(bf16[20480,256]{1,0:T(8,128)(2,1)} %all-gather.3.cloned.1.call-done.gathered, bf16[2560,256]{1,0:T(8,128)(2,1)} %collective-permute-done.8.refs_6_.top, bf16[2560,256]{1,0:T(8,128)(2,1)} %collective-permute-done.9.refs_7_.bottom, f32[1024,256]{1,0:T(8,128)} %copy-done.3), custom_call_target="tpu_custom_call" | custom-call | flops 536870912 | bytes 9437184 | tf_op jit(solution)/shard_map/plane_last/pallas_call | solution.py:197
  91.1 6.1 %occ_first.1 = (bf16[1024,256]{1,0:T(8,128)(2,1)S(1)}, f32[8,128]{1,0:T(8,128)S(1)}) custom-call(bf16[4096,256]{1,0:T(8,128)(2,1)S(1)} %copy-done, bf16[4096,256]{1,0:T(8,128)(2,1)} %collective-permute-done.10.other, bf16[20480,256]{1,0:T(8,128)(2,1)} %all-gather.3.cloned.1.call-done.gathered), custom_call_target="tpu_custom_call" | custom-call | flops 2147483648 | bytes 9437184 | tf_op jit(solution)/shard_map/occ_first/pallas_call | solution.py:197
  99.3 7.2 %collective-permute-done.11.refs_1_ = bf16[1024,256]{1,0:T(8,128)(2,1)S(1)} collective-permute-done((bf16[1024,256]{1,0:T(8,128)(2,1)S(1)}, bf16[1024,256]{1,0:T(8,128)(2,1)S(1)}, u32[]{:S(2)}, u32[]{:S(2)}) %collective-permute-start.11) | collective-permute-done | bytes 524320 | tf_op jit(solution)/shard_map/ppermute | solution.py:40
  112.9 1.9 %collective-permute-done.16.refs_2_ = bf16[512,256]{1,0:T(8,128)(2,1)S(1)} collective-permute-done((bf16[512,256]{1,0:T(8,128)(2,1)S(1)}, bf16[512,256]{1,0:T(8,128)(2,1)S(1)}, u32[]{:S(2)}, u32[]{:S(2)}) %collective-permute-start.16) | collective-permute-done | bytes 262176 | tf_op jit(solution)/shard_map/ppermute | solution.py:40
  115.0 4.0 %collective-permute-start.17 = (bf16[2048,256]{1,0:T(8,128)(2,1)S(1)}, bf16[2048,256]{1,0:T(8,128)(2,1)S(1)}, u32[]{:S(2)}, u32[]{:S(2)}) collective-permute-start(bf16[2048,256]{1,0:T(8,128)(2,1)S(1)} %pack.7.refs_1_), channel_id=1, source_target_pairs={{0,8},{1,3},{2,10},{3,5},{4,12},{5,7},{6,14},{7,1},{8,16},{9,11},{... | collective-permute-start | bytes 3145736 | tf_op jit(solution)/shard_map/ppermute | solution.py:40
  120.4 4.6 %collective-permute-done.12.refs_2_ = bf16[2048,256]{1,0:T(8,128)(2,1)S(1)} collective-permute-done((bf16[2048,256]{1,0:T(8,128)(2,1)S(1)}, bf16[2048,256]{1,0:T(8,128)(2,1)S(1)}, u32[]{:S(2)}, u32[]{:S(2)}) %collective-permute-start.12) | collective-permute-done | bytes 1048608 | tf_op jit(solution)/shard_map/ppermute | solution.py:40
  125.2 11.1 %collective-permute-done.17.refs_4_ = bf16[2048,256]{1,0:T(8,128)(2,1)S(1)} collective-permute-done((bf16[2048,256]{1,0:T(8,128)(2,1)S(1)}, bf16[2048,256]{1,0:T(8,128)(2,1)S(1)}, u32[]{:S(2)}, u32[]{:S(2)}) %collective-permute-start.17) | collective-permute-done | bytes 1048608 | tf_op jit(solution)/shard_map/ppermute | solution.py:40
  139.8 3.8 %plane_near.3.plane_sum = f32[1024,256]{1,0:T(8,128)S(1)} custom-call(bf16[20480,256]{1,0:T(8,128)(2,1)} %all-gather.3.cloned.1.call-done.gathered, bf16[2048,256]{1,0:T(8,128)(2,1)S(1)} %pack.6.refs_0_, bf16[2048,256]{1,0:T(8,128)(2,1)} %copy-done.5, bf16[2048,256]{1,0:T(8,128)(2,1)} %copy-done.11, bf16[2048,256]{1,0:T(8,128)(2,1)} %copy-done.13, ...), custom_call_target="tpu_custom_call" | custom-call | flops 2147483648 | bytes 9437184 | tf_op jit(solution)/shard_map/plane_near/pallas_call | solution.py:197
  144.6 5.3 %polar_ring.1.ring_part = bf16[1024,256]{1,0:T(8,128)(2,1)} custom-call(bf16[4096,256]{1,0:T(8,128)(2,1)} %occ_tiles.1.own, bf16[4096,256]{1,0:T(8,128)(2,1)} %collective-permute-done.10.other, bf16[8192,256]{1,0:T(8,128)(2,1)} %all-gather.5.cloned.1.call-done.gathered), custom_call_target="tpu_custom_call" | custom-call | flops 2147483648 | bytes 9437184 | tf_op jit(solution)/shard_map/polar_ring/pallas_call | solution.py:197
  149.9 2.8 %collective-permute-done.19.top = bf16[2048,256]{1,0:T(8,128)(2,1)} collective-permute-done((bf16[2048,256]{1,0:T(8,128)(2,1)S(1)}, bf16[2048,256]{1,0:T(8,128)(2,1)}, u32[]{:S(2)}, u32[]{:S(2)}) %collective-permute-start.19) | collective-permute-done | bytes 1048608 | tf_op jit(solution)/shard_map/ppermute | solution.py:40
  153.2 4.9 %polar_product.1 = (bf16[2048,256]{1,0:T(8,128)(2,1)}, f32[128,128]{1,0:T(8,128)}) custom-call(bf16[20480,256]{1,0:T(8,128)(2,1)} %all-gather.3.cloned.1.call-done.gathered, bf16[2048,256]{1,0:T(8,128)(2,1)} %collective-permute-done.19.top, bf16[2048,256]{1,0:T(8,128)(2,1)} %collective-permute-done.20.bottom, f32[1024,256]{1,0:T(8,128)} %copy-done.4, ...), custom_call_target="tpu_custom_call" | custom-call | flops 536870912 | bytes 9437184 | tf_op jit(solution)/shard_map/polar_product/pallas_call | solution.py:197
  158.1 22.3 %all_to_all.5 = f32[128,1,128]{2,1,0:T(1,128)S(1)} all-to-all(f32[128,1,128]{2,1,0:T(1,128)} %bitcast.8), channel_id=1, replica_groups=mesh['row'=8,'col'=16,'layer'=2] {'row','col'}, dimensions={0} | all-to-all | bytes 131072 | tf_op jit(solution)/shard_map/all_to_all | solution.py:458
  (76 shorter events, 27.0 us)
Async XLA Ops:
  7.2 71.7 %all-gather.3.cloned.1.call-start = ((), (), s32[]{:S(2)}) async-start(), calls=%async_computation.1 | async-start | bytes 11141120 | tf_op jit(solution)/shard_map/all_gather | solution.py:440
  10.0 134.6 %all-gather.5.cloned.1.call-start = ((), (), s32[]{:S(2)}) async-start(), calls=%async_computation.2 | async-start | bytes 4718592 | tf_op jit(solution)/shard_map/all_gather | solution.py:450
  10.0 11.1 %collective-permute-start = (bf16[1280,256]{1,0:T(8,128)(2,1)}, bf16[1280,256]{1,0:T(8,128)(2,1)S(1)}, u32[]{:S(2)}, u32[]{:S(2)}) collective-permute-start(bf16[1280,256]{1,0:T(8,128)(2,1)} %get-tuple-element.27.refs_0_), channel_id=1, source_target_pairs={{0,2},{1,9},{2,4},{3,11},{4,6},{5,13},{6,0},{7,15},{8,10},{9,17},{... | collective-permute-start | bytes 1966088 | tf_op jit(solution)/shard_map/ppermute | solution.py:40
  11.6 10.9 %collective-permute-start.1 = (bf16[1280,256]{1,0:T(8,128)(2,1)}, bf16[1280,256]{1,0:T(8,128)(2,1)S(1)}, u32[]{:S(2)}, u32[]{:S(2)}) collective-permute-start(bf16[1280,256]{1,0:T(8,128)(2,1)} %get-tuple-element.27.refs_0_), channel_id=1, source_target_pairs={{0,6},{1,25},{2,0},{3,27},{4,2},{5,29},{6,4},{7,31},{8,14},{9,1},{... | collective-permute-start | bytes 1966088 | tf_op jit(solution)/shard_map/ppermute | solution.py:40
  21.2 10.6 %collective-permute-start.2 = (bf16[640,256]{1,0:T(8,128)(2,1)S(1)}, bf16[640,256]{1,0:T(8,128)(2,1)S(1)}, u32[]{:S(2)}, u32[]{:S(2)}) collective-permute-start(bf16[640,256]{1,0:T(8,128)(2,1)S(1)} %slice.25), channel_id=1, source_target_pairs={{0,2},{1,9},{2,4},{3,11},{4,6},{5,13},{6,0},{7,15},{8,10},{9,17},{... | collective-permute-start | bytes 983048 | tf_op jit(solution)/shard_map/ppermute | solution.py:40
  22.5 9.4 %collective-permute-start.3 = (bf16[640,256]{1,0:T(8,128)(2,1)S(1)}, bf16[640,256]{1,0:T(8,128)(2,1)S(1)}, u32[]{:S(2)}, u32[]{:S(2)}) collective-permute-start(bf16[640,256]{1,0:T(8,128)(2,1)S(1)} %slice.26), channel_id=1, source_target_pairs={{0,6},{1,25},{2,0},{3,27},{4,2},{5,29},{6,4},{7,31},{8,14},{9,1},{... | collective-permute-start | bytes 983048 | tf_op jit(solution)/shard_map/ppermute | solution.py:40
  25.5 19.0 %collective-permute-start.4 = (bf16[2560,256]{1,0:T(8,128)(2,1)S(1)}, bf16[2560,256]{1,0:T(8,128)(2,1)}, u32[]{:S(2)}, u32[]{:S(2)}) collective-permute-start(bf16[2560,256]{1,0:T(8,128)(2,1)S(1)} %pack.4.refs_0_), channel_id=1, source_target_pairs={{0,8},{1,3},{2,10},{3,5},{4,12},{5,7},{6,14},{7,1},{8,16},{9,11},{... | collective-permute-start | bytes 3932168 | tf_op jit(solution)/shard_map/ppermute | solution.py:40
  25.7 18.8 %collective-permute-start.5 = (bf16[2560,256]{1,0:T(8,128)(2,1)S(1)}, bf16[2560,256]{1,0:T(8,128)(2,1)S(1)}, u32[]{:S(2)}, u32[]{:S(2)}) collective-permute-start(bf16[2560,256]{1,0:T(8,128)(2,1)S(1)} %pack.4.refs_0_), channel_id=1, source_target_pairs={{0,24},{1,7},{2,26},{3,1},{4,28},{5,3},{6,30},{7,5},{8,0},{9,15},{... | collective-permute-start | bytes 3932168 | tf_op jit(solution)/shard_map/ppermute | solution.py:40
  32.8 25.7 %collective-permute-start.6 = (bf16[2560,256]{1,0:T(8,128)(2,1)S(1)}, bf16[2560,256]{1,0:T(8,128)(2,1)S(1)}, u32[]{:S(2)}, u32[]{:S(2)}) collective-permute-start(bf16[2560,256]{1,0:T(8,128)(2,1)S(1)} %pack.5.refs_1_), channel_id=1, source_target_pairs={{0,8},{1,3},{2,10},{3,5},{4,12},{5,7},{6,14},{7,1},{8,16},{9,11},{... | collective-permute-start | bytes 3932168 | tf_op jit(solution)/shard_map/ppermute | solution.py:40
  35.6 22.9 %collective-permute-start.7 = (bf16[2560,256]{1,0:T(8,128)(2,1)S(1)}, bf16[2560,256]{1,0:T(8,128)(2,1)}, u32[]{:S(2)}, u32[]{:S(2)}) collective-permute-start(bf16[2560,256]{1,0:T(8,128)(2,1)S(1)} %pack.5.refs_1_), channel_id=1, source_target_pairs={{0,24},{1,7},{2,26},{3,1},{4,28},{5,3},{6,30},{7,5},{8,0},{9,15},{... | collective-permute-start | bytes 3932168 | tf_op jit(solution)/shard_map/ppermute | solution.py:40
  58.5 25.2 %collective-permute-start.8 = (bf16[2560,256]{1,0:T(8,128)(2,1)}, bf16[2560,256]{1,0:T(8,128)(2,1)}, u32[]{:S(2)}, u32[]{:S(2)}) collective-permute-start(bf16[2560,256]{1,0:T(8,128)(2,1)} %collective-permute-done.4.refs_2_), channel_id=1, source_target_pairs={{0,8},{1,3},{2,10},{3,5},{4,12},{5,7},{6,14},{7,1},{8,16},{9,11},{... | collective-permute-start | bytes 3932168 | tf_op jit(solution)/shard_map/ppermute | solution.py:40
  59.5 24.1 %collective-permute-start.9 = (bf16[2560,256]{1,0:T(8,128)(2,1)}, bf16[2560,256]{1,0:T(8,128)(2,1)}, u32[]{:S(2)}, u32[]{:S(2)}) collective-permute-start(bf16[2560,256]{1,0:T(8,128)(2,1)} %collective-permute-done.7.refs_5_), channel_id=1, source_target_pairs={{0,24},{1,7},{2,26},{3,1},{4,28},{5,3},{6,30},{7,5},{8,0},{9,15},{... | collective-permute-start | bytes 3932168 | tf_op jit(solution)/shard_map/ppermute | solution.py:40
  86.3 4.8 %collective-permute-start.10 = (bf16[4096,256]{1,0:T(8,128)(2,1)}, bf16[4096,256]{1,0:T(8,128)(2,1)}, u32[]{:S(2)}, u32[]{:S(2)}) collective-permute-start(bf16[4096,256]{1,0:T(8,128)(2,1)} %occ_tiles.1.own), channel_id=1, source_target_pairs={{0,1},{1,0},{2,3},{3,2},{4,5},{5,4},{6,7},{7,6},{8,9},{9,8},{10,11... | collective-permute-start | bytes 6291464 | tf_op jit(solution)/shard_map/ppermute | solution.py:44
  97.2 9.3 %collective-permute-start.11 = (bf16[1024,256]{1,0:T(8,128)(2,1)S(1)}, bf16[1024,256]{1,0:T(8,128)(2,1)S(1)}, u32[]{:S(2)}, u32[]{:S(2)}) collective-permute-start(bf16[1024,256]{1,0:T(8,128)(2,1)S(1)} %get-tuple-element.38.refs_0_), channel_id=1, source_target_pairs={{0,2},{1,9},{2,4},{3,11},{4,6},{5,13},{6,0},{7,15},{8,10},{9,17},{... | collective-permute-start | bytes 1572872 | tf_op jit(solution)/shard_map/ppermute | solution.py:40
  98.7 9.3 %collective-permute-start.14 = (bf16[1024,256]{1,0:T(8,128)(2,1)S(1)}, bf16[1024,256]{1,0:T(8,128)(2,1)S(1)}, u32[]{:S(2)}, u32[]{:S(2)}) collective-permute-start(bf16[1024,256]{1,0:T(8,128)(2,1)S(1)} %get-tuple-element.38.refs_0_), channel_id=1, source_target_pairs={{0,6},{1,25},{2,0},{3,27},{4,2},{5,29},{6,4},{7,31},{8,14},{9,1},{... | collective-permute-start | bytes 1572872 | tf_op jit(solution)/shard_map/ppermute | solution.py:40
  106.5 6.4 %collective-permute-start.15 = (bf16[512,256]{1,0:T(8,128)(2,1)S(1)}, bf16[512,256]{1,0:T(8,128)(2,1)S(1)}, u32[]{:S(2)}, u32[]{:S(2)}) collective-permute-start(bf16[512,256]{1,0:T(8,128)(2,1)S(1)} %slice.27), channel_id=1, source_target_pairs={{0,2},{1,9},{2,4},{3,11},{4,6},{5,13},{6,0},{7,15},{8,10},{9,17},{... | collective-permute-start | bytes 786440 | tf_op jit(solution)/shard_map/ppermute | solution.py:40
  108.0 6.8 %collective-permute-start.16 = (bf16[512,256]{1,0:T(8,128)(2,1)S(1)}, bf16[512,256]{1,0:T(8,128)(2,1)S(1)}, u32[]{:S(2)}, u32[]{:S(2)}) collective-permute-start(bf16[512,256]{1,0:T(8,128)(2,1)S(1)} %slice.28), channel_id=1, source_target_pairs={{0,6},{1,25},{2,0},{3,27},{4,2},{5,29},{6,4},{7,31},{8,14},{9,1},{... | collective-permute-start | bytes 786440 | tf_op jit(solution)/shard_map/ppermute | solution.py:40
  108.9 16.2 %collective-permute-start.12 = (bf16[2048,256]{1,0:T(8,128)(2,1)S(1)}, bf16[2048,256]{1,0:T(8,128)(2,1)S(1)}, u32[]{:S(2)}, u32[]{:S(2)}) collective-permute-start(bf16[2048,256]{1,0:T(8,128)(2,1)S(1)} %pack.6.refs_0_), channel_id=1, source_target_pairs={{0,8},{1,3},{2,10},{3,5},{4,12},{5,7},{6,14},{7,1},{8,16},{9,11},{... | collective-permute-start | bytes 3145736 | tf_op jit(solution)/shard_map/ppermute | solution.py:40
  110.4 14.8 %collective-permute-start.13 = (bf16[2048,256]{1,0:T(8,128)(2,1)S(1)}, bf16[2048,256]{1,0:T(8,128)(2,1)S(1)}, u32[]{:S(2)}, u32[]{:S(2)}) collective-permute-start(bf16[2048,256]{1,0:T(8,128)(2,1)S(1)} %pack.6.refs_0_), channel_id=1, source_target_pairs={{0,24},{1,7},{2,26},{3,1},{4,28},{5,3},{6,30},{7,5},{8,0},{9,15},{... | collective-permute-start | bytes 3145736 | tf_op jit(solution)/shard_map/ppermute | solution.py:40
  115.0 21.3 %collective-permute-start.17 = (bf16[2048,256]{1,0:T(8,128)(2,1)S(1)}, bf16[2048,256]{1,0:T(8,128)(2,1)S(1)}, u32[]{:S(2)}, u32[]{:S(2)}) collective-permute-start(bf16[2048,256]{1,0:T(8,128)(2,1)S(1)} %pack.7.refs_1_), channel_id=1, source_target_pairs={{0,8},{1,3},{2,10},{3,5},{4,12},{5,7},{6,14},{7,1},{8,16},{9,11},{... | collective-permute-start | bytes 3145736 | tf_op jit(solution)/shard_map/ppermute | solution.py:40
  119.0 17.6 %collective-permute-start.18 = (bf16[2048,256]{1,0:T(8,128)(2,1)S(1)}, bf16[2048,256]{1,0:T(8,128)(2,1)}, u32[]{:S(2)}, u32[]{:S(2)}) collective-permute-start(bf16[2048,256]{1,0:T(8,128)(2,1)S(1)} %pack.7.refs_1_), channel_id=1, source_target_pairs={{0,24},{1,7},{2,26},{3,1},{4,28},{5,3},{6,30},{7,5},{8,0},{9,15},{... | collective-permute-start | bytes 3145736 | tf_op jit(solution)/shard_map/ppermute | solution.py:40
  120.4 29.5 %collective-permute-start.21 = (bf16[4,512,256]{2,1,0:T(8,128)(2,1)S(1)}, bf16[4,512,256]{2,1,0:T(8,128)(2,1)S(1)}, u32[]{:S(2)}, u32[]{:S(2)}) collective-permute-start(bf16[4,512,256]{2,1,0:T(8,128)(2,1)S(1)} %copy-done.10), channel_id=1, source_target_pairs={{0,1},{1,0},{2,3},{3,2},{4,5},{5,4},{6,7},{7,6},{8,9},{9,8},{10,11... | collective-permute-start | bytes 3145736 | tf_op jit(solution)/shard_map/ppermute | solution.py:44
  136.6 16.1 %collective-permute-start.19 = (bf16[2048,256]{1,0:T(8,128)(2,1)S(1)}, bf16[2048,256]{1,0:T(8,128)(2,1)}, u32[]{:S(2)}, u32[]{:S(2)}) collective-permute-start(bf16[2048,256]{1,0:T(8,128)(2,1)S(1)} %collective-permute-done.12.refs_2_), channel_id=1, source_target_pairs={{0,8},{1,3},{2,10},{3,5},{4,12},{5,7},{6,14},{7,1},{8,16},{9,11},{... | collective-permute-start | bytes 3145736 | tf_op jit(solution)/shard_map/ppermute | solution.py:40
  138.0 15.1 %collective-permute-start.20 = (bf16[2048,256]{1,0:T(8,128)(2,1)}, bf16[2048,256]{1,0:T(8,128)(2,1)}, u32[]{:S(2)}, u32[]{:S(2)}) collective-permute-start(bf16[2048,256]{1,0:T(8,128)(2,1)} %collective-permute-done.18.refs_5_), channel_id=1, source_target_pairs={{0,24},{1,7},{2,26},{3,1},{4,28},{5,3},{6,30},{7,5},{8,0},{9,15},{... | collective-permute-start | bytes 3145736 | tf_op jit(solution)/shard_map/ppermute | solution.py:40
  (15 other events, 223.3 us)
Sparse Core Ops, SparseCore 0:
  10.1 68.7 all-gather.2
  91.2 53.3 all-gather.4
